TPU v7x, 256 devices: a whole 4x4x8 slice. The times are simulated.
256 devices in a mesh: space: 32 (over z, y), group: 8 (over x, core).
Axes of the slice: x: 4, y: 4, z: 8, core: 2. Of those that a mesh axis runs over, the one named last changes fastest.
Arguments:
- feats: bfloat16 [8, 262144, 128], P('group', 'space'), may hold values from -6 to 6
- geom: bfloat16 [8, 262144, 128], P('group', 'space'), may hold values from -6 to 6
- w_value: bfloat16 [128, 128], replicated, may hold values from -0.5 to 0.5
- w_kern: bfloat16 [128, 64], replicated, may hold values from -0.5 to 0.5
- w_out: bfloat16 [128, 128], replicated, may hold values from -0.5 to 0.5
- gain: float32 [128], replicated, may hold values from 0.1 to 1.9
- t_local: int32 [8, 2048], P('group', 'space'), may hold values from 0 to 31
- t_dest: int32 [8, 2048, 1], P('group', 'space'), may hold values from 0 to 31; in each aligned block of 64 rows (0 to 63, 64 to 127, ..., all dimensions but the last counted through in order) at most 3 rows name the same one
- t_block: int32 [8, 2048], P('group', 'space'), may hold values from 0 to 31
- t_cut: int32 [8, 2048], P('group', 'space'), may hold values from 64 to 511
- x_local: int32 [8, 256], P('group', 'space'), may hold values from 0 to 31
- x_block: int32 [8, 256], P('group', 'space'), may hold values from 0 to 31
- x_cut: int32 [8, 256], P('group', 'space'), may hold values from 64 to 511
Outputs:
- mixed: bfloat16 [8, 262144, 128], P('group', 'space')
Inputs may be any that keep to these rules, and one draw needn't show every extreme that they name: `t_dest`: among the 64 pairs of one device, no index is named by more than 3 pairs, a bound that some block reaches.
All inputs are finite; a program needn't handle non-finite values.
Results may differ from a plain program's by a relative error of at most 0.0054.
Values may be sent and summed in bfloat16 or wider, within the bound.
No kernel may reach another device: no remote copies, remote signals or barrier semaphores. Data moves between devices by JAX's collectives and lax.ppermute only.
A program may use at most 192 MiB of HBM per device.

v0:
```python
import math

import jax
import jax.numpy as jnp
from jax import lax
from jax.experimental import pallas as pl
from jax.experimental.pallas import tpu as pltpu
from jax.sharding import PartitionSpec as P

C = 128
K = 64
BLK = 256
HALF = BLK // 2
ROWS = BLK + HALF
CAP = 3
VMEM_LIMIT = 56 * 1024 * 1024
SPAN_Z, SPAN_Y = 8, 4
SPACES = SPAN_Z * SPAN_Y
SHIFTS = tuple(
    shift for dy in range(SPAN_Y) for shift in ((3, dy), (-3, -dy), (1, dy), (-1, -dy))
)
BATCHES = ((0, 8), (8, 14), (14, 16))
PASSED = 1
MEMBERS = SPACES // 2
TEAMS = [[z * SPAN_Y + y for z in range(p, SPAN_Z, 2) for y in range(SPAN_Y)] for p in range(2)]
LATE = 8
STAGE = 6
LONG = 10**12
SMEM = pl.BlockSpec(memory_space=pltpu.SMEM)
VMEM = pl.BlockSpec(memory_space=pltpu.VMEM)
ANYWHERE = pl.BlockSpec(memory_space=pl.ANY)
CREW = 4
NOTES = CAP * ROWS
LOAD = NOTES + 16


def space_shift(value, shift):
    return lax.ppermute(
        value,
        "space",
        [
            (z * SPAN_Y + y, (z + shift[0]) % SPAN_Z * SPAN_Y + (y + shift[1]) % SPAN_Y)
            for z in range(SPAN_Z)
            for y in range(SPAN_Y)
        ],
    )


def partner_of(me, shift):
    return (me // SPAN_Y + shift[0]) % SPAN_Z * SPAN_Y + (me % SPAN_Y + shift[1]) % SPAN_Y


def team_exchange(value):
    return lax.all_to_all(
        value, "space", split_axis=0, concat_axis=0, tiled=True, axis_index_groups=TEAMS
    )


def group_shift(value, steps):
    count = lax.axis_size("group")
    leading, last = (max(0, -steps), min(count, count - steps))
    return lax.ppermute(value, "group", [(source, source + steps) for source in range(leading, last)])


def project_and_pack(points, geom, w_value, w_kern, lists, x_local, team, dests):
    blocks = points.shape[0] // BLK
    cross = x_local.shape[0]
    tiles = lists[0].shape[0]
    count = len(SHIFTS)
    slots = SPACES * CAP
    step = 8

    def kernel(
        local_ref, dest_ref, block_ref, cut_ref, cross_ref, team_ref, dests_ref,
        points_ref, geom_ref, wv_ref, wk_ref, used_ref, own_ref, up_ref, team_out_ref, *rest
    ):
        out_refs, (held, notes, filled, partner, cuts, sems) = rest[:count], rest[count:]
        i = pl.program_id(0)

        @pl.when(i == 0)
        def _():
            @pl.loop(0, slots, unroll=8)
            def _(s):
                used_ref[s] = -1
                partner[s] = 0
                cuts[s] = 0

            @pl.loop(0, SPACES, unroll=8)
            def _(s):
                filled[s] = 0

            @pl.loop(0, tiles, unroll=4)
            def _(t):
                dest = dest_ref[t]
                slot = dest * CAP + filled[dest]
                filled[dest] = filled[dest] + 1
                used_ref[slot] = local_ref[t]
                partner[slot] = block_ref[t]
                cuts[slot] = cut_ref[t]

            row = lax.broadcasted_iota(jnp.int32, (16, C), 0)

            @pl.loop(0, SPACES, unroll=4)
            def _(d):
                note = jnp.zeros((16, C), jnp.int32)
                for j in range(CAP):
                    cut = cuts[d * CAP + j]
                    note = jnp.where(row == j, partner[d * CAP + j], note)
                    note = jnp.where(row == CAP + j, cut // 16, note)
                    note = jnp.where(row == 2 * CAP + j, cut % 16, note)
                notes[d] = note.astype(jnp.float32).astype(jnp.bfloat16)

        @pl.loop(0, step, unroll=2)
        def _(b):
            upper = pl.ds(pl.multiple_of(b * BLK, BLK), HALF)
            lower = pl.ds(pl.multiple_of(b * BLK + HALF, HALF), HALF)
            whole = pl.ds(pl.multiple_of(b * BLK, BLK), BLK)
            held[i * step + b, :BLK, :] = jnp.dot(
                points_ref[whole, :], wv_ref[...], preferred_element_type=jnp.float32
            ).astype(jnp.bfloat16)
            wide = jnp.concatenate([geom_ref[upper, :], geom_ref[lower, :]], axis=1)
            held[i * step + b, BLK:, :] = jnp.dot(
                wide, wk_ref[...], preferred_element_type=jnp.float32
            ).astype(jnp.bfloat16)

        @pl.when(i == pl.num_programs(0) - 1)
        def _():
            copies = []

            def leave(dest, out):
                for j in range(CAP):
                    block = jnp.maximum(used_ref[dest * CAP + j], 0)
                    copies.append((held.at[block], out.at[pl.ds(j * ROWS, ROWS)]))
                copies.append((notes.at[dest], out.at[pl.ds(NOTES, 16)]))

            for m in range(MEMBERS):
                leave(team_ref[m], team_out_ref.at[m])
            for k in range(count):
                leave(dests_ref[k], out_refs[k])
            for t in range(cross):
                copies.append((held.at[cross_ref[t]], up_ref.at[t]))
            copies.append((held, own_ref))
            started = [pltpu.make_async_copy(source, target, sems) for source, target in copies]
            for copy in started:
                copy.start()
            for copy in started:
                copy.wait()

    zero = jnp.zeros_like(w_kern)
    twice = jnp.concatenate(
        [jnp.concatenate([w_kern, zero], 1), jnp.concatenate([zero, w_kern], 1)], 0
    )
    results = pl.pallas_call(
        kernel,
        grid_spec=pltpu.PrefetchScalarGridSpec(
            num_scalar_prefetch=7,
            grid=(blocks // step,),
            in_specs=[
                pl.BlockSpec((step * BLK, C), lambda i, *_: (i, 0)),
                pl.BlockSpec((step * BLK, C), lambda i, *_: (i, 0)),
                pl.BlockSpec((C, C), lambda i, *_: (0, 0)),
                pl.BlockSpec((2 * C, 2 * K), lambda i, *_: (0, 0)),
            ],
            out_specs=(SMEM,) + (ANYWHERE,) * (3 + count),
            scratch_shapes=[
                pltpu.VMEM((blocks, ROWS, C), jnp.bfloat16),
                pltpu.VMEM((SPACES, 16, C), jnp.bfloat16),
                pltpu.SMEM((SPACES,), jnp.int32),
                pltpu.SMEM((slots,), jnp.int32),
                pltpu.SMEM((slots,), jnp.int32),
                pltpu.SemaphoreType.DMA,
            ],
        ),
        out_shape=(
            jax.ShapeDtypeStruct((slots,), jnp.int32),
            jax.ShapeDtypeStruct((blocks, ROWS, C), jnp.bfloat16),
            jax.ShapeDtypeStruct((cross, ROWS, C), jnp.bfloat16),
            jax.ShapeDtypeStruct((MEMBERS, LOAD, C), jnp.bfloat16),
        )
        + (jax.ShapeDtypeStruct((LOAD, C), jnp.bfloat16),) * count,
        compiler_params=pltpu.CompilerParams(vmem_limit_bytes=VMEM_LIMIT),
        name="project_and_pack",
    )(*lists, x_local, team, dests, points, geom, w_value, twice)
    return results[:4], results[4:]


def read_notes(load):
    note = load[pl.ds(NOTES, 16), :].astype(jnp.float32)
    entry = note[:CAP] * 512 + note[CAP : 2 * CAP] * 16 + note[2 * CAP : 3 * CAP]
    entries = [entry[j, 0].astype(jnp.int32) for j in range(CAP)]
    return [(value // 512, value % 512) for value in entries]


def unpack_kernels(packed):
    return jnp.concatenate([packed[:, :K], packed[:, K:]], axis=0)


def pair_terms(pairs):
    rows = lax.broadcasted_iota(jnp.int32, (BLK, BLK), 0)
    columns = lax.broadcasted_iota(jnp.int32, (BLK, BLK), 1)
    level = rows + columns
    scores = [
        lax.dot_general(
            unpack_kernels(a[BLK:, :]),
            unpack_kernels(b[BLK:, :]),
            (((1,), (1,)), ((), ())),
            preferred_element_type=jnp.float32,
        )
        for a, b, _ in pairs
    ]
    tiles = [
        jnp.where(level < cut, jnp.tanh(score * (1.0 / math.sqrt(K))), 0.0).astype(jnp.bfloat16)
        for score, (_, _, cut) in zip(scores, pairs)
    ]
    forward = [
        jnp.dot(tile, b[:BLK, :], preferred_element_type=jnp.float32) for tile, (_, b, _) in zip(tiles, pairs)
    ]
    backward = [
        lax.dot_general(tile, a[:BLK, :], (((0,), (0,)), ((), ())), preferred_element_type=jnp.float32)
        for tile, (a, _, _) in zip(tiles, pairs)
    ]
    return forward, backward


def pair_cost(number, blocks):
    return pl.CostEstimate(
        flops=2 * number * BLK * BLK * (K + 2 * C),
        bytes_accessed=number * (ROWS + BLK) * C * 2 + blocks * BLK * C * 8,
        transcendentals=number * BLK * BLK,
    )


def pairs_above(cross_meta, below, own):
    cross = below.shape[0]
    blocks = own.shape[0]
    some = math.gcd(cross, 4)

    def kernel(cross_ref, below_ref, own_ref, back_ref, total):
        total[...] = jnp.zeros_like(total)

        @pl.loop(0, cross, step=some)
        def _(first):
            mine = [cross_ref[2 * (first + t)] for t in range(some)]
            forward, backward = pair_terms(
                [
                    (below_ref.at[first + t], own_ref.at[mine[t]], cross_ref[2 * (first + t) + 1])
                    for t in range(some)
                ]
            )
            for t in range(some):
                back_ref[first + t] = forward[t].astype(jnp.bfloat16)
            for t in range(some):
                total[mine[t]] = total[mine[t]] + backward[t]

    return pl.pallas_call(
        kernel,
        in_specs=[SMEM, VMEM, VMEM],
        out_specs=(VMEM, VMEM),
        out_shape=(
            jax.ShapeDtypeStruct((cross, BLK, C), jnp.bfloat16),
            jax.ShapeDtypeStruct((blocks, BLK, C), jnp.float32),
        ),
        compiler_params=pltpu.CompilerParams(vmem_limit_bytes=VMEM_LIMIT),
        cost_estimate=pl.CostEstimate(flops=LONG, bytes_accessed=0, transcendentals=0),
        name="pairs_above",
    )(cross_meta, below, own)


def team_pairs(arrived, own, aggregate, passing):
    blocks = own.shape[0]
    some = CREW * CAP
    handed = len(passing)

    def kernel(arrived_ref, own_ref, given_ref, *rest):
        back_ref, total_ref, total, sem = rest[handed], rest[handed + 1], rest[-2], rest[-1]
        i = pl.program_id(0)

        @pl.when(i == 0)
        def _():
            copy = pltpu.make_async_copy(given_ref, total, sem)
            copy.start()
            copy.wait()

        @pl.loop(0, CREW, step=STAGE // CAP)
        def _(first):
            places = []
            for m in range(STAGE // CAP):
                load = arrived_ref.at[first + m]
                for j, (block, cut) in enumerate(read_notes(load)):
                    places.append((load.at[pl.ds(j * ROWS, ROWS)], block, cut))
            forward, backward = pair_terms([(a, own_ref.at[block], cut) for a, block, cut in places])
            for n in range(STAGE):
                back_ref[first * CAP + n] = forward[n].astype(jnp.bfloat16)
            for n, (_, block, _) in enumerate(places):
                total[block] = total[block] + backward[n]

        @pl.when(i == pl.num_programs(0) - 1)
        def _():
            copy = pltpu.make_async_copy(total, total_ref, sem)
            copy.start()
            copy.wait()

    results = pl.pallas_call(
        kernel,
        grid=(MEMBERS // CREW,),
        in_specs=[
            pl.BlockSpec((CREW, LOAD, C), lambda i: (i, 0, 0)),
            pl.BlockSpec((blocks, ROWS, C), lambda i: (0, 0, 0)),
            ANYWHERE,
        ]
        + [ANYWHERE] * handed,
        out_specs=(pl.BlockSpec((some, BLK, C), lambda i: (i, 0, 0)), ANYWHERE) + (ANYWHERE,) * handed,
        scratch_shapes=[
            pltpu.VMEM((blocks, BLK, C), jnp.float32),
            pltpu.SemaphoreType.DMA,
        ],
        out_shape=(
            jax.ShapeDtypeStruct((MEMBERS * CAP, BLK, C), jnp.bfloat16),
            jax.ShapeDtypeStruct((blocks, BLK, C), jnp.float32),
        )
        + tuple(jax.ShapeDtypeStruct(array.shape, array.dtype) for array in passing),
        input_output_aliases={3 + n: 2 + n for n in range(handed)},
        compiler_params=pltpu.CompilerParams(vmem_limit_bytes=VMEM_LIMIT),
        cost_estimate=pair_cost(MEMBERS * CAP, blocks),
        name="team_pairs",
    )(arrived, own, aggregate, *passing)
    return results[0], results[1], results[2:]


def shifted_pairs(arrived, own, aggregate, passing, cost):
    count = len(arrived)
    blocks = own.shape[0]
    handed = len(passing)

    def kernel(own_ref, given_ref, *rest):
        arrived_refs, rest = rest[handed : handed + count], rest[handed + count :]
        back_refs, total, loads, backs = rest[:count], rest[count], rest[-2], rest[-1]
        total[...] = given_ref[...]
        for k in range(count):
            loads[k] = arrived_refs[k][...]

        @pl.loop(0, count, step=STAGE // CAP)
        def _(first):
            places = []
            for k in range(STAGE // CAP):
                load = loads.at[first + k]
                for j, (block, cut) in enumerate(read_notes(load)):
                    places.append((load.at[pl.ds(j * ROWS, ROWS)], block, cut))
            forward, backward = pair_terms([(a, own_ref.at[block], cut) for a, block, cut in places])
            for n in range(STAGE):
                backs[first + n // CAP, n % CAP] = forward[n].astype(jnp.bfloat16)
            for n, (_, block, _) in enumerate(places):
                total[block] = total[block] + backward[n]

        for k in range(count):
            back_refs[k][...] = backs[k]

    results = pl.pallas_call(
        kernel,
        in_specs=[VMEM] * 2 + [ANYWHERE] * handed + [VMEM] * count,
        out_specs=(VMEM,) * (count + 1) + (ANYWHERE,) * handed,
        out_shape=(jax.ShapeDtypeStruct((CAP, BLK, C), jnp.bfloat16),) * count
        + (jax.ShapeDtypeStruct((blocks, BLK, C), jnp.float32),)
        + tuple(jax.ShapeDtypeStruct(array.shape, array.dtype) for array in passing),
        input_output_aliases={1: count} | {2 + n: count + 1 + n for n in range(handed)},
        scratch_shapes=[
            pltpu.VMEM((count, LOAD, C), jnp.bfloat16),
            pltpu.VMEM((count, CAP, BLK, C), jnp.bfloat16),
        ],
        compiler_params=pltpu.CompilerParams(vmem_limit_bytes=VMEM_LIMIT),
        cost_estimate=cost,
        name="shifted_pairs",
    )(own, aggregate, *passing, *arrived)
    return results[:count], results[count], results[count + 1 :]


def add_back(used_ref, places_ref, back_refs, total):
    for k, back_ref in enumerate(back_refs):
        for j in range(CAP):
            mine = used_ref[places_ref[k] * CAP + j]

            @pl.when(mine >= 0)
            def _():
                total[mine] = total[mine] + back_ref[j].astype(jnp.float32)


def gather_team(used, team, x_local, returned, returned_x, aggregate, passing):
    cross = returned_x.shape[0]
    handed = len(passing)

    def kernel(used_ref, team_ref, cross_ref, given_ref, back_ref, back_x_ref, *rest):
        total = rest[handed]
        total[...] = given_ref[...]
        for t in range(cross):
            mine = cross_ref[t]
            total[mine] = total[mine] + back_x_ref[t].astype(jnp.float32)

        @pl.loop(0, MEMBERS)
        def _(m):
            for j in range(CAP):
                mine = used_ref[team_ref[m] * CAP + j]

                @pl.when(mine >= 0)
                def _():
                    total[mine] = total[mine] + back_ref[m * CAP + j].astype(jnp.float32)

    results = pl.pallas_call(
        kernel,
        in_specs=[SMEM] * 3 + [VMEM] * 3 + [ANYWHERE] * handed,
        out_specs=(VMEM,) + (ANYWHERE,) * handed,
        out_shape=(jax.ShapeDtypeStruct(aggregate.shape, jnp.float32),)
        + tuple(jax.ShapeDtypeStruct(array.shape, array.dtype) for array in passing),
        input_output_aliases={3: 0} | {6 + n: 1 + n for n in range(handed)},
        compiler_params=pltpu.CompilerParams(vmem_limit_bytes=VMEM_LIMIT),
        cost_estimate=pl.CostEstimate(
            flops=returned.size, bytes_accessed=returned.size * 2 + aggregate.size * 8, transcendentals=0
        ),
        name="gather_team",
    )(used, team, x_local, aggregate, returned, returned_x, *passing)
    return results[0], results[1:]


def gather_and_mix(used, dests, returned, aggregate, points, w_out, gain):
    count = len(returned)
    blocks = aggregate.shape[0]
    some = 8

    def kernel(used_ref, dests_ref, total_ref, points_ref, w_ref, gain_ref, *rest):
        back_refs, out_ref, total, sem = rest[:count], rest[count], rest[count + 1], rest[count + 2]
        i = pl.program_id(0)

        @pl.when(i == 0)
        def _():
            copy = pltpu.make_async_copy(total_ref, total, sem)
            copy.start()
            copy.wait()
            add_back(used_ref, dests_ref, back_refs, total)

        @pl.loop(0, some, unroll=2)
        def _(b):
            rows = pl.ds(pl.multiple_of(b * BLK, BLK), BLK)
            flat = total[i * some + b]
            meansq = jnp.mean(flat * flat, -1, keepdims=True)
            normed = flat * lax.rsqrt(meansq + 1e-06) * gain_ref[...]
            hidden = jax.nn.gelu(normed).astype(jnp.bfloat16)
            mixed = points_ref[rows, :].astype(jnp.float32) + jnp.dot(
                hidden, w_ref[...], preferred_element_type=jnp.float32
            )
            out_ref[rows, :] = mixed.astype(jnp.bfloat16)

    return pl.pallas_call(
        kernel,
        grid_spec=pltpu.PrefetchScalarGridSpec(
            num_scalar_prefetch=2,
            grid=(blocks // some,),
            in_specs=[
                pl.BlockSpec(memory_space=pl.ANY),
                pl.BlockSpec((some * BLK, C), lambda i, *_: (i, 0)),
                pl.BlockSpec((C, C), lambda i, *_: (0, 0)),
                pl.BlockSpec((1, C), lambda i, *_: (0, 0)),
            ]
            + [pl.BlockSpec((CAP, BLK, C), lambda i, *_: (0, 0, 0))] * count,
            out_specs=pl.BlockSpec((some * BLK, C), lambda i, *_: (i, 0)),
            scratch_shapes=[
                pltpu.VMEM((blocks, BLK, C), jnp.float32),
                pltpu.SemaphoreType.DMA,
            ],
        ),
        out_shape=jax.ShapeDtypeStruct((blocks * BLK, C), jnp.bfloat16),
        compiler_params=pltpu.CompilerParams(vmem_limit_bytes=VMEM_LIMIT),
        name="gather_and_mix",
    )(used, dests, aggregate, points, w_out, gain[None], *returned)


def body(feats, geom, w_value, w_kern, w_out, gain, t_local, t_dest, t_block, t_cut, x_local, x_block, x_cut):
    points = feats[0]
    me = lax.axis_index("space")
    dests = jnp.stack([partner_of(me, shift) for shift in SHIFTS]).astype(jnp.int32)
    member = jnp.arange(MEMBERS, dtype=jnp.int32)
    team = (member // SPAN_Y * 2 + me // SPAN_Y % 2) * SPAN_Y + member % SPAN_Y
    lists = (t_local[0], t_dest[0, :, 0], t_block[0], t_cut[0])
    (used, own, rising, leaving), shifting = project_and_pack(
        points, geom[0], w_value, w_kern, lists, x_local[0], team, dests
    )
    arrived = team_exchange(leaving)
    cross_meta = group_shift(jnp.stack([x_block[0], x_cut[0]], 1), 1).reshape(-1)
    below = group_shift(rising, 1)
    shifting = list(shifting)
    shifted = [None] * len(SHIFTS)

    def send(first, end):
        for k in range(first, end):
            shifted[k] = space_shift(shifting[k], SHIFTS[k])

    back_x, aggregate = pairs_above(cross_meta, below, own)
    returned_x = group_shift(back_x, -1)
    send(*BATCHES[0])
    first, end = BATCHES[1]
    back, aggregate, shifting[first:end] = team_pairs(
        arrived, own, aggregate, shifting[first:end]
    )
    going_back = []
    for turn, (first, end) in enumerate(BATCHES):
        later = slice(*BATCHES[turn + 2]) if turn + 2 < len(BATCHES) else slice(0, 0)
        if turn + 1 < len(BATCHES):
            send(*BATCHES[turn + 1])
        passing = shifting[later] + ([back] if turn == PASSED else [])
        back_some, aggregate, passing = shifted_pairs(
            shifted[first:end], own, aggregate, passing,
            pl.CostEstimate(flops=LONG, bytes_accessed=0, transcendentals=0)
            if turn > PASSED
            else pair_cost((end - first) * CAP, own.shape[0]),
        )
        shifting[later] = passing[: later.stop - later.start]
        if turn == PASSED:
            returned = team_exchange(passing[-1])
        going_back += back_some
    back_shifted = [None] * len(SHIFTS)

    def send_back(first, end):
        for k in range(first, end):
            dz, dy = SHIFTS[k]
            back_shifted[k] = space_shift(going_back[k], (-dz, -dy))

    send_back(0, LATE)
    aggregate, going_back[LATE:] = gather_team(
        used, team, x_local[0], returned, returned_x, aggregate, going_back[LATE:]
    )
    send_back(LATE, len(SHIFTS))
    mixed = gather_and_mix(used, dests, back_shifted, aggregate, points, w_out, gain)
    return mixed[None]


def solution(mesh):
    in_specs = (
        P("group", "space", None),
        P("group", "space", None),
        P(),
        P(),
        P(),
        P(),
        P("group", "space"),
        P("group", "space", None),
        P("group", "space"),
        P("group", "space"),
        P("group", "space"),
        P("group", "space"),
        P("group", "space"),
    )
    out_specs = P("group", "space", None)
    return jax.shard_map(body, mesh=mesh, in_specs=in_specs, out_specs=out_specs, check_vma=False)
```

profile of v0, /device:TPU:42, one launch (start us, length us, event | category | flops | bytes accessed | tf_op | source)
XLA Modules:
  0.0 402.2 jit_solution(10969086342058433898)
XLA Ops:
  0.6 0.8 copy.38
  2.7 12.0 %project_and_pack.1 = (s32[96]{0:T(128)}, bf16[32,384,128]{2,1,0:T(8,128)(2,1)}, bf16[8,384,128]{2,1,0:T(8,128)(2,1)}, bf16[16,1168,128]{2,1,0:T(8,128)(2,1)}, b...) custom-call(s32[64]{0:T(128)} %bitcast.32, ...), custom_call_target="tpu_custom_call" | custom-call | tf_op jit(solution)/shard_map/project_and_pack/pallas_call | solution.py:153
  14.7 1.9 collective-permute-start.1
  16.7 3.5 collective-permute-start
  20.2 10.7 %all-to-all-start = ((bf16[16,1168,128]{2,1,0:T(8,128)(2,1)}), bf16[16,1168,128]{2,1,0:T(8,128)(2,1)}, u32[]{:S(2)}, u32[]{:S(2)}) async-start(bf16[16,1168,128]{2,1,0:T(8,128)(2,1)} %get-tuple-element.68), calls=%async_computation | async-start | bytes 9568256 | tf_op jit(solution)/shard_map/all_to_all | solution.py:54
  30.9 4.9 %collective-permute-start.2 = (bf16[1168,128]{1,0:T(8,128)(2,1)}, bf16[1168,128]{1,0:T(8,128)(2,1)}, u32[]{:S(2)}, u32[]{:S(2)}) collective-permute-start(bf16[1168,128]{1,0:T(8,128)(2,1)} %get-tuple-element.80), channel_id=1, source_target_pairs={{0,96},{8,104},{16,112},{24,120},{32,128},{40,136},{48,144},{56,15... | collective-permute-start | bytes 897032 | tf_op jit(solution)/shard_map/ppermute | solution.py:38
  35.9 1.9 collective-permute-start.4
  38.7 7.0 %collective-permute-start.6 = (bf16[1168,128]{1,0:T(8,128)(2,1)}, bf16[1168,128]{1,0:T(8,128)(2,1)}, u32[]{:S(2)}, u32[]{:S(2)}) collective-permute-start(bf16[1168,128]{1,0:T(8,128)(2,1)} %get-tuple-element.84), channel_id=1, source_target_pairs={{0,104},{8,112},{16,120},{24,96},{32,136},{40,144},{48,152},{56,12... | collective-permute-start | bytes 897032 | tf_op jit(solution)/shard_map/ppermute | solution.py:38
  45.7 6.0 %pairs_above.1 = (bf16[8,256,128]{2,1,0:T(8,128)(2,1)}, f32[32,256,128]{2,1,0:T(8,128)}) custom-call(s32[16]{0:T(128)} %reshape.3.cross_ref, bf16[8,384,128]{2,1,0:T(8,128)(2,1)} %copy-done.23, bf16[32,384,128]{2,1,0:T(8,128)(2,1)} %get-tuple-element.67.own_ref), custom_call_target="tpu_custom_call" | custom-call | flops 999999995904 | tf_op jit(solution)/shard_map/pairs_above/pallas_call | solution.py:255
  51.7 106.0 %collective-permute-done.2.rest_2_ = bf16[1168,128]{1,0:T(8,128)(2,1)} collective-permute-done((bf16[1168,128]{1,0:T(8,128)(2,1)}, bf16[1168,128]{1,0:T(8,128)(2,1)}, u32[]{:S(2)}, u32[]{:S(2)}) %collective-permute-start.2) | collective-permute-done | bytes 299040 | tf_op jit(solution)/shard_map/ppermute | solution.py:38
  157.7 1.8 collective-permute-start.7
  159.5 3.3 collective-permute-start.8
  162.8 2.8 collective-permute-start.9
  165.6 15.5 %team_pairs.1 = (bf16[48,256,128]{2,1,0:T(8,128)(2,1)}, f32[32,256,128]{2,1,0:T(8,128)}, bf16[1168,128]{1,0:T(8,128)(2,1)}, bf16[1168,128]{1,0:T(8,128)(2,1)}, b...) custom-call(bf16[16,1168,128]{2,1,0:T(8,128)(2,1)} %all-to-all-done., ...), custom_call_target="tpu_custom_call", output_to_operand_aliasing={{2}: (3, {}), {3}: (4, {}), {4}: (5, {}), {5}: (6, {}), {6}... | custom-call | flops 2013265920 | bytes 16252928 | tf_op jit(solution)/shard_map/team_pairs/pallas_call | solution.py:303
  181.1 7.4 %collective-permute-start.10 = (bf16[1168,128]{1,0:T(8,128)(2,1)}, bf16[1168,128]{1,0:T(8,128)(2,1)S(1)}, u32[]{:S(2)}, u32[]{:S(2)}) collective-permute-start(bf16[1168,128]{1,0:T(8,128)(2,1)} %get-tuple-element.90), channel_id=1, source_target_pairs={{0,112},{8,120},{16,96},{24,104},{32,144},{40,152},{48,128},{56,13... | collective-permute-start | bytes 897032 | tf_op jit(solution)/shard_map/ppermute | solution.py:38
  188.6 2.3 collective-permute-start.12
  191.0 2.1 collective-permute-start.13
  193.1 1.9 collective-permute-start.18
  195.0 15.6 %collective-permute-done.10.rest_1_ = bf16[1168,128]{1,0:T(8,128)(2,1)S(1)} collective-permute-done((bf16[1168,128]{1,0:T(8,128)(2,1)}, bf16[1168,128]{1,0:T(8,128)(2,1)S(1)}, u32[]{:S(2)}, u32[]{:S(2)}) %collective-permute-start.10) | collective-permute-done | bytes 299040 | tf_op jit(solution)/shard_map/ppermute | solution.py:38
  210.6 8.2 %collective-permute-start.14 = (bf16[1168,128]{1,0:T(8,128)(2,1)}, bf16[1168,128]{1,0:T(8,128)(2,1)S(1)}, u32[]{:S(2)}, u32[]{:S(2)}) collective-permute-start(bf16[1168,128]{1,0:T(8,128)(2,1)} %get-tuple-element.94), channel_id=1, source_target_pairs={{0,120},{8,96},{16,104},{24,112},{32,152},{40,128},{48,136},{56,14... | collective-permute-start | bytes 897032 | tf_op jit(solution)/shard_map/ppermute | solution.py:38
  218.8 10.8 %shifted_pairs.3 = (bf16[3,256,128]{2,1,0:T(8,128)(2,1)}, bf16[3,256,128]{2,1,0:T(8,128)(2,1)}, bf16[3,256,128]{2,1,0:T(8,128)(2,1)}, bf16[3,256,128]{2,1,0:T(8,...) custom-call(bf16[32,384,128]{2,1,0:T(8,128)(2,1)} %get-tuple-element, ...), custom_call_target="tpu_custom_call", output_to_operand_aliasing={{8}: (1, {}), {9}: (2, {}), {10}: (3, {})} | custom-call | flops 1006632960 | bytes 12320768 | tf_op jit(solution)/shard_map/shifted_pairs/pallas_call | solution.py:358
  229.7 5.0 %collective-permute-start.17 = (bf16[1168,128]{1,0:T(8,128)(2,1)}, bf16[1168,128]{1,0:T(8,128)(2,1)S(1)}, u32[]{:S(2)}, u32[]{:S(2)}) collective-permute-start(bf16[1168,128]{1,0:T(8,128)(2,1)} %get-tuple-element.98), channel_id=1, source_target_pairs={{0,232},{8,240},{16,248},{24,224},{32,8},{40,16},{48,24},{56,0},{6... | collective-permute-start | bytes 897032 | tf_op jit(solution)/shard_map/ppermute | solution.py:38
  234.7 4.7 %collective-permute-done.14.rest_5_ = bf16[1168,128]{1,0:T(8,128)(2,1)S(1)} collective-permute-done((bf16[1168,128]{1,0:T(8,128)(2,1)}, bf16[1168,128]{1,0:T(8,128)(2,1)S(1)}, u32[]{:S(2)}, u32[]{:S(2)}) %collective-permute-start.14) | collective-permute-done | bytes 299040 | tf_op jit(solution)/shard_map/ppermute | solution.py:38
  239.5 5.0 %collective-permute-start.20 = (bf16[3,256,128]{2,1,0:T(8,128)(2,1)}, bf16[3,256,128]{2,1,0:T(8,128)(2,1)}, u32[]{:S(2)}, u32[]{:S(2)}) collective-permute-start(bf16[3,256,128]{2,1,0:T(8,128)(2,1)} %get-tuple-element.112), channel_id=1, source_target_pairs={{0,96},{8,104},{16,112},{24,120},{32,128},{40,136},{48,144},{56,15... | collective-permute-start | bytes 589832 | tf_op jit(solution)/shard_map/ppermute | solution.py:38
  244.5 9.4 %shifted_pairs.4 = (bf16[3,256,128]{2,1,0:T(8,128)(2,1)}, bf16[3,256,128]{2,1,0:T(8,128)(2,1)}, bf16[3,256,128]{2,1,0:T(8,128)(2,1)}, bf16[3,256,128]{2,1,0:T(8,...) custom-call(bf16[32,384,128]{2,1,0:T(8,128)(2,1)} %get-tuple-element, ...), custom_call_target="tpu_custom_call", output_to_operand_aliasing={{6}: (1, {}), {7}: (2, {})} | custom-call | flops 754974720 | bytes 11337728 | tf_op jit(solution)/shard_map/shifted_pairs/pallas_call | solution.py:358
  253.9 8.0 %all-to-all-start.1 = ((bf16[48,256,128]{2,1,0:T(8,128)(2,1)}), bf16[48,256,128]{2,1,0:T(8,128)(2,1)}, u32[]{:S(2)}, u32[]{:S(2)}) async-start(bf16[48,256,128]{2,1,0:T(8,128)(2,1)} %get-tuple-element.100), calls=%async_computation.1 | async-start | bytes 6291456 | tf_op jit(solution)/shard_map/all_to_all | solution.py:54
  261.9 1.7 collective-permute-start.21
  263.6 1.0 collective-permute-start.22
  264.6 4.0 %collective-permute-start.23 = (bf16[3,256,128]{2,1,0:T(8,128)(2,1)}, bf16[3,256,128]{2,1,0:T(8,128)(2,1)}, u32[]{:S(2)}, u32[]{:S(2)}) collective-permute-start(bf16[3,256,128]{2,1,0:T(8,128)(2,1)} %get-tuple-element.115), channel_id=1, source_target_pairs={{0,184},{8,160},{16,168},{24,176},{32,216},{40,192},{48,200},{56,2... | collective-permute-start | bytes 589832 | tf_op jit(solution)/shard_map/ppermute | solution.py:38
  268.6 2.1 collective-permute-start.24
  270.8 6.5 %shifted_pairs.5 = (bf16[3,256,128]{2,1,0:T(8,128)(2,1)}, bf16[3,256,128]{2,1,0:T(8,128)(2,1)}, f32[32,256,128]{2,1,0:T(8,128)}) custom-call(bf16[32,384,128]{2,1,0:T(8,128)(2,1)} %get-tuple-element.67.own_ref, f32[32,256,128]{2,1,0:T(8,128)} %get-tuple-element.96.given_ref, bf16[1168,128]{1,0:T(8,128)(2,1)} %copy-done.28, ...), custom_call_target="tpu_custom_call", output_to_operand_aliasing={{2}: (1, {})} | custom-call | flops 999999995904 | tf_op jit(solution)/shard_map/shifted_pairs/pallas_call | solution.py:358
  277.2 57.3 %all-to-all-done.1.back_ref = bf16[48,256,128]{2,1,0:T(8,128)(2,1)} async-done(((bf16[48,256,128]{2,1,0:T(8,128)(2,1)}), bf16[48,256,128]{2,1,0:T(8,128)(2,1)}, u32[]{:S(2)}, u32[]{:S(2)}) %all-to-all-start.1) | async-done | bytes 3145760 | tf_op jit(solution)/shard_map/all_to_all | solution.py:54
  334.5 6.6 %gather_team.1 = (f32[32,256,128]{2,1,0:T(8,128)}, bf16[3,256,128]{2,1,0:T(8,128)(2,1)}, bf16[3,256,128]{2,1,0:T(8,128)(2,1)}, bf16[3,256,128]{2,1,0:T(8,128)(2,...) custom-call(s32[96]{0:T(128)} %get-tuple-element.66.used_ref, ...), custom_call_target="tpu_custom_call", output_to_operand_aliasing={{0}: (3, {}), {1}: (6, {}), {2}: (7, {}), {3}: (8, {}), {4}... | custom-call | flops 1572864 | bytes 11534336 | tf_op jit(solution)/shard_map/gather_team/pallas_call | solution.py:407
  341.2 2.7 collective-permute-start.25
  344.2 5.2 %collective-permute-start.27 = (bf16[3,256,128]{2,1,0:T(8,128)(2,1)}, bf16[3,256,128]{2,1,0:T(8,128)(2,1)S(1)}, u32[]{:S(2)}, u32[]{:S(2)}) collective-permute-start(bf16[3,256,128]{2,1,0:T(8,128)(2,1)} %get-tuple-element.119), channel_id=1, source_target_pairs={{0,176},{8,184},{16,160},{24,168},{32,208},{40,216},{48,192},{56,2... | collective-permute-start | bytes 589832 | tf_op jit(solution)/shard_map/ppermute | solution.py:38
  349.7 3.3 collective-permute-start.28
  353.1 3.1 collective-permute-start.29
  356.2 0.9 collective-permute-done.25.rest_6_
  357.6 6.6 %collective-permute-start.31 = (bf16[3,256,128]{2,1,0:T(8,128)(2,1)}, bf16[3,256,128]{2,1,0:T(8,128)(2,1)S(1)}, u32[]{:S(2)}, u32[]{:S(2)}) collective-permute-start(bf16[3,256,128]{2,1,0:T(8,128)(2,1)} %get-tuple-element.123), channel_id=1, source_target_pairs={{0,168},{8,176},{16,184},{24,160},{32,200},{40,208},{48,216},{56,1... | collective-permute-start | bytes 589832 | tf_op jit(solution)/shard_map/ppermute | solution.py:38
  364.1 3.6 collective-permute-done.27.rest_8_
  367.8 5.0 %collective-permute-start.32 = (bf16[3,256,128]{2,1,0:T(8,128)(2,1)}, bf16[3,256,128]{2,1,0:T(8,128)(2,1)S(1)}, u32[]{:S(2)}, u32[]{:S(2)}) collective-permute-start(bf16[3,256,128]{2,1,0:T(8,128)(2,1)} %get-tuple-element.124), channel_id=1, source_target_pairs={{0,120},{8,96},{16,104},{24,112},{32,152},{40,128},{48,136},{56,14... | collective-permute-start | bytes 589832 | tf_op jit(solution)/shard_map/ppermute | solution.py:38
  372.7 2.1 collective-permute-start.33
  374.9 1.5 collective-permute-done.29.rest_10_
  376.4 2.3 collective-permute-start.34
  378.6 1.0 collective-permute-done.30.rest_11_
  379.7 7.5 %collective-permute-done.32.rest_13_ = bf16[3,256,128]{2,1,0:T(8,128)(2,1)S(1)} collective-permute-done((bf16[3,256,128]{2,1,0:T(8,128)(2,1)}, bf16[3,256,128]{2,1,0:T(8,128)(2,1)S(1)}, u32[]{:S(2)}, u32[]{:S(2)}) %collective-permute-start.32) | collective-permute-done | bytes 196640 | tf_op jit(solution)/shard_map/ppermute | solution.py:38
  387.2 2.0 collective-permute-done.33.rest_14_
  389.9 12.1 %gather_and_mix.1 = bf16[8192,128]{1,0:T(8,128)(2,1)} custom-call(s32[96]{0:T(128)} %get-tuple-element.66.used_ref, s32[16]{0:T(128)} %stack.70.dests_ref, f32[32,256,128]{2,1,0:T(8,128)} %get-tuple-element.110.total_ref, bf16[8192,128]{1,0:T(8,128)(2,1)} %bitcast.28, bf16[128,128]{1,0:T(8,128)(2,1)} %w_ref.1, f32[1,128]{1,0:T(1,128)} %bitcast.36, ...), custom_call_target="tpu_custom_call" | custom-call | tf_op jit(solution)/shard_map/gather_and_mix/pallas_call | solution.py:451
  (105 shorter events, 5.1 us)
Async XLA Ops:
  14.7 23.9 %collective-permute-start.1 = (bf16[8,384,128]{2,1,0:T(8,128)(2,1)}, bf16[8,384,128]{2,1,0:T(8,128)(2,1)S(1)}, u32[]{:S(2)}, u32[]{:S(2)}) collective-permute-start(bf16[8,384,128]{2,1,0:T(8,128)(2,1)} %get-tuple-element.69), channel_id=1, source_target_pairs={{0,1},{1,2},{2,3},{3,4},{4,5},{5,6},{6,7},{8,9},{9,10},{10,11},{11... | collective-permute-start | bytes 2359304 | tf_op jit(solution)/shard_map/ppermute | solution.py:62
  16.7 21.1 %collective-permute-start = (s32[8,2]{0,1:T(2,128)S(1)}, s32[8,2]{0,1:T(2,128)S(1)}, u32[]{:S(2)}, u32[]{:S(2)}) collective-permute-start(s32[8,2]{0,1:T(2,128)S(1)} %pad_add_fusion), channel_id=1, source_target_pairs={{0,1},{1,2},{2,3},{3,4},{4,5},{5,6},{6,7},{8,9},{9,10},{10,11},{11... | collective-permute-start | bytes 200 | tf_op jit(solution)/shard_map/ppermute | solution.py:62
  20.2 145.3 %all-to-all-start = ((bf16[16,1168,128]{2,1,0:T(8,128)(2,1)}), bf16[16,1168,128]{2,1,0:T(8,128)(2,1)}, u32[]{:S(2)}, u32[]{:S(2)}) async-start(bf16[16,1168,128]{2,1,0:T(8,128)(2,1)} %get-tuple-element.68), calls=%async_computation | async-start | bytes 9568256 | tf_op jit(solution)/shard_map/all_to_all | solution.py:54
  30.9 126.8 %collective-permute-start.2 = (bf16[1168,128]{1,0:T(8,128)(2,1)}, bf16[1168,128]{1,0:T(8,128)(2,1)}, u32[]{:S(2)}, u32[]{:S(2)}) collective-permute-start(bf16[1168,128]{1,0:T(8,128)(2,1)} %get-tuple-element.80), channel_id=1, source_target_pairs={{0,96},{8,104},{16,112},{24,120},{32,128},{40,136},{48,144},{56,15... | collective-permute-start | bytes 897032 | tf_op jit(solution)/shard_map/ppermute | solution.py:38
  35.8 123.7 %collective-permute-start.3 = (bf16[1168,128]{1,0:T(8,128)(2,1)}, bf16[1168,128]{1,0:T(8,128)(2,1)}, u32[]{:S(2)}, u32[]{:S(2)}) collective-permute-start(bf16[1168,128]{1,0:T(8,128)(2,1)} %get-tuple-element.81), channel_id=1, source_target_pairs={{0,160},{8,168},{16,176},{24,184},{32,192},{40,200},{48,208},{56,2... | collective-permute-start | bytes 897032 | tf_op jit(solution)/shard_map/ppermute | solution.py:38
  35.9 126.8 %collective-permute-start.4 = (bf16[1168,128]{1,0:T(8,128)(2,1)}, bf16[1168,128]{1,0:T(8,128)(2,1)}, u32[]{:S(2)}, u32[]{:S(2)}) collective-permute-start(bf16[1168,128]{1,0:T(8,128)(2,1)} %get-tuple-element.82), channel_id=1, source_target_pairs={{0,32},{8,40},{16,48},{24,56},{32,64},{40,72},{48,80},{56,88},{64,... | collective-permute-start | bytes 897032 | tf_op jit(solution)/shard_map/ppermute | solution.py:38
  37.8 143.3 %collective-permute-start.5 = (bf16[1168,128]{1,0:T(8,128)(2,1)}, bf16[1168,128]{1,0:T(8,128)(2,1)}, u32[]{:S(2)}, u32[]{:S(2)}) collective-permute-start(bf16[1168,128]{1,0:T(8,128)(2,1)} %get-tuple-element.83), channel_id=1, source_target_pairs={{0,224},{8,232},{16,240},{24,248},{32,0},{40,8},{48,16},{56,24},{6... | collective-permute-start | bytes 897032 | tf_op jit(solution)/shard_map/ppermute | solution.py:38
  38.7 149.8 %collective-permute-start.6 = (bf16[1168,128]{1,0:T(8,128)(2,1)}, bf16[1168,128]{1,0:T(8,128)(2,1)}, u32[]{:S(2)}, u32[]{:S(2)}) collective-permute-start(bf16[1168,128]{1,0:T(8,128)(2,1)} %get-tuple-element.84), channel_id=1, source_target_pairs={{0,104},{8,112},{16,120},{24,96},{32,136},{40,144},{48,152},{56,12... | collective-permute-start | bytes 897032 | tf_op jit(solution)/shard_map/ppermute | solution.py:38
  45.7 112.0 %copy-start.27 = (bf16[1168,128]{1,0:T(8,128)(2,1)S(1)}, bf16[1168,128]{1,0:T(8,128)(2,1)}, u32[]{:S(2)}) copy-start(bf16[1168,128]{1,0:T(8,128)(2,1)} %get-tuple-element.85) | copy-start | bytes 897028
  45.7 113.8 %copy-start.26 = (bf16[1168,128]{1,0:T(8,128)(2,1)S(1)}, bf16[1168,128]{1,0:T(8,128)(2,1)}, u32[]{:S(2)}) copy-start(bf16[1168,128]{1,0:T(8,128)(2,1)} %get-tuple-element.86) | copy-start | bytes 897028
  45.7 117.1 %copy-start.25 = (bf16[1168,128]{1,0:T(8,128)(2,1)S(1)}, bf16[1168,128]{1,0:T(8,128)(2,1)}, u32[]{:S(2)}) copy-start(bf16[1168,128]{1,0:T(8,128)(2,1)} %get-tuple-element.87) | copy-start | bytes 897028
  157.7 30.9 %collective-permute-start.7 = (bf16[1168,128]{1,0:T(8,128)(2,1)S(1)}, bf16[1168,128]{1,0:T(8,128)(2,1)S(1)}, u32[]{:S(2)}, u32[]{:S(2)}) collective-permute-start(bf16[1168,128]{1,0:T(8,128)(2,1)S(1)} %copy-done.27), channel_id=1, source_target_pairs={{0,184},{8,160},{16,168},{24,176},{32,216},{40,192},{48,200},{56,2... | collective-permute-start | bytes 897032 | tf_op jit(solution)/shard_map/ppermute | solution.py:38
  159.5 31.5 %collective-permute-start.8 = (bf16[1168,128]{1,0:T(8,128)(2,1)S(1)}, bf16[1168,128]{1,0:T(8,128)(2,1)S(1)}, u32[]{:S(2)}, u32[]{:S(2)}) collective-permute-start(bf16[1168,128]{1,0:T(8,128)(2,1)S(1)} %copy-done.26), channel_id=1, source_target_pairs={{0,40},{8,48},{16,56},{24,32},{32,72},{40,80},{48,88},{56,64},{64,... | collective-permute-start | bytes 897032 | tf_op jit(solution)/shard_map/ppermute | solution.py:38
  162.8 30.3 %collective-permute-start.9 = (bf16[1168,128]{1,0:T(8,128)(2,1)S(1)}, bf16[1168,128]{1,0:T(8,128)(2,1)S(1)}, u32[]{:S(2)}, u32[]{:S(2)}) collective-permute-start(bf16[1168,128]{1,0:T(8,128)(2,1)S(1)} %copy-done.25), channel_id=1, source_target_pairs={{0,248},{8,224},{16,232},{24,240},{32,24},{40,0},{48,8},{56,16},{6... | collective-permute-start | bytes 897032 | tf_op jit(solution)/shard_map/ppermute | solution.py:38
  165.6 27.5 %copy-start.24 = (bf16[8,256,128]{2,1,0:T(8,128)(2,1)S(1)}, bf16[8,256,128]{2,1,0:T(8,128)(2,1)}, u32[]{:S(2)}) copy-start(bf16[8,256,128]{2,1,0:T(8,128)(2,1)} %get-tuple-element.101) | copy-start | bytes 1572868
  181.1 29.5 %collective-permute-start.10 = (bf16[1168,128]{1,0:T(8,128)(2,1)}, bf16[1168,128]{1,0:T(8,128)(2,1)S(1)}, u32[]{:S(2)}, u32[]{:S(2)}) collective-permute-start(bf16[1168,128]{1,0:T(8,128)(2,1)} %get-tuple-element.90), channel_id=1, source_target_pairs={{0,112},{8,120},{16,96},{24,104},{32,144},{40,152},{48,128},{56,13... | collective-permute-start | bytes 897032 | tf_op jit(solution)/shard_map/ppermute | solution.py:38
  188.5 30.2 %collective-permute-start.11 = (bf16[1168,128]{1,0:T(8,128)(2,1)}, bf16[1168,128]{1,0:T(8,128)(2,1)S(1)}, u32[]{:S(2)}, u32[]{:S(2)}) collective-permute-start(bf16[1168,128]{1,0:T(8,128)(2,1)} %get-tuple-element.91), channel_id=1, source_target_pairs={{0,176},{8,184},{16,160},{24,168},{32,208},{40,216},{48,192},{56,2... | collective-permute-start | bytes 897032 | tf_op jit(solution)/shard_map/ppermute | solution.py:38
  188.6 30.1 %copy-start.2 = (bf16[1168,128]{1,0:T(8,128)(2,1)}, bf16[1168,128]{1,0:T(8,128)(2,1)S(1)}, u32[]{:S(2)}) copy-start(bf16[1168,128]{1,0:T(8,128)(2,1)S(1)} %collective-permute-done.7.rest_7_) | copy-start | bytes 897028
  188.6 41.0 %collective-permute-start.12 = (bf16[1168,128]{1,0:T(8,128)(2,1)}, bf16[1168,128]{1,0:T(8,128)(2,1)S(1)}, u32[]{:S(2)}, u32[]{:S(2)}) collective-permute-start(bf16[1168,128]{1,0:T(8,128)(2,1)} %get-tuple-element.92), channel_id=1, source_target_pairs={{0,48},{8,56},{16,32},{24,40},{32,80},{40,88},{48,64},{56,72},{64,... | collective-permute-start | bytes 897032 | tf_op jit(solution)/shard_map/ppermute | solution.py:38
  191.0 27.8 %copy-start.4 = (bf16[1168,128]{1,0:T(8,128)(2,1)}, bf16[1168,128]{1,0:T(8,128)(2,1)S(1)}, u32[]{:S(2)}) copy-start(bf16[1168,128]{1,0:T(8,128)(2,1)S(1)} %collective-permute-done.8.rest_8_) | copy-start | bytes 897028
  191.0 38.7 %collective-permute-start.13 = (bf16[1168,128]{1,0:T(8,128)(2,1)}, bf16[1168,128]{1,0:T(8,128)(2,1)S(1)}, u32[]{:S(2)}, u32[]{:S(2)}) collective-permute-start(bf16[1168,128]{1,0:T(8,128)(2,1)} %get-tuple-element.93), channel_id=1, source_target_pairs={{0,240},{8,248},{16,224},{24,232},{32,16},{40,24},{48,0},{56,8},{6... | collective-permute-start | bytes 897032 | tf_op jit(solution)/shard_map/ppermute | solution.py:38
  193.1 25.7 %copy-start.6 = (bf16[1168,128]{1,0:T(8,128)(2,1)}, bf16[1168,128]{1,0:T(8,128)(2,1)S(1)}, u32[]{:S(2)}) copy-start(bf16[1168,128]{1,0:T(8,128)(2,1)S(1)} %collective-permute-done.9.rest_9_) | copy-start | bytes 897028
  193.1 68.8 %collective-permute-start.18 = (bf16[8,256,128]{2,1,0:T(8,128)(2,1)S(1)}, bf16[8,256,128]{2,1,0:T(8,128)(2,1)S(1)}, u32[]{:S(2)}, u32[]{:S(2)}) collective-permute-start(bf16[8,256,128]{2,1,0:T(8,128)(2,1)S(1)} %copy-done.24), channel_id=1, source_target_pairs={{1,0},{2,1},{3,2},{4,3},{5,4},{6,5},{7,6},{9,8},{10,9},{11,10},{12... | collective-permute-start | bytes 1572872 | tf_op jit(solution)/shard_map/ppermute | solution.py:62
  210.6 19.0 %copy-start.1 = (bf16[1168,128]{1,0:T(8,128)(2,1)}, bf16[1168,128]{1,0:T(8,128)(2,1)S(1)}, u32[]{:S(2)}) copy-start(bf16[1168,128]{1,0:T(8,128)(2,1)S(1)} %collective-permute-done.10.rest_1_) | copy-start | bytes 897028
  210.6 28.9 %collective-permute-start.14 = (bf16[1168,128]{1,0:T(8,128)(2,1)}, bf16[1168,128]{1,0:T(8,128)(2,1)S(1)}, u32[]{:S(2)}, u32[]{:S(2)}) collective-permute-start(bf16[1168,128]{1,0:T(8,128)(2,1)} %get-tuple-element.94), channel_id=1, source_target_pairs={{0,120},{8,96},{16,104},{24,112},{32,152},{40,128},{48,136},{56,14... | collective-permute-start | bytes 897032 | tf_op jit(solution)/shard_map/ppermute | solution.py:38
  218.8 20.7 %collective-permute-start.15 = (bf16[1168,128]{1,0:T(8,128)(2,1)}, bf16[1168,128]{1,0:T(8,128)(2,1)S(1)}, u32[]{:S(2)}, u32[]{:S(2)}) collective-permute-start(bf16[1168,128]{1,0:T(8,128)(2,1)} %get-tuple-element.95), channel_id=1, source_target_pairs={{0,168},{8,176},{16,184},{24,160},{32,200},{40,208},{48,216},{56,1... | collective-permute-start | bytes 897032 | tf_op jit(solution)/shard_map/ppermute | solution.py:38
  229.6 35.0 %collective-permute-start.16 = (bf16[1168,128]{1,0:T(8,128)(2,1)}, bf16[1168,128]{1,0:T(8,128)(2,1)S(1)}, u32[]{:S(2)}, u32[]{:S(2)}) collective-permute-start(bf16[1168,128]{1,0:T(8,128)(2,1)} %get-tuple-element.97), channel_id=1, source_target_pairs={{0,56},{8,32},{16,40},{24,48},{32,88},{40,64},{48,72},{56,80},{64,... | collective-permute-start | bytes 897032 | tf_op jit(solution)/shard_map/ppermute | solution.py:38
  229.7 38.9 %collective-permute-start.17 = (bf16[1168,128]{1,0:T(8,128)(2,1)}, bf16[1168,128]{1,0:T(8,128)(2,1)S(1)}, u32[]{:S(2)}, u32[]{:S(2)}) collective-permute-start(bf16[1168,128]{1,0:T(8,128)(2,1)} %get-tuple-element.98), channel_id=1, source_target_pairs={{0,232},{8,240},{16,248},{24,224},{32,8},{40,16},{48,24},{56,0},{6... | collective-permute-start | bytes 897032 | tf_op jit(solution)/shard_map/ppermute | solution.py:38
  239.4 24.1 %collective-permute-start.19 = (bf16[3,256,128]{2,1,0:T(8,128)(2,1)}, bf16[3,256,128]{2,1,0:T(8,128)(2,1)S(1)}, u32[]{:S(2)}, u32[]{:S(2)}) collective-permute-start(bf16[3,256,128]{2,1,0:T(8,128)(2,1)} %get-tuple-element.111), channel_id=1, source_target_pairs={{0,160},{8,168},{16,176},{24,184},{32,192},{40,200},{48,208},{56,2... | collective-permute-start | bytes 589832 | tf_op jit(solution)/shard_map/ppermute | solution.py:38
  239.5 101.7 %collective-permute-start.20 = (bf16[3,256,128]{2,1,0:T(8,128)(2,1)}, bf16[3,256,128]{2,1,0:T(8,128)(2,1)}, u32[]{:S(2)}, u32[]{:S(2)}) collective-permute-start(bf16[3,256,128]{2,1,0:T(8,128)(2,1)} %get-tuple-element.112), channel_id=1, source_target_pairs={{0,96},{8,104},{16,112},{24,120},{32,128},{40,136},{48,144},{56,15... | collective-permute-start | bytes 589832 | tf_op jit(solution)/shard_map/ppermute | solution.py:38
  253.9 80.6 %all-to-all-start.1 = ((bf16[48,256,128]{2,1,0:T(8,128)(2,1)}), bf16[48,256,128]{2,1,0:T(8,128)(2,1)}, u32[]{:S(2)}, u32[]{:S(2)}) async-start(bf16[48,256,128]{2,1,0:T(8,128)(2,1)} %get-tuple-element.100), calls=%async_computation.1 | async-start | bytes 6291456 | tf_op jit(solution)/shard_map/all_to_all | solution.py:54
  261.9 82.0 %collective-permute-start.21 = (bf16[3,256,128]{2,1,0:T(8,128)(2,1)}, bf16[3,256,128]{2,1,0:T(8,128)(2,1)}, u32[]{:S(2)}, u32[]{:S(2)}) collective-permute-start(bf16[3,256,128]{2,1,0:T(8,128)(2,1)} %get-tuple-element.113), channel_id=1, source_target_pairs={{0,224},{8,232},{16,240},{24,248},{32,0},{40,8},{48,16},{56,24},{6... | collective-permute-start | bytes 589832 | tf_op jit(solution)/shard_map/ppermute | solution.py:38
  263.6 80.6 %collective-permute-start.22 = (bf16[3,256,128]{2,1,0:T(8,128)(2,1)}, bf16[3,256,128]{2,1,0:T(8,128)(2,1)}, u32[]{:S(2)}, u32[]{:S(2)}) collective-permute-start(bf16[3,256,128]{2,1,0:T(8,128)(2,1)} %get-tuple-element.114), channel_id=1, source_target_pairs={{0,32},{8,40},{16,48},{24,56},{32,64},{40,72},{48,80},{56,88},{64,... | collective-permute-start | bytes 589832 | tf_op jit(solution)/shard_map/ppermute | solution.py:38
  264.6 85.1 %collective-permute-start.23 = (bf16[3,256,128]{2,1,0:T(8,128)(2,1)}, bf16[3,256,128]{2,1,0:T(8,128)(2,1)}, u32[]{:S(2)}, u32[]{:S(2)}) collective-permute-start(bf16[3,256,128]{2,1,0:T(8,128)(2,1)} %get-tuple-element.115), channel_id=1, source_target_pairs={{0,184},{8,160},{16,168},{24,176},{32,216},{40,192},{48,200},{56,2... | collective-permute-start | bytes 589832 | tf_op jit(solution)/shard_map/ppermute | solution.py:38
  268.6 84.4 %collective-permute-start.24 = (bf16[3,256,128]{2,1,0:T(8,128)(2,1)}, bf16[3,256,128]{2,1,0:T(8,128)(2,1)}, u32[]{:S(2)}, u32[]{:S(2)}) collective-permute-start(bf16[3,256,128]{2,1,0:T(8,128)(2,1)} %get-tuple-element.116), channel_id=1, source_target_pairs={{0,104},{8,112},{16,120},{24,96},{32,136},{40,144},{48,152},{56,12... | collective-permute-start | bytes 589832 | tf_op jit(solution)/shard_map/ppermute | solution.py:38
  341.2 15.9 %collective-permute-start.25 = (bf16[3,256,128]{2,1,0:T(8,128)(2,1)S(1)}, bf16[3,256,128]{2,1,0:T(8,128)(2,1)S(1)}, u32[]{:S(2)}, u32[]{:S(2)}) collective-permute-start(bf16[3,256,128]{2,1,0:T(8,128)(2,1)S(1)} %copy-done.31), channel_id=1, source_target_pairs={{0,248},{8,224},{16,232},{24,240},{32,24},{40,0},{48,8},{56,16},{6... | collective-permute-start | bytes 589832 | tf_op jit(solution)/shard_map/ppermute | solution.py:38
  343.9 13.7 %collective-permute-start.26 = (bf16[3,256,128]{2,1,0:T(8,128)(2,1)S(1)}, bf16[3,256,128]{2,1,0:T(8,128)(2,1)S(1)}, u32[]{:S(2)}, u32[]{:S(2)}) collective-permute-start(bf16[3,256,128]{2,1,0:T(8,128)(2,1)S(1)} %copy-done.30), channel_id=1, source_target_pairs={{0,40},{8,48},{16,56},{24,32},{32,72},{40,80},{48,88},{56,64},{64,... | collective-permute-start | bytes 589832 | tf_op jit(solution)/shard_map/ppermute | solution.py:38
  344.2 23.6 %collective-permute-start.27 = (bf16[3,256,128]{2,1,0:T(8,128)(2,1)}, bf16[3,256,128]{2,1,0:T(8,128)(2,1)S(1)}, u32[]{:S(2)}, u32[]{:S(2)}) collective-permute-start(bf16[3,256,128]{2,1,0:T(8,128)(2,1)} %get-tuple-element.119), channel_id=1, source_target_pairs={{0,176},{8,184},{16,160},{24,168},{32,208},{40,216},{48,192},{56,2... | collective-permute-start | bytes 589832 | tf_op jit(solution)/shard_map/ppermute | solution.py:38
  349.7 23.0 %collective-permute-start.28 = (bf16[3,256,128]{2,1,0:T(8,128)(2,1)}, bf16[3,256,128]{2,1,0:T(8,128)(2,1)S(1)}, u32[]{:S(2)}, u32[]{:S(2)}) collective-permute-start(bf16[3,256,128]{2,1,0:T(8,128)(2,1)} %get-tuple-element.120), channel_id=1, source_target_pairs={{0,112},{8,120},{16,96},{24,104},{32,144},{40,152},{48,128},{56,13... | collective-permute-start | bytes 589832 | tf_op jit(solution)/shard_map/ppermute | solution.py:38
  353.1 23.3 %collective-permute-start.29 = (bf16[3,256,128]{2,1,0:T(8,128)(2,1)}, bf16[3,256,128]{2,1,0:T(8,128)(2,1)S(1)}, u32[]{:S(2)}, u32[]{:S(2)}) collective-permute-start(bf16[3,256,128]{2,1,0:T(8,128)(2,1)} %get-tuple-element.121), channel_id=1, source_target_pairs={{0,240},{8,248},{16,224},{24,232},{32,16},{40,24},{48,0},{56,8},{6... | collective-permute-start | bytes 589832 | tf_op jit(solution)/shard_map/ppermute | solution.py:38
  357.1 32.1 %copy-start.11 = (bf16[3,256,128]{2,1,0:T(8,128)(2,1)}, bf16[3,256,128]{2,1,0:T(8,128)(2,1)S(1)}, u32[]{:S(2)}) copy-start(bf16[3,256,128]{2,1,0:T(8,128)(2,1)S(1)} %collective-permute-done.25.rest_6_) | copy-start | bytes 589828
  357.1 22.6 %collective-permute-start.30 = (bf16[3,256,128]{2,1,0:T(8,128)(2,1)}, bf16[3,256,128]{2,1,0:T(8,128)(2,1)S(1)}, u32[]{:S(2)}, u32[]{:S(2)}) collective-permute-start(bf16[3,256,128]{2,1,0:T(8,128)(2,1)} %get-tuple-element.122), channel_id=1, source_target_pairs={{0,48},{8,56},{16,32},{24,40},{32,80},{40,88},{48,64},{56,72},{64,... | collective-permute-start | bytes 589832 | tf_op jit(solution)/shard_map/ppermute | solution.py:38
  357.5 31.6 %copy-start.12 = (bf16[3,256,128]{2,1,0:T(8,128)(2,1)}, bf16[3,256,128]{2,1,0:T(8,128)(2,1)S(1)}, u32[]{:S(2)}) copy-start(bf16[3,256,128]{2,1,0:T(8,128)(2,1)S(1)} %collective-permute-done.26.rest_7_) | copy-start | bytes 589828
  357.6 22.1 %collective-permute-start.31 = (bf16[3,256,128]{2,1,0:T(8,128)(2,1)}, bf16[3,256,128]{2,1,0:T(8,128)(2,1)S(1)}, u32[]{:S(2)}, u32[]{:S(2)}) collective-permute-start(bf16[3,256,128]{2,1,0:T(8,128)(2,1)} %get-tuple-element.123), channel_id=1, source_target_pairs={{0,168},{8,176},{16,184},{24,160},{32,200},{40,208},{48,216},{56,1... | collective-permute-start | bytes 589832 | tf_op jit(solution)/shard_map/ppermute | solution.py:38
  367.8 21.4 %copy-start.13 = (bf16[3,256,128]{2,1,0:T(8,128)(2,1)}, bf16[3,256,128]{2,1,0:T(8,128)(2,1)S(1)}, u32[]{:S(2)}) copy-start(bf16[3,256,128]{2,1,0:T(8,128)(2,1)S(1)} %collective-permute-done.27.rest_8_) | copy-start | bytes 589828
  367.8 19.4 %collective-permute-start.32 = (bf16[3,256,128]{2,1,0:T(8,128)(2,1)}, bf16[3,256,128]{2,1,0:T(8,128)(2,1)S(1)}, u32[]{:S(2)}, u32[]{:S(2)}) collective-permute-start(bf16[3,256,128]{2,1,0:T(8,128)(2,1)} %get-tuple-element.124), channel_id=1, source_target_pairs={{0,120},{8,96},{16,104},{24,112},{32,152},{40,128},{48,136},{56,14... | collective-permute-start | bytes 589832 | tf_op jit(solution)/shard_map/ppermute | solution.py:38
  372.7 16.4 %collective-permute-start.33 = (bf16[3,256,128]{2,1,0:T(8,128)(2,1)}, bf16[3,256,128]{2,1,0:T(8,128)(2,1)S(1)}, u32[]{:S(2)}, u32[]{:S(2)}) collective-permute-start(bf16[3,256,128]{2,1,0:T(8,128)(2,1)} %get-tuple-element.125), channel_id=1, source_target_pairs={{0,232},{8,240},{16,248},{24,224},{32,8},{40,16},{48,24},{56,0},{6... | collective-permute-start | bytes 589832 | tf_op jit(solution)/shard_map/ppermute | solution.py:38
  376.4 12.8 %collective-permute-start.34 = (bf16[3,256,128]{2,1,0:T(8,128)(2,1)}, bf16[3,256,128]{2,1,0:T(8,128)(2,1)S(1)}, u32[]{:S(2)}, u32[]{:S(2)}) collective-permute-start(bf16[3,256,128]{2,1,0:T(8,128)(2,1)} %get-tuple-element.126), channel_id=1, source_target_pairs={{0,56},{8,32},{16,40},{24,48},{32,88},{40,64},{48,72},{56,80},{64,... | collective-permute-start | bytes 589832 | tf_op jit(solution)/shard_map/ppermute | solution.py:38
  (21 other events, 196.0 us)
where the time goes:
time: 405 us; the launch traced here: 402 us
  waiting for transfers between devices  201 us (50%)
  starting transfers between devices  118 us (29%)
  Pallas kernels  78.9 us (19%)
    ppermute x32, waiting for transfers between devices, space_shift(): lax.ppermute(value, 'space', [(z * SPAN_Y + y, (z + shift[0]) % SPAN_Z *...  143 us
    ppermute x32, starting transfers between devices, space_shift(): lax.ppermute(value, 'space', [(z * SPAN_Y + y, (z + shift[0]) % SPAN_Z *...  92 us
    all_to_all x2, waiting for transfers between devices, team_exchange(): lax.all_to_all(value, 'space', split_axis=0, concat_axis=0, tiled=True, a...  57.3 us
    pallas_call x3, Pallas kernels, shifted_pairs(): pl.pallas_call(kernel, in_specs=[VMEM] * 2 + [ANYWHERE] * handed + [VMEM]...  26.7 us
    all_to_all x2, starting transfers between devices, team_exchange(): lax.all_to_all(value, 'space', split_axis=0, concat_axis=0, tiled=True, a...  18.7 us
    pallas_call x1, Pallas kernels, team_pairs(): pl.pallas_call(kernel, grid=(MEMBERS // CREW,), in_specs=[pl.BlockSpec((C...  15.5 us
    pallas_call x1, Pallas kernels, gather_and_mix(): pl.pallas_call(kernel, grid_spec=pltpu.PrefetchScalarGridSpec(num_scalar_...  12.1 us
    pallas_call x1, Pallas kernels, project_and_pack(): pl.pallas_call(kernel, grid_spec=pltpu.PrefetchScalarGridSpec(num_scalar_...  12 us
  transfers between devices with their start and end apart: 37, of which 11 were waited for; matrix products, arithmetic and copies ran while one was open for 0% of the time, Pallas kernels for 14%

commit v1 on v0

--- a/solution.py
+++ b/solution.py
@@ -20,6 +20,8 @@
     shift for dy in range(SPAN_Y) for shift in ((3, dy), (-3, -dy), (1, dy), (-1, -dy))
 )
 BATCHES = ((0, 8), (8, 14), (14, 16))
+GATES = (4, 14)
+GATE = 0
 PASSED = 1
 MEMBERS = SPACES // 2
 TEAMS = [[z * SPAN_Y + y for z in range(p, SPAN_Z, 2) for y in range(SPAN_Y)] for p in range(2)]
@@ -110,7 +112,7 @@
                     note = jnp.where(row == 2 * CAP + j, cut % 16, note)
                 notes[d] = note.astype(jnp.float32).astype(jnp.bfloat16)
 
-        @pl.loop(0, step, unroll=2)
+        @pl.loop(0, step, unroll=4)
         def _(b):
             upper = pl.ds(pl.multiple_of(b * BLK, BLK), HALF)
             lower = pl.ds(pl.multiple_of(b * BLK + HALF, HALF), HALF)
@@ -494,16 +496,13 @@
 
     back_x, aggregate = pairs_above(cross_meta, below, own)
     returned_x = group_shift(back_x, -1)
-    send(*BATCHES[0])
-    first, end = BATCHES[1]
-    back, aggregate, shifting[first:end] = team_pairs(
-        arrived, own, aggregate, shifting[first:end]
-    )
+    send(0, GATES[0])
+    first, end = GATES
+    back, aggregate, shifting[first:end] = team_pairs(arrived, own, aggregate, shifting[first:end])
+    send(first, end)
     going_back = []
     for turn, (first, end) in enumerate(BATCHES):
-        later = slice(*BATCHES[turn + 2]) if turn + 2 < len(BATCHES) else slice(0, 0)
-        if turn + 1 < len(BATCHES):
-            send(*BATCHES[turn + 1])
+        later = slice(GATES[1], len(SHIFTS)) if turn == GATE else slice(0, 0)
         passing = shifting[later] + ([back] if turn == PASSED else [])
         back_some, aggregate, passing = shifted_pairs(
             shifted[first:end], own, aggregate, passing,
@@ -512,6 +511,8 @@
             else pair_cost((end - first) * CAP, own.shape[0]),
         )
         shifting[later] = passing[: later.stop - later.start]
+        if turn == GATE:
+            send(GATES[1], len(SHIFTS))
         if turn == PASSED:
             returned = team_exchange(passing[-1])
         going_back += back_some

time: 405 us -> 404 us (level)
  starting transfers between devices: 118 us -> 126 us
  waiting for transfers between devices: 201 us -> 194 us
    ppermute x32, waiting for transfers between devices: 143 us -> 41 us  [space_shift(): lax.ppermute(value, 'space', [(z * SPAN_Y + y, (z + shift[0]) % SPAN_Z *...]
    all_to_all x2, waiting for transfers between devices: 57.3 us -> 153 us  [team_exchange(): lax.all_to_all(value, 'space', split_axis=0, concat_axis=0, tiled=True, a...]
    ppermute x32, starting transfers between devices: 92 us -> 100 us  [space_shift(): lax.ppermute(value, 'space', [(z * SPAN_Y + y, (z + shift[0]) % SPAN_Z *...]
  transfers between devices with their start and end apart: 37 -> 37, of which waited for: 11 -> 10; matrix products, arithmetic and copies ran while one was open for 0% -> 0% of each run, Pallas kernels for 14% -> 14%
where the time goes in v1:
time: 404 us; the launch traced here: 403 us
  waiting for transfers between devices  194 us (48%)
  starting transfers between devices  126 us (31%)
  Pallas kernels  77.9 us (19%)
    all_to_all x2, waiting for transfers between devices, team_exchange(): lax.all_to_all(value, 'space', split_axis=0, concat_axis=0, tiled=True, a...  153 us
    ppermute x32, starting transfers between devices, space_shift(): lax.ppermute(value, 'space', [(z * SPAN_Y + y, (z + shift[0]) % SPAN_Z *...  100 us
    ppermute x32, waiting for transfers between devices, space_shift(): lax.ppermute(value, 'space', [(z * SPAN_Y + y, (z + shift[0]) % SPAN_Z *...  41 us
    pallas_call x3, Pallas kernels, shifted_pairs(): pl.pallas_call(kernel, in_specs=[VMEM] * 2 + [ANYWHERE] * handed + [VMEM]...  26.5 us
    all_to_all x2, starting transfers between devices, team_exchange(): lax.all_to_all(value, 'space', split_axis=0, concat_axis=0, tiled=True, a...  18.6 us
    pallas_call x1, Pallas kernels, team_pairs(): pl.pallas_call(kernel, grid=(MEMBERS // CREW,), in_specs=[pl.BlockSpec((C...  15.5 us
    pallas_call x1, Pallas kernels, gather_and_mix(): pl.pallas_call(kernel, grid_spec=pltpu.PrefetchScalarGridSpec(num_scalar_...  12.1 us
    pallas_call x1, Pallas kernels, project_and_pack(): pl.pallas_call(kernel, grid_spec=pltpu.PrefetchScalarGridSpec(num_scalar_...  11.1 us
  transfers between devices with their start and end apart: 37, of which 10 were waited for; matrix products, arithmetic and copies ran while one was open for 0% of the time, Pallas kernels for 14%

profile of v1, /device:TPU:42, one launch (start us, length us, event | category | flops | bytes accessed | tf_op | source)
XLA Modules:
  0.0 403.0 jit_solution(15444857420855017487)
XLA Ops:
  0.5 0.8 copy.42
  1.3 0.7 fusion.2.wk_ref
  2.7 11.1 %project_and_pack.1 = (s32[96]{0:T(128)}, bf16[32,384,128]{2,1,0:T(8,128)(2,1)}, bf16[8,384,128]{2,1,0:T(8,128)(2,1)}, bf16[16,1168,128]{2,1,0:T(8,128)(2,1)}, b...) custom-call(s32[64]{0:T(128)} %bitcast.32, ...), custom_call_target="tpu_custom_call" | custom-call | tf_op jit(solution)/shard_map/project_and_pack/pallas_call | solution.py:155
  13.9 1.9 collective-permute-start.1
  15.8 3.5 collective-permute-start
  19.3 10.7 %all-to-all-start = ((bf16[16,1168,128]{2,1,0:T(8,128)(2,1)}), bf16[16,1168,128]{2,1,0:T(8,128)(2,1)}, u32[]{:S(2)}, u32[]{:S(2)}) async-start(bf16[16,1168,128]{2,1,0:T(8,128)(2,1)} %get-tuple-element.72), calls=%async_computation | async-start | bytes 9568256 | tf_op jit(solution)/shard_map/all_to_all | solution.py:56
  30.0 4.9 %collective-permute-start.2 = (bf16[1168,128]{1,0:T(8,128)(2,1)}, bf16[1168,128]{1,0:T(8,128)(2,1)}, u32[]{:S(2)}, u32[]{:S(2)}) collective-permute-start(bf16[1168,128]{1,0:T(8,128)(2,1)} %get-tuple-element.88), channel_id=1, source_target_pairs={{0,96},{8,104},{16,112},{24,120},{32,128},{40,136},{48,144},{56,15... | collective-permute-start | bytes 897032 | tf_op jit(solution)/shard_map/ppermute | solution.py:40
  35.0 1.9 collective-permute-start.4
  37.8 0.9 copy-done.24
  38.7 5.9 %pairs_above.1 = (bf16[8,256,128]{2,1,0:T(8,128)(2,1)}, f32[32,256,128]{2,1,0:T(8,128)}) custom-call(s32[16]{0:T(128)} %reshape.3.cross_ref, bf16[8,384,128]{2,1,0:T(8,128)(2,1)} %copy-done.24, bf16[32,384,128]{2,1,0:T(8,128)(2,1)} %get-tuple-element.71.own_ref), custom_call_target="tpu_custom_call" | custom-call | flops 999999995904 | tf_op jit(solution)/shard_map/pairs_above/pallas_call | solution.py:257
  44.6 96.3 %all-to-all-done.arrived_ref = bf16[16,1168,128]{2,1,0:T(8,128)(2,1)} async-done(((bf16[16,1168,128]{2,1,0:T(8,128)(2,1)}), bf16[16,1168,128]{2,1,0:T(8,128)(2,1)}, u32[]{:S(2)}, u32[]{:S(2)}) %all-to-all-start) | async-done | bytes 4784160 | tf_op jit(solution)/shard_map/all_to_all | solution.py:56
  140.9 15.5 %team_pairs.1 = (bf16[48,256,128]{2,1,0:T(8,128)(2,1)}, f32[32,256,128]{2,1,0:T(8,128)}, bf16[1168,128]{1,0:T(8,128)(2,1)}, bf16[1168,128]{1,0:T(8,128)(2,1)}, b...) custom-call(bf16[16,1168,128]{2,1,0:T(8,128)(2,1)} %all-to-all-done., ...), custom_call_target="tpu_custom_call", output_to_operand_aliasing={{2}: (3, {}), {3}: (4, {}), {4}: (5, {}), {5}: (6, {}), {6}... | custom-call | flops 2013265920 | bytes 16252928 | tf_op jit(solution)/shard_map/team_pairs/pallas_call | solution.py:305
  156.4 1.2 collective-permute-start.6
  157.7 4.8 %collective-permute-start.7 = (bf16[1168,128]{1,0:T(8,128)(2,1)}, bf16[1168,128]{1,0:T(8,128)(2,1)S(1)}, u32[]{:S(2)}, u32[]{:S(2)}) collective-permute-start(bf16[1168,128]{1,0:T(8,128)(2,1)} %get-tuple-element.93), channel_id=1, source_target_pairs={{0,184},{8,160},{16,168},{24,176},{32,216},{40,192},{48,200},{56,2... | collective-permute-start | bytes 897032 | tf_op jit(solution)/shard_map/ppermute | solution.py:40
  162.5 8.1 %collective-permute-start.8 = (bf16[1168,128]{1,0:T(8,128)(2,1)}, bf16[1168,128]{1,0:T(8,128)(2,1)S(1)}, u32[]{:S(2)}, u32[]{:S(2)}) collective-permute-start(bf16[1168,128]{1,0:T(8,128)(2,1)} %get-tuple-element.94), channel_id=1, source_target_pairs={{0,40},{8,48},{16,56},{24,32},{32,72},{40,80},{48,88},{56,64},{64,... | collective-permute-start | bytes 897032 | tf_op jit(solution)/shard_map/ppermute | solution.py:40
  170.6 3.6 collective-permute-start.10
  174.2 7.7 %collective-permute-done.6.rest_6_ = bf16[1168,128]{1,0:T(8,128)(2,1)S(1)} collective-permute-done((bf16[1168,128]{1,0:T(8,128)(2,1)}, bf16[1168,128]{1,0:T(8,128)(2,1)S(1)}, u32[]{:S(2)}, u32[]{:S(2)}) %collective-permute-start.6) | collective-permute-done | bytes 299040 | tf_op jit(solution)/shard_map/ppermute | solution.py:40
  181.9 5.9 %collective-permute-start.11 = (bf16[1168,128]{1,0:T(8,128)(2,1)}, bf16[1168,128]{1,0:T(8,128)(2,1)S(1)}, u32[]{:S(2)}, u32[]{:S(2)}) collective-permute-start(bf16[1168,128]{1,0:T(8,128)(2,1)} %get-tuple-element.99), channel_id=1, source_target_pairs={{0,176},{8,184},{16,160},{24,168},{32,208},{40,216},{48,192},{56,2... | collective-permute-start | bytes 897032 | tf_op jit(solution)/shard_map/ppermute | solution.py:40
  187.8 0.9 collective-permute-start.12
  188.7 12.8 %collective-permute-start.13 = (bf16[1168,128]{1,0:T(8,128)(2,1)}, bf16[1168,128]{1,0:T(8,128)(2,1)S(1)}, u32[]{:S(2)}, u32[]{:S(2)}) collective-permute-start(bf16[1168,128]{1,0:T(8,128)(2,1)} %get-tuple-element.101), channel_id=1, source_target_pairs={{0,240},{8,248},{16,224},{24,232},{32,16},{40,24},{48,0},{56,8},{6... | collective-permute-start | bytes 897032 | tf_op jit(solution)/shard_map/ppermute | solution.py:40
  201.5 1.9 collective-permute-start.18
  203.4 7.6 %collective-permute-done.10.rest_1_ = bf16[1168,128]{1,0:T(8,128)(2,1)S(1)} collective-permute-done((bf16[1168,128]{1,0:T(8,128)(2,1)}, bf16[1168,128]{1,0:T(8,128)(2,1)S(1)}, u32[]{:S(2)}, u32[]{:S(2)}) %collective-permute-start.10) | collective-permute-done | bytes 299040 | tf_op jit(solution)/shard_map/ppermute | solution.py:40
  211.1 6.6 %collective-permute-start.15 = (bf16[1168,128]{1,0:T(8,128)(2,1)}, bf16[1168,128]{1,0:T(8,128)(2,1)S(1)}, u32[]{:S(2)}, u32[]{:S(2)}) collective-permute-start(bf16[1168,128]{1,0:T(8,128)(2,1)} %get-tuple-element.103), channel_id=1, source_target_pairs={{0,168},{8,176},{16,184},{24,160},{32,200},{40,208},{48,216},{56,1... | collective-permute-start | bytes 897032 | tf_op jit(solution)/shard_map/ppermute | solution.py:40
  217.7 10.7 %shifted_pairs.3 = (bf16[3,256,128]{2,1,0:T(8,128)(2,1)}, bf16[3,256,128]{2,1,0:T(8,128)(2,1)}, bf16[3,256,128]{2,1,0:T(8,128)(2,1)}, bf16[3,256,128]{2,1,0:T(8,...) custom-call(bf16[32,384,128]{2,1,0:T(8,128)(2,1)} %get-tuple-element, ...), custom_call_target="tpu_custom_call", output_to_operand_aliasing={{8}: (1, {}), {9}: (2, {}), {10}: (3, {})} | custom-call | flops 1006632960 | bytes 12320768 | tf_op jit(solution)/shard_map/shifted_pairs/pallas_call | solution.py:360
  228.4 5.7 %collective-permute-start.16 = (bf16[1168,128]{1,0:T(8,128)(2,1)}, bf16[1168,128]{1,0:T(8,128)(2,1)S(1)}, u32[]{:S(2)}, u32[]{:S(2)}) collective-permute-start(bf16[1168,128]{1,0:T(8,128)(2,1)} %get-tuple-element.105), channel_id=1, source_target_pairs={{0,56},{8,32},{16,40},{24,48},{32,88},{40,64},{48,72},{56,80},{64,... | collective-permute-start | bytes 897032 | tf_op jit(solution)/shard_map/ppermute | solution.py:40
  234.1 5.7 %collective-permute-done.14.rest_5_ = bf16[1168,128]{1,0:T(8,128)(2,1)S(1)} collective-permute-done((bf16[1168,128]{1,0:T(8,128)(2,1)}, bf16[1168,128]{1,0:T(8,128)(2,1)S(1)}, u32[]{:S(2)}, u32[]{:S(2)}) %collective-permute-start.14) | collective-permute-done | bytes 299040 | tf_op jit(solution)/shard_map/ppermute | solution.py:40
  239.8 1.9 collective-permute-start.19
  241.7 3.2 collective-permute-start.20
  244.9 9.4 %shifted_pairs.4 = (bf16[3,256,128]{2,1,0:T(8,128)(2,1)}, bf16[3,256,128]{2,1,0:T(8,128)(2,1)}, bf16[3,256,128]{2,1,0:T(8,128)(2,1)}, bf16[3,256,128]{2,1,0:T(8,...) custom-call(bf16[32,384,128]{2,1,0:T(8,128)(2,1)} %get-tuple-element, ...), custom_call_target="tpu_custom_call", output_to_operand_aliasing={{6}: (1, {}), {7}: (2, {})} | custom-call | flops 754974720 | bytes 11337728 | tf_op jit(solution)/shard_map/shifted_pairs/pallas_call | solution.py:360
  254.3 7.9 %all-to-all-start.1 = ((bf16[48,256,128]{2,1,0:T(8,128)(2,1)}), bf16[48,256,128]{2,1,0:T(8,128)(2,1)}, u32[]{:S(2)}, u32[]{:S(2)}) async-start(bf16[48,256,128]{2,1,0:T(8,128)(2,1)} %get-tuple-element.108), calls=%async_computation.1 | async-start | bytes 6291456 | tf_op jit(solution)/shard_map/all_to_all | solution.py:56
  262.2 0.8 collective-permute-start.21
  263.0 1.3 collective-permute-start.22
  264.3 4.1 %collective-permute-start.23 = (bf16[3,256,128]{2,1,0:T(8,128)(2,1)}, bf16[3,256,128]{2,1,0:T(8,128)(2,1)}, u32[]{:S(2)}, u32[]{:S(2)}) collective-permute-start(bf16[3,256,128]{2,1,0:T(8,128)(2,1)} %get-tuple-element.123), channel_id=1, source_target_pairs={{0,184},{8,160},{16,168},{24,176},{32,216},{40,192},{48,200},{56,2... | collective-permute-start | bytes 589832 | tf_op jit(solution)/shard_map/ppermute | solution.py:40
  268.4 1.9 collective-permute-start.24
  270.2 6.5 %shifted_pairs.5 = (bf16[3,256,128]{2,1,0:T(8,128)(2,1)}, bf16[3,256,128]{2,1,0:T(8,128)(2,1)}, f32[32,256,128]{2,1,0:T(8,128)}) custom-call(bf16[32,384,128]{2,1,0:T(8,128)(2,1)} %get-tuple-element.71.own_ref, f32[32,256,128]{2,1,0:T(8,128)} %get-tuple-element.104.given_ref, bf16[1168,128]{1,0:T(8,128)(2,1)} %copy-done.26, ...), custom_call_target="tpu_custom_call", output_to_operand_aliasing={{2}: (1, {})} | custom-call | flops 999999995904 | tf_op jit(solution)/shard_map/shifted_pairs/pallas_call | solution.py:360
  276.7 56.2 %all-to-all-done.1.back_ref = bf16[48,256,128]{2,1,0:T(8,128)(2,1)} async-done(((bf16[48,256,128]{2,1,0:T(8,128)(2,1)}), bf16[48,256,128]{2,1,0:T(8,128)(2,1)}, u32[]{:S(2)}, u32[]{:S(2)}) %all-to-all-start.1) | async-done | bytes 3145760 | tf_op jit(solution)/shard_map/all_to_all | solution.py:56
  332.9 6.6 %gather_team.1 = (f32[32,256,128]{2,1,0:T(8,128)}, bf16[3,256,128]{2,1,0:T(8,128)(2,1)}, bf16[3,256,128]{2,1,0:T(8,128)(2,1)}, bf16[3,256,128]{2,1,0:T(8,128)(2,...) custom-call(s32[96]{0:T(128)} %get-tuple-element.70.used_ref, ...), custom_call_target="tpu_custom_call", output_to_operand_aliasing={{0}: (3, {}), {1}: (6, {}), {2}: (7, {}), {3}: (8, {}), {4}... | custom-call | flops 1572864 | bytes 11534336 | tf_op jit(solution)/shard_map/gather_team/pallas_call | solution.py:409
  339.6 6.4 %collective-permute-start.25 = (bf16[3,256,128]{2,1,0:T(8,128)(2,1)S(1)}, bf16[3,256,128]{2,1,0:T(8,128)(2,1)S(1)}, u32[]{:S(2)}, u32[]{:S(2)}) collective-permute-start(bf16[3,256,128]{2,1,0:T(8,128)(2,1)S(1)} %copy-done.29), channel_id=1, source_target_pairs={{0,248},{8,224},{16,232},{24,240},{32,24},{40,0},{48,8},{56,16},{6... | collective-permute-start | bytes 589832 | tf_op jit(solution)/shard_map/ppermute | solution.py:40
  346.2 9.9 %collective-permute-start.27 = (bf16[3,256,128]{2,1,0:T(8,128)(2,1)}, bf16[3,256,128]{2,1,0:T(8,128)(2,1)S(1)}, u32[]{:S(2)}, u32[]{:S(2)}) collective-permute-start(bf16[3,256,128]{2,1,0:T(8,128)(2,1)} %get-tuple-element.127), channel_id=1, source_target_pairs={{0,176},{8,184},{16,160},{24,168},{32,208},{40,216},{48,192},{56,2... | collective-permute-start | bytes 589832 | tf_op jit(solution)/shard_map/ppermute | solution.py:40
  356.2 4.4 %collective-permute-start.30 = (bf16[3,256,128]{2,1,0:T(8,128)(2,1)}, bf16[3,256,128]{2,1,0:T(8,128)(2,1)S(1)}, u32[]{:S(2)}, u32[]{:S(2)}) collective-permute-start(bf16[3,256,128]{2,1,0:T(8,128)(2,1)} %get-tuple-element.130), channel_id=1, source_target_pairs={{0,48},{8,56},{16,32},{24,40},{32,80},{40,88},{48,64},{56,72},{64,... | collective-permute-start | bytes 589832 | tf_op jit(solution)/shard_map/ppermute | solution.py:40
  360.6 3.8 collective-permute-start.31
  364.4 3.8 collective-permute-done.27.rest_8_
  368.2 2.5 collective-permute-start.32
  370.7 4.2 %collective-permute-done.28.rest_9_ = bf16[3,256,128]{2,1,0:T(8,128)(2,1)S(1)} collective-permute-done((bf16[3,256,128]{2,1,0:T(8,128)(2,1)}, bf16[3,256,128]{2,1,0:T(8,128)(2,1)S(1)}, u32[]{:S(2)}, u32[]{:S(2)}) %collective-permute-start.28) | collective-permute-done | bytes 196640 | tf_op jit(solution)/shard_map/ppermute | solution.py:40
  375.0 3.0 collective-permute-start.33
  378.0 5.4 %collective-permute-done.31.rest_12_ = bf16[3,256,128]{2,1,0:T(8,128)(2,1)S(1)} collective-permute-done((bf16[3,256,128]{2,1,0:T(8,128)(2,1)}, bf16[3,256,128]{2,1,0:T(8,128)(2,1)S(1)}, u32[]{:S(2)}, u32[]{:S(2)}) %collective-permute-start.31) | collective-permute-done | bytes 196640 | tf_op jit(solution)/shard_map/ppermute | solution.py:40
  383.4 6.5 %collective-permute-done.32.rest_13_ = bf16[3,256,128]{2,1,0:T(8,128)(2,1)S(1)} collective-permute-done((bf16[3,256,128]{2,1,0:T(8,128)(2,1)}, bf16[3,256,128]{2,1,0:T(8,128)(2,1)S(1)}, u32[]{:S(2)}, u32[]{:S(2)}) %collective-permute-start.32) | collective-permute-done | bytes 196640 | tf_op jit(solution)/shard_map/ppermute | solution.py:40
  390.7 12.1 %gather_and_mix.1 = bf16[8192,128]{1,0:T(8,128)(2,1)} custom-call(s32[96]{0:T(128)} %get-tuple-element.70.used_ref, s32[16]{0:T(128)} %stack.70.dests_ref, f32[32,256,128]{2,1,0:T(8,128)} %get-tuple-element.118.total_ref, bf16[8192,128]{1,0:T(8,128)(2,1)} %bitcast.28, bf16[128,128]{1,0:T(8,128)(2,1)} %w_ref.1, f32[1,128]{1,0:T(1,128)} %bitcast.36, ...), custom_call_target="tpu_custom_call" | custom-call | tf_op jit(solution)/shard_map/gather_and_mix/pallas_call | solution.py:453
  (101 shorter events, 3.5 us)
Async XLA Ops:
  13.9 24.0 %collective-permute-start.1 = (bf16[8,384,128]{2,1,0:T(8,128)(2,1)}, bf16[8,384,128]{2,1,0:T(8,128)(2,1)S(1)}, u32[]{:S(2)}, u32[]{:S(2)}) collective-permute-start(bf16[8,384,128]{2,1,0:T(8,128)(2,1)} %get-tuple-element.73), channel_id=1, source_target_pairs={{0,1},{1,2},{2,3},{3,4},{4,5},{5,6},{6,7},{8,9},{9,10},{10,11},{11... | collective-permute-start | bytes 2359304 | tf_op jit(solution)/shard_map/ppermute | solution.py:64
  15.8 21.1 %collective-permute-start = (s32[8,2]{0,1:T(2,128)S(1)}, s32[8,2]{0,1:T(2,128)S(1)}, u32[]{:S(2)}, u32[]{:S(2)}) collective-permute-start(s32[8,2]{0,1:T(2,128)S(1)} %pad_add_fusion), channel_id=1, source_target_pairs={{0,1},{1,2},{2,3},{3,4},{4,5},{5,6},{6,7},{8,9},{9,10},{10,11},{11... | collective-permute-start | bytes 200 | tf_op jit(solution)/shard_map/ppermute | solution.py:64
  19.3 121.6 %all-to-all-start = ((bf16[16,1168,128]{2,1,0:T(8,128)(2,1)}), bf16[16,1168,128]{2,1,0:T(8,128)(2,1)}, u32[]{:S(2)}, u32[]{:S(2)}) async-start(bf16[16,1168,128]{2,1,0:T(8,128)(2,1)} %get-tuple-element.72), calls=%async_computation | async-start | bytes 9568256 | tf_op jit(solution)/shard_map/all_to_all | solution.py:56
  30.0 127.7 %collective-permute-start.2 = (bf16[1168,128]{1,0:T(8,128)(2,1)}, bf16[1168,128]{1,0:T(8,128)(2,1)}, u32[]{:S(2)}, u32[]{:S(2)}) collective-permute-start(bf16[1168,128]{1,0:T(8,128)(2,1)} %get-tuple-element.88), channel_id=1, source_target_pairs={{0,96},{8,104},{16,112},{24,120},{32,128},{40,136},{48,144},{56,15... | collective-permute-start | bytes 897032 | tf_op jit(solution)/shard_map/ppermute | solution.py:40
  34.9 127.5 %collective-permute-start.3 = (bf16[1168,128]{1,0:T(8,128)(2,1)}, bf16[1168,128]{1,0:T(8,128)(2,1)}, u32[]{:S(2)}, u32[]{:S(2)}) collective-permute-start(bf16[1168,128]{1,0:T(8,128)(2,1)} %get-tuple-element.89), channel_id=1, source_target_pairs={{0,160},{8,168},{16,176},{24,184},{32,192},{40,200},{48,208},{56,2... | collective-permute-start | bytes 897032 | tf_op jit(solution)/shard_map/ppermute | solution.py:40
  35.0 135.6 %collective-permute-start.4 = (bf16[1168,128]{1,0:T(8,128)(2,1)}, bf16[1168,128]{1,0:T(8,128)(2,1)}, u32[]{:S(2)}, u32[]{:S(2)}) collective-permute-start(bf16[1168,128]{1,0:T(8,128)(2,1)} %get-tuple-element.90), channel_id=1, source_target_pairs={{0,32},{8,40},{16,48},{24,56},{32,64},{40,72},{48,80},{56,88},{64,... | collective-permute-start | bytes 897032 | tf_op jit(solution)/shard_map/ppermute | solution.py:40
  36.9 133.7 %collective-permute-start.5 = (bf16[1168,128]{1,0:T(8,128)(2,1)}, bf16[1168,128]{1,0:T(8,128)(2,1)}, u32[]{:S(2)}, u32[]{:S(2)}) collective-permute-start(bf16[1168,128]{1,0:T(8,128)(2,1)} %get-tuple-element.91), channel_id=1, source_target_pairs={{0,224},{8,232},{16,240},{24,248},{32,0},{40,8},{48,16},{56,24},{6... | collective-permute-start | bytes 897032 | tf_op jit(solution)/shard_map/ppermute | solution.py:40
  140.9 60.6 %copy-start.25 = (bf16[8,256,128]{2,1,0:T(8,128)(2,1)S(1)}, bf16[8,256,128]{2,1,0:T(8,128)(2,1)}, u32[]{:S(2)}) copy-start(bf16[8,256,128]{2,1,0:T(8,128)(2,1)} %get-tuple-element.109) | copy-start | bytes 1572868
  156.4 25.4 %collective-permute-start.6 = (bf16[1168,128]{1,0:T(8,128)(2,1)}, bf16[1168,128]{1,0:T(8,128)(2,1)S(1)}, u32[]{:S(2)}, u32[]{:S(2)}) collective-permute-start(bf16[1168,128]{1,0:T(8,128)(2,1)} %get-tuple-element.92), channel_id=1, source_target_pairs={{0,104},{8,112},{16,120},{24,96},{32,136},{40,144},{48,152},{56,12... | collective-permute-start | bytes 897032 | tf_op jit(solution)/shard_map/ppermute | solution.py:40
  157.7 30.1 %collective-permute-start.7 = (bf16[1168,128]{1,0:T(8,128)(2,1)}, bf16[1168,128]{1,0:T(8,128)(2,1)S(1)}, u32[]{:S(2)}, u32[]{:S(2)}) collective-permute-start(bf16[1168,128]{1,0:T(8,128)(2,1)} %get-tuple-element.93), channel_id=1, source_target_pairs={{0,184},{8,160},{16,168},{24,176},{32,216},{40,192},{48,200},{56,2... | collective-permute-start | bytes 897032 | tf_op jit(solution)/shard_map/ppermute | solution.py:40
  162.5 26.2 %collective-permute-start.8 = (bf16[1168,128]{1,0:T(8,128)(2,1)}, bf16[1168,128]{1,0:T(8,128)(2,1)S(1)}, u32[]{:S(2)}, u32[]{:S(2)}) collective-permute-start(bf16[1168,128]{1,0:T(8,128)(2,1)} %get-tuple-element.94), channel_id=1, source_target_pairs={{0,40},{8,48},{16,56},{24,32},{32,72},{40,80},{48,88},{56,64},{64,... | collective-permute-start | bytes 897032 | tf_op jit(solution)/shard_map/ppermute | solution.py:40
  170.6 30.9 %collective-permute-start.9 = (bf16[1168,128]{1,0:T(8,128)(2,1)}, bf16[1168,128]{1,0:T(8,128)(2,1)S(1)}, u32[]{:S(2)}, u32[]{:S(2)}) collective-permute-start(bf16[1168,128]{1,0:T(8,128)(2,1)} %get-tuple-element.95), channel_id=1, source_target_pairs={{0,248},{8,224},{16,232},{24,240},{32,24},{40,0},{48,8},{56,16},{6... | collective-permute-start | bytes 897032 | tf_op jit(solution)/shard_map/ppermute | solution.py:40
  170.6 40.4 %collective-permute-start.10 = (bf16[1168,128]{1,0:T(8,128)(2,1)}, bf16[1168,128]{1,0:T(8,128)(2,1)S(1)}, u32[]{:S(2)}, u32[]{:S(2)}) collective-permute-start(bf16[1168,128]{1,0:T(8,128)(2,1)} %get-tuple-element.98), channel_id=1, source_target_pairs={{0,112},{8,120},{16,96},{24,104},{32,144},{40,152},{48,128},{56,13... | collective-permute-start | bytes 897032 | tf_op jit(solution)/shard_map/ppermute | solution.py:40
  181.9 35.8 %copy-start.4 = (bf16[1168,128]{1,0:T(8,128)(2,1)}, bf16[1168,128]{1,0:T(8,128)(2,1)S(1)}, u32[]{:S(2)}) copy-start(bf16[1168,128]{1,0:T(8,128)(2,1)S(1)} %collective-permute-done.6.rest_6_) | copy-start | bytes 897028
  181.9 29.2 %collective-permute-start.11 = (bf16[1168,128]{1,0:T(8,128)(2,1)}, bf16[1168,128]{1,0:T(8,128)(2,1)S(1)}, u32[]{:S(2)}, u32[]{:S(2)}) collective-permute-start(bf16[1168,128]{1,0:T(8,128)(2,1)} %get-tuple-element.99), channel_id=1, source_target_pairs={{0,176},{8,184},{16,160},{24,168},{32,208},{40,216},{48,192},{56,2... | collective-permute-start | bytes 897032 | tf_op jit(solution)/shard_map/ppermute | solution.py:40
  187.8 29.9 %copy-start.6 = (bf16[1168,128]{1,0:T(8,128)(2,1)}, bf16[1168,128]{1,0:T(8,128)(2,1)S(1)}, u32[]{:S(2)}) copy-start(bf16[1168,128]{1,0:T(8,128)(2,1)S(1)} %collective-permute-done.7.rest_7_) | copy-start | bytes 897028
  187.8 40.6 %collective-permute-start.12 = (bf16[1168,128]{1,0:T(8,128)(2,1)}, bf16[1168,128]{1,0:T(8,128)(2,1)S(1)}, u32[]{:S(2)}, u32[]{:S(2)}) collective-permute-start(bf16[1168,128]{1,0:T(8,128)(2,1)} %get-tuple-element.100), channel_id=1, source_target_pairs={{0,48},{8,56},{16,32},{24,40},{32,80},{40,88},{48,64},{56,72},{64,... | collective-permute-start | bytes 897032 | tf_op jit(solution)/shard_map/ppermute | solution.py:40
  188.6 29.0 %copy-start.7 = (bf16[1168,128]{1,0:T(8,128)(2,1)}, bf16[1168,128]{1,0:T(8,128)(2,1)S(1)}, u32[]{:S(2)}) copy-start(bf16[1168,128]{1,0:T(8,128)(2,1)S(1)} %collective-permute-done.8.rest_8_) | copy-start | bytes 897028
  188.7 45.4 %collective-permute-start.13 = (bf16[1168,128]{1,0:T(8,128)(2,1)}, bf16[1168,128]{1,0:T(8,128)(2,1)S(1)}, u32[]{:S(2)}, u32[]{:S(2)}) collective-permute-start(bf16[1168,128]{1,0:T(8,128)(2,1)} %get-tuple-element.101), channel_id=1, source_target_pairs={{0,240},{8,248},{16,224},{24,232},{32,16},{40,24},{48,0},{56,8},{6... | collective-permute-start | bytes 897032 | tf_op jit(solution)/shard_map/ppermute | solution.py:40
  201.5 16.2 %copy-start.8 = (bf16[1168,128]{1,0:T(8,128)(2,1)}, bf16[1168,128]{1,0:T(8,128)(2,1)S(1)}, u32[]{:S(2)}) copy-start(bf16[1168,128]{1,0:T(8,128)(2,1)S(1)} %collective-permute-done.9.rest_9_) | copy-start | bytes 897028
  201.5 60.7 %collective-permute-start.18 = (bf16[8,256,128]{2,1,0:T(8,128)(2,1)S(1)}, bf16[8,256,128]{2,1,0:T(8,128)(2,1)S(1)}, u32[]{:S(2)}, u32[]{:S(2)}) collective-permute-start(bf16[8,256,128]{2,1,0:T(8,128)(2,1)S(1)} %copy-done.25), channel_id=1, source_target_pairs={{1,0},{2,1},{3,2},{4,3},{5,4},{6,5},{7,6},{9,8},{10,9},{11,10},{12... | collective-permute-start | bytes 1572872 | tf_op jit(solution)/shard_map/ppermute | solution.py:64
  211.0 17.4 %copy-start.1 = (bf16[1168,128]{1,0:T(8,128)(2,1)}, bf16[1168,128]{1,0:T(8,128)(2,1)S(1)}, u32[]{:S(2)}) copy-start(bf16[1168,128]{1,0:T(8,128)(2,1)S(1)} %collective-permute-done.10.rest_1_) | copy-start | bytes 897028
  211.0 28.8 %collective-permute-start.14 = (bf16[1168,128]{1,0:T(8,128)(2,1)}, bf16[1168,128]{1,0:T(8,128)(2,1)S(1)}, u32[]{:S(2)}, u32[]{:S(2)}) collective-permute-start(bf16[1168,128]{1,0:T(8,128)(2,1)} %get-tuple-element.102), channel_id=1, source_target_pairs={{0,120},{8,96},{16,104},{24,112},{32,152},{40,128},{48,136},{56,14... | collective-permute-start | bytes 897032 | tf_op jit(solution)/shard_map/ppermute | solution.py:40
  211.1 17.3 %copy-start.2 = (bf16[1168,128]{1,0:T(8,128)(2,1)}, bf16[1168,128]{1,0:T(8,128)(2,1)S(1)}, u32[]{:S(2)}) copy-start(bf16[1168,128]{1,0:T(8,128)(2,1)S(1)} %collective-permute-done.11.rest_2_) | copy-start | bytes 897028
  211.1 30.6 %collective-permute-start.15 = (bf16[1168,128]{1,0:T(8,128)(2,1)}, bf16[1168,128]{1,0:T(8,128)(2,1)S(1)}, u32[]{:S(2)}, u32[]{:S(2)}) collective-permute-start(bf16[1168,128]{1,0:T(8,128)(2,1)} %get-tuple-element.103), channel_id=1, source_target_pairs={{0,168},{8,176},{16,184},{24,160},{32,200},{40,208},{48,216},{56,1... | collective-permute-start | bytes 897032 | tf_op jit(solution)/shard_map/ppermute | solution.py:40
  228.4 16.4 %copy-start.3 = (bf16[1168,128]{1,0:T(8,128)(2,1)}, bf16[1168,128]{1,0:T(8,128)(2,1)S(1)}, u32[]{:S(2)}) copy-start(bf16[1168,128]{1,0:T(8,128)(2,1)S(1)} %collective-permute-done.12.rest_3_) | copy-start | bytes 897028
  228.4 35.9 %collective-permute-start.16 = (bf16[1168,128]{1,0:T(8,128)(2,1)}, bf16[1168,128]{1,0:T(8,128)(2,1)S(1)}, u32[]{:S(2)}, u32[]{:S(2)}) collective-permute-start(bf16[1168,128]{1,0:T(8,128)(2,1)} %get-tuple-element.105), channel_id=1, source_target_pairs={{0,56},{8,32},{16,40},{24,48},{32,88},{40,64},{48,72},{56,80},{64,... | collective-permute-start | bytes 897032 | tf_op jit(solution)/shard_map/ppermute | solution.py:40
  234.1 34.3 %collective-permute-start.17 = (bf16[1168,128]{1,0:T(8,128)(2,1)}, bf16[1168,128]{1,0:T(8,128)(2,1)S(1)}, u32[]{:S(2)}, u32[]{:S(2)}) collective-permute-start(bf16[1168,128]{1,0:T(8,128)(2,1)} %get-tuple-element.106), channel_id=1, source_target_pairs={{0,232},{8,240},{16,248},{24,224},{32,8},{40,16},{48,24},{56,0},{6... | collective-permute-start | bytes 897032 | tf_op jit(solution)/shard_map/ppermute | solution.py:40
  239.8 23.2 %collective-permute-start.19 = (bf16[3,256,128]{2,1,0:T(8,128)(2,1)}, bf16[3,256,128]{2,1,0:T(8,128)(2,1)S(1)}, u32[]{:S(2)}, u32[]{:S(2)}) collective-permute-start(bf16[3,256,128]{2,1,0:T(8,128)(2,1)} %get-tuple-element.119), channel_id=1, source_target_pairs={{0,160},{8,168},{16,176},{24,184},{32,192},{40,200},{48,208},{56,2... | collective-permute-start | bytes 589832 | tf_op jit(solution)/shard_map/ppermute | solution.py:40
  241.7 97.9 %collective-permute-start.20 = (bf16[3,256,128]{2,1,0:T(8,128)(2,1)}, bf16[3,256,128]{2,1,0:T(8,128)(2,1)}, u32[]{:S(2)}, u32[]{:S(2)}) collective-permute-start(bf16[3,256,128]{2,1,0:T(8,128)(2,1)} %get-tuple-element.120), channel_id=1, source_target_pairs={{0,96},{8,104},{16,112},{24,120},{32,128},{40,136},{48,144},{56,15... | collective-permute-start | bytes 589832 | tf_op jit(solution)/shard_map/ppermute | solution.py:40
  254.3 78.6 %all-to-all-start.1 = ((bf16[48,256,128]{2,1,0:T(8,128)(2,1)}), bf16[48,256,128]{2,1,0:T(8,128)(2,1)}, u32[]{:S(2)}, u32[]{:S(2)}) async-start(bf16[48,256,128]{2,1,0:T(8,128)(2,1)} %get-tuple-element.108), calls=%async_computation.1 | async-start | bytes 6291456 | tf_op jit(solution)/shard_map/all_to_all | solution.py:56
  262.2 83.7 %collective-permute-start.21 = (bf16[3,256,128]{2,1,0:T(8,128)(2,1)}, bf16[3,256,128]{2,1,0:T(8,128)(2,1)}, u32[]{:S(2)}, u32[]{:S(2)}) collective-permute-start(bf16[3,256,128]{2,1,0:T(8,128)(2,1)} %get-tuple-element.121), channel_id=1, source_target_pairs={{0,224},{8,232},{16,240},{24,248},{32,0},{40,8},{48,16},{56,24},{6... | collective-permute-start | bytes 589832 | tf_op jit(solution)/shard_map/ppermute | solution.py:40
  263.0 83.2 %collective-permute-start.22 = (bf16[3,256,128]{2,1,0:T(8,128)(2,1)}, bf16[3,256,128]{2,1,0:T(8,128)(2,1)}, u32[]{:S(2)}, u32[]{:S(2)}) collective-permute-start(bf16[3,256,128]{2,1,0:T(8,128)(2,1)} %get-tuple-element.122), channel_id=1, source_target_pairs={{0,32},{8,40},{16,48},{24,56},{32,64},{40,72},{48,80},{56,88},{64,... | collective-permute-start | bytes 589832 | tf_op jit(solution)/shard_map/ppermute | solution.py:40
  264.3 91.8 %collective-permute-start.23 = (bf16[3,256,128]{2,1,0:T(8,128)(2,1)}, bf16[3,256,128]{2,1,0:T(8,128)(2,1)}, u32[]{:S(2)}, u32[]{:S(2)}) collective-permute-start(bf16[3,256,128]{2,1,0:T(8,128)(2,1)} %get-tuple-element.123), channel_id=1, source_target_pairs={{0,184},{8,160},{16,168},{24,176},{32,216},{40,192},{48,200},{56,2... | collective-permute-start | bytes 589832 | tf_op jit(solution)/shard_map/ppermute | solution.py:40
  268.4 87.7 %collective-permute-start.24 = (bf16[3,256,128]{2,1,0:T(8,128)(2,1)}, bf16[3,256,128]{2,1,0:T(8,128)(2,1)}, u32[]{:S(2)}, u32[]{:S(2)}) collective-permute-start(bf16[3,256,128]{2,1,0:T(8,128)(2,1)} %get-tuple-element.124), channel_id=1, source_target_pairs={{0,104},{8,112},{16,120},{24,96},{32,136},{40,144},{48,152},{56,12... | collective-permute-start | bytes 589832 | tf_op jit(solution)/shard_map/ppermute | solution.py:40
  339.6 16.6 %collective-permute-start.25 = (bf16[3,256,128]{2,1,0:T(8,128)(2,1)S(1)}, bf16[3,256,128]{2,1,0:T(8,128)(2,1)S(1)}, u32[]{:S(2)}, u32[]{:S(2)}) collective-permute-start(bf16[3,256,128]{2,1,0:T(8,128)(2,1)S(1)} %copy-done.29), channel_id=1, source_target_pairs={{0,248},{8,224},{16,232},{24,240},{32,24},{40,0},{48,8},{56,16},{6... | collective-permute-start | bytes 589832 | tf_op jit(solution)/shard_map/ppermute | solution.py:40
  345.9 14.7 %collective-permute-start.26 = (bf16[3,256,128]{2,1,0:T(8,128)(2,1)S(1)}, bf16[3,256,128]{2,1,0:T(8,128)(2,1)S(1)}, u32[]{:S(2)}, u32[]{:S(2)}) collective-permute-start(bf16[3,256,128]{2,1,0:T(8,128)(2,1)S(1)} %copy-done.28), channel_id=1, source_target_pairs={{0,40},{8,48},{16,56},{24,32},{32,72},{40,80},{48,88},{56,64},{64,... | collective-permute-start | bytes 589832 | tf_op jit(solution)/shard_map/ppermute | solution.py:40
  346.2 22.0 %collective-permute-start.27 = (bf16[3,256,128]{2,1,0:T(8,128)(2,1)}, bf16[3,256,128]{2,1,0:T(8,128)(2,1)S(1)}, u32[]{:S(2)}, u32[]{:S(2)}) collective-permute-start(bf16[3,256,128]{2,1,0:T(8,128)(2,1)} %get-tuple-element.127), channel_id=1, source_target_pairs={{0,176},{8,184},{16,160},{24,168},{32,208},{40,216},{48,192},{56,2... | collective-permute-start | bytes 589832 | tf_op jit(solution)/shard_map/ppermute | solution.py:40
  356.1 18.9 %collective-permute-start.28 = (bf16[3,256,128]{2,1,0:T(8,128)(2,1)}, bf16[3,256,128]{2,1,0:T(8,128)(2,1)S(1)}, u32[]{:S(2)}, u32[]{:S(2)}) collective-permute-start(bf16[3,256,128]{2,1,0:T(8,128)(2,1)} %get-tuple-element.128), channel_id=1, source_target_pairs={{0,112},{8,120},{16,96},{24,104},{32,144},{40,152},{48,128},{56,13... | collective-permute-start | bytes 589832 | tf_op jit(solution)/shard_map/ppermute | solution.py:40
  356.1 21.9 %collective-permute-start.29 = (bf16[3,256,128]{2,1,0:T(8,128)(2,1)}, bf16[3,256,128]{2,1,0:T(8,128)(2,1)S(1)}, u32[]{:S(2)}, u32[]{:S(2)}) collective-permute-start(bf16[3,256,128]{2,1,0:T(8,128)(2,1)} %get-tuple-element.129), channel_id=1, source_target_pairs={{0,240},{8,248},{16,224},{24,232},{32,16},{40,24},{48,0},{56,8},{6... | collective-permute-start | bytes 589832 | tf_op jit(solution)/shard_map/ppermute | solution.py:40
  356.2 33.8 %copy-start.12 = (bf16[3,256,128]{2,1,0:T(8,128)(2,1)}, bf16[3,256,128]{2,1,0:T(8,128)(2,1)S(1)}, u32[]{:S(2)}) copy-start(bf16[3,256,128]{2,1,0:T(8,128)(2,1)S(1)} %collective-permute-done.25.rest_6_) | copy-start | bytes 589828
  356.2 21.8 %collective-permute-start.30 = (bf16[3,256,128]{2,1,0:T(8,128)(2,1)}, bf16[3,256,128]{2,1,0:T(8,128)(2,1)S(1)}, u32[]{:S(2)}, u32[]{:S(2)}) collective-permute-start(bf16[3,256,128]{2,1,0:T(8,128)(2,1)} %get-tuple-element.130), channel_id=1, source_target_pairs={{0,48},{8,56},{16,32},{24,40},{32,80},{40,88},{48,64},{56,72},{64,... | collective-permute-start | bytes 589832 | tf_op jit(solution)/shard_map/ppermute | solution.py:40
  360.6 29.4 %copy-start.13 = (bf16[3,256,128]{2,1,0:T(8,128)(2,1)}, bf16[3,256,128]{2,1,0:T(8,128)(2,1)S(1)}, u32[]{:S(2)}) copy-start(bf16[3,256,128]{2,1,0:T(8,128)(2,1)S(1)} %collective-permute-done.26.rest_7_) | copy-start | bytes 589828
  360.6 22.8 %collective-permute-start.31 = (bf16[3,256,128]{2,1,0:T(8,128)(2,1)}, bf16[3,256,128]{2,1,0:T(8,128)(2,1)S(1)}, u32[]{:S(2)}, u32[]{:S(2)}) collective-permute-start(bf16[3,256,128]{2,1,0:T(8,128)(2,1)} %get-tuple-element.131), channel_id=1, source_target_pairs={{0,168},{8,176},{16,184},{24,160},{32,200},{40,208},{48,216},{56,1... | collective-permute-start | bytes 589832 | tf_op jit(solution)/shard_map/ppermute | solution.py:40
  368.2 21.8 %copy-start.14 = (bf16[3,256,128]{2,1,0:T(8,128)(2,1)}, bf16[3,256,128]{2,1,0:T(8,128)(2,1)S(1)}, u32[]{:S(2)}) copy-start(bf16[3,256,128]{2,1,0:T(8,128)(2,1)S(1)} %collective-permute-done.27.rest_8_) | copy-start | bytes 589828
  368.2 21.7 %collective-permute-start.32 = (bf16[3,256,128]{2,1,0:T(8,128)(2,1)}, bf16[3,256,128]{2,1,0:T(8,128)(2,1)S(1)}, u32[]{:S(2)}, u32[]{:S(2)}) collective-permute-start(bf16[3,256,128]{2,1,0:T(8,128)(2,1)} %get-tuple-element.132), channel_id=1, source_target_pairs={{0,120},{8,96},{16,104},{24,112},{32,152},{40,128},{48,136},{56,14... | collective-permute-start | bytes 589832 | tf_op jit(solution)/shard_map/ppermute | solution.py:40
  375.0 15.0 %collective-permute-start.33 = (bf16[3,256,128]{2,1,0:T(8,128)(2,1)}, bf16[3,256,128]{2,1,0:T(8,128)(2,1)S(1)}, u32[]{:S(2)}, u32[]{:S(2)}) collective-permute-start(bf16[3,256,128]{2,1,0:T(8,128)(2,1)} %get-tuple-element.133), channel_id=1, source_target_pairs={{0,232},{8,240},{16,248},{24,224},{32,8},{40,16},{48,24},{56,0},{6... | collective-permute-start | bytes 589832 | tf_op jit(solution)/shard_map/ppermute | solution.py:40
  378.0 12.0 %collective-permute-start.34 = (bf16[3,256,128]{2,1,0:T(8,128)(2,1)}, bf16[3,256,128]{2,1,0:T(8,128)(2,1)S(1)}, u32[]{:S(2)}, u32[]{:S(2)}) collective-permute-start(bf16[3,256,128]{2,1,0:T(8,128)(2,1)} %get-tuple-element.134), channel_id=1, source_target_pairs={{0,56},{8,32},{16,40},{24,48},{32,88},{40,64},{48,72},{56,80},{64,... | collective-permute-start | bytes 589832 | tf_op jit(solution)/shard_map/ppermute | solution.py:40
  (19 other events, 155.1 us)

commit v2 on v1

--- a/solution.py
+++ b/solution.py
@@ -20,8 +20,9 @@
     shift for dy in range(SPAN_Y) for shift in ((3, dy), (-3, -dy), (1, dy), (-1, -dy))
 )
 BATCHES = ((0, 8), (8, 14), (14, 16))
-GATES = (4, 14)
+GATES = (6, 14)
 GATE = 0
+FIRST = 2
 PASSED = 1
 MEMBERS = SPACES // 2
 TEAMS = [[z * SPAN_Y + y for z in range(p, SPAN_Z, 2) for y in range(SPAN_Y)] for p in range(2)]
@@ -232,12 +233,13 @@
     )
 
 
-def pairs_above(cross_meta, below, own):
+def pairs_above(cross_meta, below, own, before):
     cross = below.shape[0]
     blocks = own.shape[0]
     some = math.gcd(cross, 4)
 
-    def kernel(cross_ref, below_ref, own_ref, back_ref, total):
+    def kernel(cross_ref, below_ref, own_ref, *rest):
+        back_ref, total = rest[len(before) :]
         total[...] = jnp.zeros_like(total)
 
         @pl.loop(0, cross, step=some)
@@ -256,7 +258,7 @@
 
     return pl.pallas_call(
         kernel,
-        in_specs=[SMEM, VMEM, VMEM],
+        in_specs=[SMEM, VMEM, VMEM] + [ANYWHERE] * len(before),
         out_specs=(VMEM, VMEM),
         out_shape=(
             jax.ShapeDtypeStruct((cross, BLK, C), jnp.bfloat16),
@@ -265,7 +267,7 @@
         compiler_params=pltpu.CompilerParams(vmem_limit_bytes=VMEM_LIMIT),
         cost_estimate=pl.CostEstimate(flops=LONG, bytes_accessed=0, transcendentals=0),
         name="pairs_above",
-    )(cross_meta, below, own)
+    )(cross_meta, below, own, *before)
 
 
 def team_pairs(arrived, own, aggregate, passing):
@@ -494,9 +496,9 @@
         for k in range(first, end):
             shifted[k] = space_shift(shifting[k], SHIFTS[k])
 
-    back_x, aggregate = pairs_above(cross_meta, below, own)
+    send(0, GATES[0])
+    back_x, aggregate = pairs_above(cross_meta, below, own, shifted[:FIRST])
     returned_x = group_shift(back_x, -1)
-    send(0, GATES[0])
     first, end = GATES
     back, aggregate, shifting[first:end] = team_pairs(arrived, own, aggregate, shifting[first:end])
     send(first, end)

time: 404 us -> 404 us (level); the launches traced: 403 us -> 399 us
  waiting for transfers between devices: 194 us -> 186 us
    ppermute x32, waiting for transfers between devices: 41 us -> 34.2 us  [space_shift(): lax.ppermute(value, 'space', [(z * SPAN_Y + y, (z + shift[0]) % SPAN_Z *...]
  transfers between devices with their start and end apart: 37 -> 37, of which waited for: 10 -> 9; matrix products, arithmetic and copies ran while one was open for 0% -> 0% of each run, Pallas kernels for 14% -> 14%
where the time goes in v2:
time: 404 us; the launch traced here: 399 us
  waiting for transfers between devices  186 us (46%)
  starting transfers between devices  130 us (32%)
  Pallas kernels  77.9 us (19%)
    all_to_all x2, waiting for transfers between devices, team_exchange(): lax.all_to_all(value, 'space', split_axis=0, concat_axis=0, tiled=True, a...  151 us
    ppermute x32, starting transfers between devices, space_shift(): lax.ppermute(value, 'space', [(z * SPAN_Y + y, (z + shift[0]) % SPAN_Z *...  99.3 us
    ppermute x32, waiting for transfers between devices, space_shift(): lax.ppermute(value, 'space', [(z * SPAN_Y + y, (z + shift[0]) % SPAN_Z *...  34.2 us
    pallas_call x3, Pallas kernels, shifted_pairs(): pl.pallas_call(kernel, in_specs=[VMEM] * 2 + [ANYWHERE] * handed + [VMEM]...  26.6 us
    all_to_all x2, starting transfers between devices, team_exchange(): lax.all_to_all(value, 'space', split_axis=0, concat_axis=0, tiled=True, a...  20.4 us
    pallas_call x1, Pallas kernels, team_pairs(): pl.pallas_call(kernel, grid=(MEMBERS // CREW,), in_specs=[pl.BlockSpec((C...  15.5 us
    pallas_call x1, Pallas kernels, gather_and_mix(): pl.pallas_call(kernel, grid_spec=pltpu.PrefetchScalarGridSpec(num_scalar_...  12.1 us
    pallas_call x1, Pallas kernels, project_and_pack(): pl.pallas_call(kernel, grid_spec=pltpu.PrefetchScalarGridSpec(num_scalar_...  11.1 us
  transfers between devices with their start and end apart: 37, of which 9 were waited for; matrix products, arithmetic and copies ran while one was open for 0% of the time, Pallas kernels for 14%

profile of v2, /device:TPU:42, one launch (start us, length us, event | category | flops | bytes accessed | tf_op | source)
XLA Modules:
  0.0 398.7 jit_solution(16415144046308955747)
XLA Ops:
  0.5 0.8 copy.40
  1.3 0.7 fusion.2.wk_ref
  2.0 0.7 stack.70.dests_ref
  2.7 11.1 %project_and_pack.1 = (s32[96]{0:T(128)}, bf16[32,384,128]{2,1,0:T(8,128)(2,1)}, bf16[8,384,128]{2,1,0:T(8,128)(2,1)}, bf16[16,1168,128]{2,1,0:T(8,128)(2,1)}, b...) custom-call(s32[64]{0:T(128)} %bitcast.32, ...), custom_call_target="tpu_custom_call" | custom-call | tf_op jit(solution)/shard_map/project_and_pack/pallas_call | solution.py:156
  13.9 1.9 collective-permute-start.1
  15.8 5.9 %collective-permute-start.2 = (bf16[1168,128]{1,0:T(8,128)(2,1)}, bf16[1168,128]{1,0:T(8,128)(2,1)S(1)}, u32[]{:S(2)}, u32[]{:S(2)}) collective-permute-start(bf16[1168,128]{1,0:T(8,128)(2,1)} %get-tuple-element.72), channel_id=1, source_target_pairs={{0,96},{8,104},{16,112},{24,120},{32,128},{40,136},{48,144},{56,15... | collective-permute-start | bytes 897032 | tf_op jit(solution)/shard_map/ppermute | solution.py:41
  21.8 3.2 collective-permute-start
  25.0 9.5 %all-to-all-start = ((bf16[16,1168,128]{2,1,0:T(8,128)(2,1)}), bf16[16,1168,128]{2,1,0:T(8,128)(2,1)}, u32[]{:S(2)}, u32[]{:S(2)}) async-start(bf16[16,1168,128]{2,1,0:T(8,128)(2,1)} %get-tuple-element.70), calls=%async_computation | async-start | bytes 9568256 | tf_op jit(solution)/shard_map/all_to_all | solution.py:57
  34.5 1.9 collective-permute-start.4
  37.3 5.4 %collective-permute-done.2.rest_0_.rest_2_ = bf16[1168,128]{1,0:T(8,128)(2,1)S(1)} collective-permute-done((bf16[1168,128]{1,0:T(8,128)(2,1)}, bf16[1168,128]{1,0:T(8,128)(2,1)S(1)}, u32[]{:S(2)}, u32[]{:S(2)}) %collective-permute-start.2) | collective-permute-done | bytes 299040 | tf_op jit(solution)/shard_map/ppermute | solution.py:41
  42.7 5.4 %collective-permute-start.6 = (bf16[1168,128]{1,0:T(8,128)(2,1)}, bf16[1168,128]{1,0:T(8,128)(2,1)}, u32[]{:S(2)}, u32[]{:S(2)}) collective-permute-start(bf16[1168,128]{1,0:T(8,128)(2,1)} %get-tuple-element.88), channel_id=1, source_target_pairs={{0,104},{8,112},{16,120},{24,96},{32,136},{40,144},{48,152},{56,12... | collective-permute-start | bytes 897032 | tf_op jit(solution)/shard_map/ppermute | solution.py:41
  48.9 0.7 copy-done.24
  49.5 5.9 %pairs_above.1 = (bf16[8,256,128]{2,1,0:T(8,128)(2,1)}, f32[32,256,128]{2,1,0:T(8,128)}) custom-call(s32[16]{0:T(128)} %reshape.3.cross_ref, bf16[8,384,128]{2,1,0:T(8,128)(2,1)} %copy-done.24, bf16[32,384,128]{2,1,0:T(8,128)(2,1)} %get-tuple-element.69.own_ref, bf16[1168,128]{1,0:T(8,128)(2,1)} %copy-done.1, bf16[1168,128]{1,0:T(8,128)(2,1)} %copy-done.2), custom_call_target="tpu_custom_call" | custom-call | flops 999999995904 | tf_op jit(solution)/shard_map/pairs_above/pallas_call | solution.py:259
  55.4 89.1 %all-to-all-done.arrived_ref = bf16[16,1168,128]{2,1,0:T(8,128)(2,1)} async-done(((bf16[16,1168,128]{2,1,0:T(8,128)(2,1)}), bf16[16,1168,128]{2,1,0:T(8,128)(2,1)}, u32[]{:S(2)}, u32[]{:S(2)}) %all-to-all-start) | async-done | bytes 4784160 | tf_op jit(solution)/shard_map/all_to_all | solution.py:57
  144.5 15.5 %team_pairs.1 = (bf16[48,256,128]{2,1,0:T(8,128)(2,1)}, f32[32,256,128]{2,1,0:T(8,128)}, bf16[1168,128]{1,0:T(8,128)(2,1)}, bf16[1168,128]{1,0:T(8,128)(2,1)}, b...) custom-call(bf16[16,1168,128]{2,1,0:T(8,128)(2,1)} %all-to-all-done., ...), custom_call_target="tpu_custom_call", output_to_operand_aliasing={{2}: (3, {}), {3}: (4, {}), {4}: (5, {}), {5}: (6, {}), {6}... | custom-call | flops 2013265920 | bytes 16252928 | tf_op jit(solution)/shard_map/team_pairs/pallas_call | solution.py:307
  160.0 1.0 collective-permute-start.8
  161.0 2.7 collective-permute-start.9
  163.7 9.1 %collective-permute-start.10 = (bf16[1168,128]{1,0:T(8,128)(2,1)}, bf16[1168,128]{1,0:T(8,128)(2,1)S(1)}, u32[]{:S(2)}, u32[]{:S(2)}) collective-permute-start(bf16[1168,128]{1,0:T(8,128)(2,1)} %get-tuple-element.94), channel_id=1, source_target_pairs={{0,112},{8,120},{16,96},{24,104},{32,144},{40,152},{48,128},{56,13... | collective-permute-start | bytes 897032 | tf_op jit(solution)/shard_map/ppermute | solution.py:41
  172.8 2.7 collective-permute-start.11
  176.1 3.9 collective-permute-start.13
  180.0 4.7 %collective-permute-start.18 = (bf16[8,256,128]{2,1,0:T(8,128)(2,1)S(1)}, bf16[8,256,128]{2,1,0:T(8,128)(2,1)S(1)}, u32[]{:S(2)}, u32[]{:S(2)}) collective-permute-start(bf16[8,256,128]{2,1,0:T(8,128)(2,1)S(1)} %copy-done.25), channel_id=1, source_target_pairs={{1,0},{2,1},{3,2},{4,3},{5,4},{6,5},{7,6},{9,8},{10,9},{11,10},{12... | collective-permute-start | bytes 1572872 | tf_op jit(solution)/shard_map/ppermute | solution.py:65
  184.7 10.3 %collective-permute-done.10.rest_1_ = bf16[1168,128]{1,0:T(8,128)(2,1)S(1)} collective-permute-done((bf16[1168,128]{1,0:T(8,128)(2,1)}, bf16[1168,128]{1,0:T(8,128)(2,1)S(1)}, u32[]{:S(2)}, u32[]{:S(2)}) %collective-permute-start.10) | collective-permute-done | bytes 299040 | tf_op jit(solution)/shard_map/ppermute | solution.py:41
  195.0 6.6 %collective-permute-start.14 = (bf16[1168,128]{1,0:T(8,128)(2,1)}, bf16[1168,128]{1,0:T(8,128)(2,1)S(1)}, u32[]{:S(2)}, u32[]{:S(2)}) collective-permute-start(bf16[1168,128]{1,0:T(8,128)(2,1)} %get-tuple-element.98), channel_id=1, source_target_pairs={{0,120},{8,96},{16,104},{24,112},{32,152},{40,128},{48,136},{56,14... | collective-permute-start | bytes 897032 | tf_op jit(solution)/shard_map/ppermute | solution.py:41
  202.0 1.6 collective-permute-start.15
  203.6 10.7 %shifted_pairs.3 = (bf16[3,256,128]{2,1,0:T(8,128)(2,1)}, bf16[3,256,128]{2,1,0:T(8,128)(2,1)}, bf16[3,256,128]{2,1,0:T(8,128)(2,1)}, bf16[3,256,128]{2,1,0:T(8,...) custom-call(bf16[32,384,128]{2,1,0:T(8,128)(2,1)} %get-tuple-element, ...), custom_call_target="tpu_custom_call", output_to_operand_aliasing={{8}: (1, {}), {9}: (2, {}), {10}: (3, {})} | custom-call | flops 1006632960 | bytes 12320768 | tf_op jit(solution)/shard_map/shifted_pairs/pallas_call | solution.py:362
  214.3 5.9 %collective-permute-start.16 = (bf16[1168,128]{1,0:T(8,128)(2,1)}, bf16[1168,128]{1,0:T(8,128)(2,1)S(1)}, u32[]{:S(2)}, u32[]{:S(2)}) collective-permute-start(bf16[1168,128]{1,0:T(8,128)(2,1)} %get-tuple-element.101), channel_id=1, source_target_pairs={{0,56},{8,32},{16,40},{24,48},{32,88},{40,64},{48,72},{56,80},{64,... | collective-permute-start | bytes 897032 | tf_op jit(solution)/shard_map/ppermute | solution.py:41
  220.3 8.9 %collective-permute-done.14.rest_5_ = bf16[1168,128]{1,0:T(8,128)(2,1)S(1)} collective-permute-done((bf16[1168,128]{1,0:T(8,128)(2,1)}, bf16[1168,128]{1,0:T(8,128)(2,1)S(1)}, u32[]{:S(2)}, u32[]{:S(2)}) %collective-permute-start.14) | collective-permute-done | bytes 299040 | tf_op jit(solution)/shard_map/ppermute | solution.py:41
  229.1 0.9 collective-permute-start.19
  230.1 4.1 %collective-permute-start.20 = (bf16[3,256,128]{2,1,0:T(8,128)(2,1)}, bf16[3,256,128]{2,1,0:T(8,128)(2,1)}, u32[]{:S(2)}, u32[]{:S(2)}) collective-permute-start(bf16[3,256,128]{2,1,0:T(8,128)(2,1)} %get-tuple-element.116), channel_id=1, source_target_pairs={{0,96},{8,104},{16,112},{24,120},{32,128},{40,136},{48,144},{56,15... | collective-permute-start | bytes 589832 | tf_op jit(solution)/shard_map/ppermute | solution.py:41
  234.2 9.5 %shifted_pairs.4 = (bf16[3,256,128]{2,1,0:T(8,128)(2,1)}, bf16[3,256,128]{2,1,0:T(8,128)(2,1)}, bf16[3,256,128]{2,1,0:T(8,128)(2,1)}, bf16[3,256,128]{2,1,0:T(8,...) custom-call(bf16[32,384,128]{2,1,0:T(8,128)(2,1)} %get-tuple-element, ...), custom_call_target="tpu_custom_call", output_to_operand_aliasing={{6}: (1, {}), {7}: (2, {})} | custom-call | flops 754974720 | bytes 11337728 | tf_op jit(solution)/shard_map/shifted_pairs/pallas_call | solution.py:362
  243.7 11.0 %all-to-all-start.1 = ((bf16[48,256,128]{2,1,0:T(8,128)(2,1)}), bf16[48,256,128]{2,1,0:T(8,128)(2,1)}, u32[]{:S(2)}, u32[]{:S(2)}) async-start(bf16[48,256,128]{2,1,0:T(8,128)(2,1)} %get-tuple-element.104), calls=%async_computation.1 | async-start | bytes 6291456 | tf_op jit(solution)/shard_map/all_to_all | solution.py:57
  254.8 2.0 collective-permute-start.22
  256.8 4.0 %collective-permute-start.23 = (bf16[3,256,128]{2,1,0:T(8,128)(2,1)}, bf16[3,256,128]{2,1,0:T(8,128)(2,1)}, u32[]{:S(2)}, u32[]{:S(2)}) collective-permute-start(bf16[3,256,128]{2,1,0:T(8,128)(2,1)} %get-tuple-element.119), channel_id=1, source_target_pairs={{0,184},{8,160},{16,168},{24,176},{32,216},{40,192},{48,200},{56,2... | collective-permute-start | bytes 589832 | tf_op jit(solution)/shard_map/ppermute | solution.py:41
  260.8 1.9 collective-permute-start.24
  262.7 6.5 %shifted_pairs.5 = (bf16[3,256,128]{2,1,0:T(8,128)(2,1)}, bf16[3,256,128]{2,1,0:T(8,128)(2,1)}, f32[32,256,128]{2,1,0:T(8,128)}) custom-call(bf16[32,384,128]{2,1,0:T(8,128)(2,1)} %get-tuple-element.69.own_ref, f32[32,256,128]{2,1,0:T(8,128)} %get-tuple-element.100.given_ref, bf16[1168,128]{1,0:T(8,128)(2,1)} %copy-done.26, ...), custom_call_target="tpu_custom_call", output_to_operand_aliasing={{2}: (1, {})} | custom-call | flops 999999995904 | tf_op jit(solution)/shard_map/shifted_pairs/pallas_call | solution.py:362
  269.2 62.4 %all-to-all-done.1.back_ref = bf16[48,256,128]{2,1,0:T(8,128)(2,1)} async-done(((bf16[48,256,128]{2,1,0:T(8,128)(2,1)}), bf16[48,256,128]{2,1,0:T(8,128)(2,1)}, u32[]{:S(2)}, u32[]{:S(2)}) %all-to-all-start.1) | async-done | bytes 3145760 | tf_op jit(solution)/shard_map/all_to_all | solution.py:57
  331.6 6.6 %gather_team.1 = (f32[32,256,128]{2,1,0:T(8,128)}, bf16[3,256,128]{2,1,0:T(8,128)(2,1)}, bf16[3,256,128]{2,1,0:T(8,128)(2,1)}, bf16[3,256,128]{2,1,0:T(8,128)(2,...) custom-call(s32[96]{0:T(128)} %get-tuple-element.68.used_ref, ...), custom_call_target="tpu_custom_call", output_to_operand_aliasing={{0}: (3, {}), {1}: (6, {}), {2}: (7, {}), {3}: (8, {}), {4}... | custom-call | flops 1572864 | bytes 11534336 | tf_op jit(solution)/shard_map/gather_team/pallas_call | solution.py:411
  338.3 2.9 collective-permute-start.26
  341.2 2.3 collective-permute-start.27
  343.6 1.2 collective-permute-done.23.rest_4_
  344.8 4.7 %collective-permute-start.28 = (bf16[3,256,128]{2,1,0:T(8,128)(2,1)}, bf16[3,256,128]{2,1,0:T(8,128)(2,1)S(1)}, u32[]{:S(2)}, u32[]{:S(2)}) collective-permute-start(bf16[3,256,128]{2,1,0:T(8,128)(2,1)} %get-tuple-element.124), channel_id=1, source_target_pairs={{0,112},{8,120},{16,96},{24,104},{32,144},{40,152},{48,128},{56,13... | collective-permute-start | bytes 589832 | tf_op jit(solution)/shard_map/ppermute | solution.py:41
  349.7 4.3 %collective-permute-start.30 = (bf16[3,256,128]{2,1,0:T(8,128)(2,1)}, bf16[3,256,128]{2,1,0:T(8,128)(2,1)S(1)}, u32[]{:S(2)}, u32[]{:S(2)}) collective-permute-start(bf16[3,256,128]{2,1,0:T(8,128)(2,1)} %get-tuple-element.126), channel_id=1, source_target_pairs={{0,48},{8,56},{16,32},{24,40},{32,80},{40,88},{48,64},{56,72},{64,... | collective-permute-start | bytes 589832 | tf_op jit(solution)/shard_map/ppermute | solution.py:41
  354.0 8.6 %collective-permute-start.31 = (bf16[3,256,128]{2,1,0:T(8,128)(2,1)}, bf16[3,256,128]{2,1,0:T(8,128)(2,1)S(1)}, u32[]{:S(2)}, u32[]{:S(2)}) collective-permute-start(bf16[3,256,128]{2,1,0:T(8,128)(2,1)} %get-tuple-element.127), channel_id=1, source_target_pairs={{0,168},{8,176},{16,184},{24,160},{32,200},{40,208},{48,216},{56,1... | collective-permute-start | bytes 589832 | tf_op jit(solution)/shard_map/ppermute | solution.py:41
  362.6 5.7 %collective-permute-start.32 = (bf16[3,256,128]{2,1,0:T(8,128)(2,1)}, bf16[3,256,128]{2,1,0:T(8,128)(2,1)S(1)}, u32[]{:S(2)}, u32[]{:S(2)}) collective-permute-start(bf16[3,256,128]{2,1,0:T(8,128)(2,1)} %get-tuple-element.128), channel_id=1, source_target_pairs={{0,120},{8,96},{16,104},{24,112},{32,152},{40,128},{48,136},{56,14... | collective-permute-start | bytes 589832 | tf_op jit(solution)/shard_map/ppermute | solution.py:41
  368.3 1.8 collective-permute-start.33
  370.2 7.7 %collective-permute-start.34 = (bf16[3,256,128]{2,1,0:T(8,128)(2,1)}, bf16[3,256,128]{2,1,0:T(8,128)(2,1)S(1)}, u32[]{:S(2)}, u32[]{:S(2)}) collective-permute-start(bf16[3,256,128]{2,1,0:T(8,128)(2,1)} %get-tuple-element.130), channel_id=1, source_target_pairs={{0,56},{8,32},{16,40},{24,48},{32,88},{40,64},{48,72},{56,80},{64,... | collective-permute-start | bytes 589832 | tf_op jit(solution)/shard_map/ppermute | solution.py:41
  377.9 7.8 %collective-permute-done.33.rest_14_ = bf16[3,256,128]{2,1,0:T(8,128)(2,1)S(1)} collective-permute-done((bf16[3,256,128]{2,1,0:T(8,128)(2,1)}, bf16[3,256,128]{2,1,0:T(8,128)(2,1)S(1)}, u32[]{:S(2)}, u32[]{:S(2)}) %collective-permute-start.33) | collective-permute-done | bytes 196640 | tf_op jit(solution)/shard_map/ppermute | solution.py:41
  386.4 12.1 %gather_and_mix.1 = bf16[8192,128]{1,0:T(8,128)(2,1)} custom-call(s32[96]{0:T(128)} %get-tuple-element.68.used_ref, s32[16]{0:T(128)} %stack.70.dests_ref, f32[32,256,128]{2,1,0:T(8,128)} %get-tuple-element.114.total_ref, bf16[8192,128]{1,0:T(8,128)(2,1)} %bitcast.28, bf16[128,128]{1,0:T(8,128)(2,1)} %w_ref.1, f32[1,128]{1,0:T(1,128)} %bitcast.36, ...), custom_call_target="tpu_custom_call" | custom-call | tf_op jit(solution)/shard_map/gather_and_mix/pallas_call | solution.py:455
  (101 shorter events, 4.4 us)
Async XLA Ops:
  0.0 21.8 %copy-start.22 = (s32[1,8]{1,0:T(1,128)S(1)}, s32[1,8]{1,0:T(1,128)}, u32[]{:S(2)}) copy-start(s32[1,8]{1,0:T(1,128)} %param.25) | copy-start | bytes 100
  0.0 21.8 %copy-start.23 = (s32[1,8]{1,0:T(1,128)S(1)}, s32[1,8]{1,0:T(1,128)}, u32[]{:S(2)}) copy-start(s32[1,8]{1,0:T(1,128)} %param.24) | copy-start | bytes 100
  13.9 34.8 %collective-permute-start.1 = (bf16[8,384,128]{2,1,0:T(8,128)(2,1)}, bf16[8,384,128]{2,1,0:T(8,128)(2,1)S(1)}, u32[]{:S(2)}, u32[]{:S(2)}) collective-permute-start(bf16[8,384,128]{2,1,0:T(8,128)(2,1)} %get-tuple-element.71), channel_id=1, source_target_pairs={{0,1},{1,2},{2,3},{3,4},{4,5},{5,6},{6,7},{8,9},{9,10},{10,11},{11... | collective-permute-start | bytes 2359304 | tf_op jit(solution)/shard_map/ppermute | solution.py:65
  15.8 26.9 %collective-permute-start.2 = (bf16[1168,128]{1,0:T(8,128)(2,1)}, bf16[1168,128]{1,0:T(8,128)(2,1)S(1)}, u32[]{:S(2)}, u32[]{:S(2)}) collective-permute-start(bf16[1168,128]{1,0:T(8,128)(2,1)} %get-tuple-element.72), channel_id=1, source_target_pairs={{0,96},{8,104},{16,112},{24,120},{32,128},{40,136},{48,144},{56,15... | collective-permute-start | bytes 897032 | tf_op jit(solution)/shard_map/ppermute | solution.py:41
  21.7 26.5 %collective-permute-start.3 = (bf16[1168,128]{1,0:T(8,128)(2,1)}, bf16[1168,128]{1,0:T(8,128)(2,1)S(1)}, u32[]{:S(2)}, u32[]{:S(2)}) collective-permute-start(bf16[1168,128]{1,0:T(8,128)(2,1)} %get-tuple-element.73), channel_id=1, source_target_pairs={{0,160},{8,168},{16,176},{24,184},{32,192},{40,200},{48,208},{56,2... | collective-permute-start | bytes 897032 | tf_op jit(solution)/shard_map/ppermute | solution.py:41
  21.8 14.6 %collective-permute-start = (s32[8,2]{0,1:T(2,128)S(1)}, s32[8,2]{0,1:T(2,128)S(1)}, u32[]{:S(2)}, u32[]{:S(2)}) collective-permute-start(s32[8,2]{0,1:T(2,128)S(1)} %pad_add_fusion), channel_id=1, source_target_pairs={{0,1},{1,2},{2,3},{3,4},{4,5},{5,6},{6,7},{8,9},{9,10},{10,11},{11... | collective-permute-start | bytes 200 | tf_op jit(solution)/shard_map/ppermute | solution.py:65
  25.0 119.5 %all-to-all-start = ((bf16[16,1168,128]{2,1,0:T(8,128)(2,1)}), bf16[16,1168,128]{2,1,0:T(8,128)(2,1)}, u32[]{:S(2)}, u32[]{:S(2)}) async-start(bf16[16,1168,128]{2,1,0:T(8,128)(2,1)} %get-tuple-element.70), calls=%async_computation | async-start | bytes 9568256 | tf_op jit(solution)/shard_map/all_to_all | solution.py:57
  34.5 126.5 %collective-permute-start.4 = (bf16[1168,128]{1,0:T(8,128)(2,1)}, bf16[1168,128]{1,0:T(8,128)(2,1)}, u32[]{:S(2)}, u32[]{:S(2)}) collective-permute-start(bf16[1168,128]{1,0:T(8,128)(2,1)} %get-tuple-element.86), channel_id=1, source_target_pairs={{0,32},{8,40},{16,48},{24,56},{32,64},{40,72},{48,80},{56,88},{64,... | collective-permute-start | bytes 897032 | tf_op jit(solution)/shard_map/ppermute | solution.py:41
  36.4 127.3 %collective-permute-start.5 = (bf16[1168,128]{1,0:T(8,128)(2,1)}, bf16[1168,128]{1,0:T(8,128)(2,1)}, u32[]{:S(2)}, u32[]{:S(2)}) collective-permute-start(bf16[1168,128]{1,0:T(8,128)(2,1)} %get-tuple-element.87), channel_id=1, source_target_pairs={{0,224},{8,232},{16,240},{24,248},{32,0},{40,8},{48,16},{56,24},{6... | collective-permute-start | bytes 897032 | tf_op jit(solution)/shard_map/ppermute | solution.py:41
  42.7 130.1 %collective-permute-start.6 = (bf16[1168,128]{1,0:T(8,128)(2,1)}, bf16[1168,128]{1,0:T(8,128)(2,1)}, u32[]{:S(2)}, u32[]{:S(2)}) collective-permute-start(bf16[1168,128]{1,0:T(8,128)(2,1)} %get-tuple-element.88), channel_id=1, source_target_pairs={{0,104},{8,112},{16,120},{24,96},{32,136},{40,144},{48,152},{56,12... | collective-permute-start | bytes 897032 | tf_op jit(solution)/shard_map/ppermute | solution.py:41
  48.1 127.4 %collective-permute-start.7 = (bf16[1168,128]{1,0:T(8,128)(2,1)}, bf16[1168,128]{1,0:T(8,128)(2,1)}, u32[]{:S(2)}, u32[]{:S(2)}) collective-permute-start(bf16[1168,128]{1,0:T(8,128)(2,1)} %get-tuple-element.89), channel_id=1, source_target_pairs={{0,184},{8,160},{16,168},{24,176},{32,216},{40,192},{48,200},{56,2... | collective-permute-start | bytes 897032 | tf_op jit(solution)/shard_map/ppermute | solution.py:41
  144.5 35.5 %copy-start.25 = (bf16[8,256,128]{2,1,0:T(8,128)(2,1)S(1)}, bf16[8,256,128]{2,1,0:T(8,128)(2,1)}, u32[]{:S(2)}) copy-start(bf16[8,256,128]{2,1,0:T(8,128)(2,1)} %get-tuple-element.105) | copy-start | bytes 1572868
  160.0 16.0 %collective-permute-start.8 = (bf16[1168,128]{1,0:T(8,128)(2,1)}, bf16[1168,128]{1,0:T(8,128)(2,1)S(1)}, u32[]{:S(2)}, u32[]{:S(2)}) collective-permute-start(bf16[1168,128]{1,0:T(8,128)(2,1)} %get-tuple-element.90), channel_id=1, source_target_pairs={{0,40},{8,48},{16,56},{24,32},{32,72},{40,80},{48,88},{56,64},{64,... | collective-permute-start | bytes 897032 | tf_op jit(solution)/shard_map/ppermute | solution.py:41
  161.0 19.0 %collective-permute-start.9 = (bf16[1168,128]{1,0:T(8,128)(2,1)}, bf16[1168,128]{1,0:T(8,128)(2,1)S(1)}, u32[]{:S(2)}, u32[]{:S(2)}) collective-permute-start(bf16[1168,128]{1,0:T(8,128)(2,1)} %get-tuple-element.91), channel_id=1, source_target_pairs={{0,248},{8,224},{16,232},{24,240},{32,24},{40,0},{48,8},{56,16},{6... | collective-permute-start | bytes 897032 | tf_op jit(solution)/shard_map/ppermute | solution.py:41
  163.7 31.3 %collective-permute-start.10 = (bf16[1168,128]{1,0:T(8,128)(2,1)}, bf16[1168,128]{1,0:T(8,128)(2,1)S(1)}, u32[]{:S(2)}, u32[]{:S(2)}) collective-permute-start(bf16[1168,128]{1,0:T(8,128)(2,1)} %get-tuple-element.94), channel_id=1, source_target_pairs={{0,112},{8,120},{16,96},{24,104},{32,144},{40,152},{48,128},{56,13... | collective-permute-start | bytes 897032 | tf_op jit(solution)/shard_map/ppermute | solution.py:41
  172.8 29.2 %collective-permute-start.11 = (bf16[1168,128]{1,0:T(8,128)(2,1)}, bf16[1168,128]{1,0:T(8,128)(2,1)S(1)}, u32[]{:S(2)}, u32[]{:S(2)}) collective-permute-start(bf16[1168,128]{1,0:T(8,128)(2,1)} %get-tuple-element.95), channel_id=1, source_target_pairs={{0,176},{8,184},{16,160},{24,168},{32,208},{40,216},{48,192},{56,2... | collective-permute-start | bytes 897032 | tf_op jit(solution)/shard_map/ppermute | solution.py:41
  175.5 38.8 %collective-permute-start.12 = (bf16[1168,128]{1,0:T(8,128)(2,1)}, bf16[1168,128]{1,0:T(8,128)(2,1)S(1)}, u32[]{:S(2)}, u32[]{:S(2)}) collective-permute-start(bf16[1168,128]{1,0:T(8,128)(2,1)} %get-tuple-element.96), channel_id=1, source_target_pairs={{0,48},{8,56},{16,32},{24,40},{32,80},{40,88},{48,64},{56,72},{64,... | collective-permute-start | bytes 897032 | tf_op jit(solution)/shard_map/ppermute | solution.py:41
  176.1 27.6 %copy-start.7 = (bf16[1168,128]{1,0:T(8,128)(2,1)}, bf16[1168,128]{1,0:T(8,128)(2,1)S(1)}, u32[]{:S(2)}) copy-start(bf16[1168,128]{1,0:T(8,128)(2,1)S(1)} %collective-permute-done.8.rest_8_) | copy-start | bytes 897028
  176.1 44.2 %collective-permute-start.13 = (bf16[1168,128]{1,0:T(8,128)(2,1)}, bf16[1168,128]{1,0:T(8,128)(2,1)S(1)}, u32[]{:S(2)}, u32[]{:S(2)}) collective-permute-start(bf16[1168,128]{1,0:T(8,128)(2,1)} %get-tuple-element.97), channel_id=1, source_target_pairs={{0,240},{8,248},{16,224},{24,232},{32,16},{40,24},{48,0},{56,8},{6... | collective-permute-start | bytes 897032 | tf_op jit(solution)/shard_map/ppermute | solution.py:41
  180.0 23.7 %copy-start.8 = (bf16[1168,128]{1,0:T(8,128)(2,1)}, bf16[1168,128]{1,0:T(8,128)(2,1)S(1)}, u32[]{:S(2)}) copy-start(bf16[1168,128]{1,0:T(8,128)(2,1)S(1)} %collective-permute-done.9.rest_9_) | copy-start | bytes 897028
  180.0 74.6 %collective-permute-start.18 = (bf16[8,256,128]{2,1,0:T(8,128)(2,1)S(1)}, bf16[8,256,128]{2,1,0:T(8,128)(2,1)S(1)}, u32[]{:S(2)}, u32[]{:S(2)}) collective-permute-start(bf16[8,256,128]{2,1,0:T(8,128)(2,1)S(1)} %copy-done.25), channel_id=1, source_target_pairs={{1,0},{2,1},{3,2},{4,3},{5,4},{6,5},{7,6},{9,8},{10,9},{11,10},{12... | collective-permute-start | bytes 1572872 | tf_op jit(solution)/shard_map/ppermute | solution.py:65
  195.0 19.3 %copy-start.3 = (bf16[1168,128]{1,0:T(8,128)(2,1)}, bf16[1168,128]{1,0:T(8,128)(2,1)S(1)}, u32[]{:S(2)}) copy-start(bf16[1168,128]{1,0:T(8,128)(2,1)S(1)} %collective-permute-done.10.rest_1_) | copy-start | bytes 897028
  195.0 34.1 %collective-permute-start.14 = (bf16[1168,128]{1,0:T(8,128)(2,1)}, bf16[1168,128]{1,0:T(8,128)(2,1)S(1)}, u32[]{:S(2)}, u32[]{:S(2)}) collective-permute-start(bf16[1168,128]{1,0:T(8,128)(2,1)} %get-tuple-element.98), channel_id=1, source_target_pairs={{0,120},{8,96},{16,104},{24,112},{32,152},{40,128},{48,136},{56,14... | collective-permute-start | bytes 897032 | tf_op jit(solution)/shard_map/ppermute | solution.py:41
  202.0 28.1 %collective-permute-start.15 = (bf16[1168,128]{1,0:T(8,128)(2,1)}, bf16[1168,128]{1,0:T(8,128)(2,1)S(1)}, u32[]{:S(2)}, u32[]{:S(2)}) collective-permute-start(bf16[1168,128]{1,0:T(8,128)(2,1)} %get-tuple-element.99), channel_id=1, source_target_pairs={{0,168},{8,176},{16,184},{24,160},{32,200},{40,208},{48,216},{56,1... | collective-permute-start | bytes 897032 | tf_op jit(solution)/shard_map/ppermute | solution.py:41
  214.3 19.9 %copy-start.5 = (bf16[1168,128]{1,0:T(8,128)(2,1)}, bf16[1168,128]{1,0:T(8,128)(2,1)S(1)}, u32[]{:S(2)}) copy-start(bf16[1168,128]{1,0:T(8,128)(2,1)S(1)} %collective-permute-done.12.rest_3_) | copy-start | bytes 897028
  214.3 42.4 %collective-permute-start.16 = (bf16[1168,128]{1,0:T(8,128)(2,1)}, bf16[1168,128]{1,0:T(8,128)(2,1)S(1)}, u32[]{:S(2)}, u32[]{:S(2)}) collective-permute-start(bf16[1168,128]{1,0:T(8,128)(2,1)} %get-tuple-element.101), channel_id=1, source_target_pairs={{0,56},{8,32},{16,40},{24,48},{32,88},{40,64},{48,72},{56,80},{64,... | collective-permute-start | bytes 897032 | tf_op jit(solution)/shard_map/ppermute | solution.py:41
  220.2 40.5 %collective-permute-start.17 = (bf16[1168,128]{1,0:T(8,128)(2,1)}, bf16[1168,128]{1,0:T(8,128)(2,1)S(1)}, u32[]{:S(2)}, u32[]{:S(2)}) collective-permute-start(bf16[1168,128]{1,0:T(8,128)(2,1)} %get-tuple-element.102), channel_id=1, source_target_pairs={{0,232},{8,240},{16,248},{24,224},{32,8},{40,16},{48,24},{56,0},{6... | collective-permute-start | bytes 897032 | tf_op jit(solution)/shard_map/ppermute | solution.py:41
  229.1 25.6 %collective-permute-start.19 = (bf16[3,256,128]{2,1,0:T(8,128)(2,1)}, bf16[3,256,128]{2,1,0:T(8,128)(2,1)S(1)}, u32[]{:S(2)}, u32[]{:S(2)}) collective-permute-start(bf16[3,256,128]{2,1,0:T(8,128)(2,1)} %get-tuple-element.115), channel_id=1, source_target_pairs={{0,160},{8,168},{16,176},{24,184},{32,192},{40,200},{48,208},{56,2... | collective-permute-start | bytes 589832 | tf_op jit(solution)/shard_map/ppermute | solution.py:41
  230.1 108.1 %collective-permute-start.20 = (bf16[3,256,128]{2,1,0:T(8,128)(2,1)}, bf16[3,256,128]{2,1,0:T(8,128)(2,1)}, u32[]{:S(2)}, u32[]{:S(2)}) collective-permute-start(bf16[3,256,128]{2,1,0:T(8,128)(2,1)} %get-tuple-element.116), channel_id=1, source_target_pairs={{0,96},{8,104},{16,112},{24,120},{32,128},{40,136},{48,144},{56,15... | collective-permute-start | bytes 589832 | tf_op jit(solution)/shard_map/ppermute | solution.py:41
  243.7 87.9 %all-to-all-start.1 = ((bf16[48,256,128]{2,1,0:T(8,128)(2,1)}), bf16[48,256,128]{2,1,0:T(8,128)(2,1)}, u32[]{:S(2)}, u32[]{:S(2)}) async-start(bf16[48,256,128]{2,1,0:T(8,128)(2,1)} %get-tuple-element.104), calls=%async_computation.1 | async-start | bytes 6291456 | tf_op jit(solution)/shard_map/all_to_all | solution.py:57
  254.6 83.7 %collective-permute-start.21 = (bf16[3,256,128]{2,1,0:T(8,128)(2,1)}, bf16[3,256,128]{2,1,0:T(8,128)(2,1)}, u32[]{:S(2)}, u32[]{:S(2)}) collective-permute-start(bf16[3,256,128]{2,1,0:T(8,128)(2,1)} %get-tuple-element.117), channel_id=1, source_target_pairs={{0,224},{8,232},{16,240},{24,248},{32,0},{40,8},{48,16},{56,24},{6... | collective-permute-start | bytes 589832 | tf_op jit(solution)/shard_map/ppermute | solution.py:41
  254.8 86.5 %collective-permute-start.22 = (bf16[3,256,128]{2,1,0:T(8,128)(2,1)}, bf16[3,256,128]{2,1,0:T(8,128)(2,1)}, u32[]{:S(2)}, u32[]{:S(2)}) collective-permute-start(bf16[3,256,128]{2,1,0:T(8,128)(2,1)} %get-tuple-element.118), channel_id=1, source_target_pairs={{0,32},{8,40},{16,48},{24,56},{32,64},{40,72},{48,80},{56,88},{64,... | collective-permute-start | bytes 589832 | tf_op jit(solution)/shard_map/ppermute | solution.py:41
  256.8 88.1 %collective-permute-start.23 = (bf16[3,256,128]{2,1,0:T(8,128)(2,1)}, bf16[3,256,128]{2,1,0:T(8,128)(2,1)}, u32[]{:S(2)}, u32[]{:S(2)}) collective-permute-start(bf16[3,256,128]{2,1,0:T(8,128)(2,1)} %get-tuple-element.119), channel_id=1, source_target_pairs={{0,184},{8,160},{16,168},{24,176},{32,216},{40,192},{48,200},{56,2... | collective-permute-start | bytes 589832 | tf_op jit(solution)/shard_map/ppermute | solution.py:41
  260.8 88.8 %collective-permute-start.24 = (bf16[3,256,128]{2,1,0:T(8,128)(2,1)}, bf16[3,256,128]{2,1,0:T(8,128)(2,1)}, u32[]{:S(2)}, u32[]{:S(2)}) collective-permute-start(bf16[3,256,128]{2,1,0:T(8,128)(2,1)} %get-tuple-element.120), channel_id=1, source_target_pairs={{0,104},{8,112},{16,120},{24,96},{32,136},{40,144},{48,152},{56,12... | collective-permute-start | bytes 589832 | tf_op jit(solution)/shard_map/ppermute | solution.py:41
  338.2 11.5 %collective-permute-start.25 = (bf16[3,256,128]{2,1,0:T(8,128)(2,1)S(1)}, bf16[3,256,128]{2,1,0:T(8,128)(2,1)S(1)}, u32[]{:S(2)}, u32[]{:S(2)}) collective-permute-start(bf16[3,256,128]{2,1,0:T(8,128)(2,1)S(1)} %copy-done.29), channel_id=1, source_target_pairs={{0,248},{8,224},{16,232},{24,240},{32,24},{40,0},{48,8},{56,16},{6... | collective-permute-start | bytes 589832 | tf_op jit(solution)/shard_map/ppermute | solution.py:41
  338.3 15.6 %collective-permute-start.26 = (bf16[3,256,128]{2,1,0:T(8,128)(2,1)S(1)}, bf16[3,256,128]{2,1,0:T(8,128)(2,1)S(1)}, u32[]{:S(2)}, u32[]{:S(2)}) collective-permute-start(bf16[3,256,128]{2,1,0:T(8,128)(2,1)S(1)} %copy-done.28), channel_id=1, source_target_pairs={{0,40},{8,48},{16,56},{24,32},{32,72},{40,80},{48,88},{56,64},{64,... | collective-permute-start | bytes 589832 | tf_op jit(solution)/shard_map/ppermute | solution.py:41
  341.2 21.4 %collective-permute-start.27 = (bf16[3,256,128]{2,1,0:T(8,128)(2,1)}, bf16[3,256,128]{2,1,0:T(8,128)(2,1)S(1)}, u32[]{:S(2)}, u32[]{:S(2)}) collective-permute-start(bf16[3,256,128]{2,1,0:T(8,128)(2,1)} %get-tuple-element.123), channel_id=1, source_target_pairs={{0,176},{8,184},{16,160},{24,168},{32,208},{40,216},{48,192},{56,2... | collective-permute-start | bytes 589832 | tf_op jit(solution)/shard_map/ppermute | solution.py:41
  344.8 23.5 %collective-permute-start.28 = (bf16[3,256,128]{2,1,0:T(8,128)(2,1)}, bf16[3,256,128]{2,1,0:T(8,128)(2,1)S(1)}, u32[]{:S(2)}, u32[]{:S(2)}) collective-permute-start(bf16[3,256,128]{2,1,0:T(8,128)(2,1)} %get-tuple-element.124), channel_id=1, source_target_pairs={{0,112},{8,120},{16,96},{24,104},{32,144},{40,152},{48,128},{56,13... | collective-permute-start | bytes 589832 | tf_op jit(solution)/shard_map/ppermute | solution.py:41
  349.5 20.6 %collective-permute-start.29 = (bf16[3,256,128]{2,1,0:T(8,128)(2,1)}, bf16[3,256,128]{2,1,0:T(8,128)(2,1)S(1)}, u32[]{:S(2)}, u32[]{:S(2)}) collective-permute-start(bf16[3,256,128]{2,1,0:T(8,128)(2,1)} %get-tuple-element.125), channel_id=1, source_target_pairs={{0,240},{8,248},{16,224},{24,232},{32,16},{40,24},{48,0},{56,8},{6... | collective-permute-start | bytes 589832 | tf_op jit(solution)/shard_map/ppermute | solution.py:41
  349.7 35.9 %copy-start.12 = (bf16[3,256,128]{2,1,0:T(8,128)(2,1)}, bf16[3,256,128]{2,1,0:T(8,128)(2,1)S(1)}, u32[]{:S(2)}) copy-start(bf16[3,256,128]{2,1,0:T(8,128)(2,1)S(1)} %collective-permute-done.25.rest_6_) | copy-start | bytes 589828
  349.7 28.1 %collective-permute-start.30 = (bf16[3,256,128]{2,1,0:T(8,128)(2,1)}, bf16[3,256,128]{2,1,0:T(8,128)(2,1)S(1)}, u32[]{:S(2)}, u32[]{:S(2)}) collective-permute-start(bf16[3,256,128]{2,1,0:T(8,128)(2,1)} %get-tuple-element.126), channel_id=1, source_target_pairs={{0,48},{8,56},{16,32},{24,40},{32,80},{40,88},{48,64},{56,72},{64,... | collective-permute-start | bytes 589832 | tf_op jit(solution)/shard_map/ppermute | solution.py:41
  354.0 31.7 %copy-start.13 = (bf16[3,256,128]{2,1,0:T(8,128)(2,1)}, bf16[3,256,128]{2,1,0:T(8,128)(2,1)S(1)}, u32[]{:S(2)}) copy-start(bf16[3,256,128]{2,1,0:T(8,128)(2,1)S(1)} %collective-permute-done.26.rest_7_) | copy-start | bytes 589828
  354.0 23.9 %collective-permute-start.31 = (bf16[3,256,128]{2,1,0:T(8,128)(2,1)}, bf16[3,256,128]{2,1,0:T(8,128)(2,1)S(1)}, u32[]{:S(2)}, u32[]{:S(2)}) collective-permute-start(bf16[3,256,128]{2,1,0:T(8,128)(2,1)} %get-tuple-element.127), channel_id=1, source_target_pairs={{0,168},{8,176},{16,184},{24,160},{32,200},{40,208},{48,216},{56,1... | collective-permute-start | bytes 589832 | tf_op jit(solution)/shard_map/ppermute | solution.py:41
  362.6 23.1 %copy-start.14 = (bf16[3,256,128]{2,1,0:T(8,128)(2,1)}, bf16[3,256,128]{2,1,0:T(8,128)(2,1)S(1)}, u32[]{:S(2)}) copy-start(bf16[3,256,128]{2,1,0:T(8,128)(2,1)S(1)} %collective-permute-done.27.rest_8_) | copy-start | bytes 589828
  362.6 15.3 %collective-permute-start.32 = (bf16[3,256,128]{2,1,0:T(8,128)(2,1)}, bf16[3,256,128]{2,1,0:T(8,128)(2,1)S(1)}, u32[]{:S(2)}, u32[]{:S(2)}) collective-permute-start(bf16[3,256,128]{2,1,0:T(8,128)(2,1)} %get-tuple-element.128), channel_id=1, source_target_pairs={{0,120},{8,96},{16,104},{24,112},{32,152},{40,128},{48,136},{56,14... | collective-permute-start | bytes 589832 | tf_op jit(solution)/shard_map/ppermute | solution.py:41
  368.3 17.4 %copy-start.15 = (bf16[3,256,128]{2,1,0:T(8,128)(2,1)}, bf16[3,256,128]{2,1,0:T(8,128)(2,1)S(1)}, u32[]{:S(2)}) copy-start(bf16[3,256,128]{2,1,0:T(8,128)(2,1)S(1)} %collective-permute-done.28.rest_9_) | copy-start | bytes 589828
  368.3 17.3 %collective-permute-start.33 = (bf16[3,256,128]{2,1,0:T(8,128)(2,1)}, bf16[3,256,128]{2,1,0:T(8,128)(2,1)S(1)}, u32[]{:S(2)}, u32[]{:S(2)}) collective-permute-start(bf16[3,256,128]{2,1,0:T(8,128)(2,1)} %get-tuple-element.129), channel_id=1, source_target_pairs={{0,232},{8,240},{16,248},{24,224},{32,8},{40,16},{48,24},{56,0},{6... | collective-permute-start | bytes 589832 | tf_op jit(solution)/shard_map/ppermute | solution.py:41
  370.2 15.5 %collective-permute-start.34 = (bf16[3,256,128]{2,1,0:T(8,128)(2,1)}, bf16[3,256,128]{2,1,0:T(8,128)(2,1)S(1)}, u32[]{:S(2)}, u32[]{:S(2)}) collective-permute-start(bf16[3,256,128]{2,1,0:T(8,128)(2,1)} %get-tuple-element.130), channel_id=1, source_target_pairs={{0,56},{8,32},{16,40},{24,48},{32,88},{40,64},{48,72},{56,80},{64,... | collective-permute-start | bytes 589832 | tf_op jit(solution)/shard_map/ppermute | solution.py:41
  (19 other events, 133.7 us)

commit v3 on v2

--- a/solution.py
+++ b/solution.py
@@ -26,7 +26,7 @@
 PASSED = 1
 MEMBERS = SPACES // 2
 TEAMS = [[z * SPAN_Y + y for z in range(p, SPAN_Z, 2) for y in range(SPAN_Y)] for p in range(2)]
-LATE = 8
+LATE = 16
 STAGE = 6
 LONG = 10**12
 SMEM = pl.BlockSpec(memory_space=pltpu.SMEM)
@@ -113,7 +113,7 @@
                     note = jnp.where(row == 2 * CAP + j, cut % 16, note)
                 notes[d] = note.astype(jnp.float32).astype(jnp.bfloat16)
 
-        @pl.loop(0, step, unroll=4)
+        @pl.loop(0, step, unroll=8)
         def _(b):
             upper = pl.ds(pl.multiple_of(b * BLK, BLK), HALF)
             lower = pl.ds(pl.multiple_of(b * BLK + HALF, HALF), HALF)
@@ -440,7 +440,7 @@
             copy.wait()
             add_back(used_ref, dests_ref, back_refs, total)
 
-        @pl.loop(0, some, unroll=2)
+        @pl.loop(0, some, unroll=8)
         def _(b):
             rows = pl.ds(pl.multiple_of(b * BLK, BLK), BLK)
             flat = total[i * some + b]

time: 404 us -> 406 us (level)
  starting transfers between devices: 130 us -> 143 us
  waiting for transfers between devices: 186 us -> 175 us
    all_to_all x2, waiting for transfers between devices: 151 us -> 80.6 us  [team_exchange(): lax.all_to_all(value, 'space', split_axis=0, concat_axis=0, tiled=True, a...]
    ppermute x32, waiting for transfers between devices: 34.2 us -> 94.9 us  [space_shift(): lax.ppermute(value, 'space', [(z * SPAN_Y + y, (z + shift[0]) % SPAN_Z *...]
    ppermute x32, starting transfers between devices: 99.3 us -> 115 us  [space_shift(): lax.ppermute(value, 'space', [(z * SPAN_Y + y, (z + shift[0]) % SPAN_Z *...]
  transfers between devices with their start and end apart: 37 -> 37, of which waited for: 9 -> 11; matrix products, arithmetic and copies ran while one was open for 0% -> 0% of each run, Pallas kernels for 14% -> 14%
where the time goes in v3:
time: 406 us; the launch traced here: 400 us
  waiting for transfers between devices  175 us (43%)
  starting transfers between devices  143 us (35%)
  Pallas kernels  75.6 us (19%)
    ppermute x32, starting transfers between devices, space_shift(): lax.ppermute(value, 'space', [(z * SPAN_Y + y, (z + shift[0]) % SPAN_Z *...  115 us
    ppermute x32, waiting for transfers between devices, space_shift(): lax.ppermute(value, 'space', [(z * SPAN_Y + y, (z + shift[0]) % SPAN_Z *...  94.9 us
    all_to_all x2, waiting for transfers between devices, team_exchange(): lax.all_to_all(value, 'space', split_axis=0, concat_axis=0, tiled=True, a...  80.6 us
    pallas_call x3, Pallas kernels, shifted_pairs(): pl.pallas_call(kernel, in_specs=[VMEM] * 2 + [ANYWHERE] * handed + [VMEM]...  26.6 us
    all_to_all x2, starting transfers between devices, team_exchange(): lax.all_to_all(value, 'space', split_axis=0, concat_axis=0, tiled=True, a...  19.8 us
    pallas_call x1, Pallas kernels, team_pairs(): pl.pallas_call(kernel, grid=(MEMBERS // CREW,), in_specs=[pl.BlockSpec((C...  15.5 us
    pallas_call x1, Pallas kernels, project_and_pack(): pl.pallas_call(kernel, grid_spec=pltpu.PrefetchScalarGridSpec(num_scalar_...  10.6 us
    pallas_call x1, Pallas kernels, gather_and_mix(): pl.pallas_call(kernel, grid_spec=pltpu.PrefetchScalarGridSpec(num_scalar_...  10.3 us
  transfers between devices with their start and end apart: 37, of which 11 were waited for; matrix products, arithmetic and copies ran while one was open for 0% of the time, Pallas kernels for 14%

profile of v3, /device:TPU:42, one launch (start us, length us, event | category | flops | bytes accessed | tf_op | source)
XLA Modules:
  0.0 400.2 jit_solution(5749030740892536622)
XLA Ops:
  0.6 0.8 copy.32
  2.8 10.6 %project_and_pack.1 = (s32[96]{0:T(128)}, bf16[32,384,128]{2,1,0:T(8,128)(2,1)}, bf16[8,384,128]{2,1,0:T(8,128)(2,1)}, bf16[16,1168,128]{2,1,0:T(8,128)(2,1)}, b...) custom-call(s32[64]{0:T(128)} %bitcast.32, ...), custom_call_target="tpu_custom_call" | custom-call | tf_op jit(solution)/shard_map/project_and_pack/pallas_call | solution.py:156
  13.5 1.9 collective-permute-start.1
  15.4 5.9 %collective-permute-start.2 = (bf16[1168,128]{1,0:T(8,128)(2,1)}, bf16[1168,128]{1,0:T(8,128)(2,1)S(1)}, u32[]{:S(2)}, u32[]{:S(2)}) collective-permute-start(bf16[1168,128]{1,0:T(8,128)(2,1)} %get-tuple-element.63), channel_id=1, source_target_pairs={{0,96},{8,104},{16,112},{24,120},{32,128},{40,136},{48,144},{56,15... | collective-permute-start | bytes 897032 | tf_op jit(solution)/shard_map/ppermute | solution.py:41
  21.4 3.2 collective-permute-start
  24.6 9.5 %all-to-all-start = ((bf16[16,1168,128]{2,1,0:T(8,128)(2,1)}), bf16[16,1168,128]{2,1,0:T(8,128)(2,1)}, u32[]{:S(2)}, u32[]{:S(2)}) async-start(bf16[16,1168,128]{2,1,0:T(8,128)(2,1)} %get-tuple-element.61), calls=%async_computation | async-start | bytes 9568256 | tf_op jit(solution)/shard_map/all_to_all | solution.py:57
  34.1 1.9 collective-permute-start.4
  36.7 5.6 %collective-permute-done.2.rest_0_.rest_2_ = bf16[1168,128]{1,0:T(8,128)(2,1)S(1)} collective-permute-done((bf16[1168,128]{1,0:T(8,128)(2,1)}, bf16[1168,128]{1,0:T(8,128)(2,1)S(1)}, u32[]{:S(2)}, u32[]{:S(2)}) %collective-permute-start.2) | collective-permute-done | bytes 299040 | tf_op jit(solution)/shard_map/ppermute | solution.py:41
  42.3 3.6 collective-permute-done.3.rest_1_.rest_3_
  46.9 6.0 %pairs_above.1 = (bf16[8,256,128]{2,1,0:T(8,128)(2,1)}, f32[32,256,128]{2,1,0:T(8,128)}) custom-call(s32[16]{0:T(128)} %reshape.3.cross_ref, bf16[8,384,128]{2,1,0:T(8,128)(2,1)} %copy-done.24, bf16[32,384,128]{2,1,0:T(8,128)(2,1)} %get-tuple-element.60.own_ref, bf16[1168,128]{1,0:T(8,128)(2,1)} %copy-done.1, bf16[1168,128]{1,0:T(8,128)(2,1)} %copy-done.2), custom_call_target="tpu_custom_call" | custom-call | flops 999999995904 | tf_op jit(solution)/shard_map/pairs_above/pallas_call | solution.py:259
  52.9 3.1 collective-permute-start.18
  56.1 7.4 %collective-permute-start.6 = (bf16[1168,128]{1,0:T(8,128)(2,1)S(1)}, bf16[1168,128]{1,0:T(8,128)(2,1)S(1)}, u32[]{:S(2)}, u32[]{:S(2)}) collective-permute-start(bf16[1168,128]{1,0:T(8,128)(2,1)S(1)} %copy-done.26), channel_id=1, source_target_pairs={{0,104},{8,112},{16,120},{24,96},{32,136},{40,144},{48,152},{56,12... | collective-permute-start | bytes 897032 | tf_op jit(solution)/shard_map/ppermute | solution.py:41
  63.5 80.6 %all-to-all-done.arrived_ref = bf16[16,1168,128]{2,1,0:T(8,128)(2,1)} async-done(((bf16[16,1168,128]{2,1,0:T(8,128)(2,1)}), bf16[16,1168,128]{2,1,0:T(8,128)(2,1)}, u32[]{:S(2)}, u32[]{:S(2)}) %all-to-all-start) | async-done | bytes 4784160 | tf_op jit(solution)/shard_map/all_to_all | solution.py:57
  144.1 15.5 %team_pairs.1 = (bf16[48,256,128]{2,1,0:T(8,128)(2,1)}, f32[32,256,128]{2,1,0:T(8,128)}, bf16[1168,128]{1,0:T(8,128)(2,1)}, bf16[1168,128]{1,0:T(8,128)(2,1)}, b...) custom-call(bf16[16,1168,128]{2,1,0:T(8,128)(2,1)} %all-to-all-done., ...), custom_call_target="tpu_custom_call", output_to_operand_aliasing={{2}: (3, {}), {3}: (4, {}), {4}: (5, {}), {5}: (6, {}), {6}... | custom-call | flops 2013265920 | bytes 16252928 | tf_op jit(solution)/shard_map/team_pairs/pallas_call | solution.py:307
  159.6 0.9 collective-permute-start.8
  160.6 2.7 collective-permute-start.9
  163.3 5.4 %collective-permute-done.6.rest_6_ = bf16[1168,128]{1,0:T(8,128)(2,1)S(1)} collective-permute-done((bf16[1168,128]{1,0:T(8,128)(2,1)S(1)}, bf16[1168,128]{1,0:T(8,128)(2,1)S(1)}, u32[]{:S(2)}, u32[]{:S(2)}) %collective-permute-start.6) | collective-permute-done | bytes 299040 | tf_op jit(solution)/shard_map/ppermute | solution.py:41
  168.7 6.1 %collective-permute-start.10 = (bf16[1168,128]{1,0:T(8,128)(2,1)}, bf16[1168,128]{1,0:T(8,128)(2,1)S(1)}, u32[]{:S(2)}, u32[]{:S(2)}) collective-permute-start(bf16[1168,128]{1,0:T(8,128)(2,1)} %get-tuple-element.85), channel_id=1, source_target_pairs={{0,112},{8,120},{16,96},{24,104},{32,144},{40,152},{48,128},{56,13... | collective-permute-start | bytes 897032 | tf_op jit(solution)/shard_map/ppermute | solution.py:41
  174.7 1.9 collective-permute-start.11
  176.6 3.7 collective-permute-start.12
  181.1 11.4 %collective-permute-start.14 = (bf16[1168,128]{1,0:T(8,128)(2,1)}, bf16[1168,128]{1,0:T(8,128)(2,1)S(1)}, u32[]{:S(2)}, u32[]{:S(2)}) collective-permute-start(bf16[1168,128]{1,0:T(8,128)(2,1)} %get-tuple-element.89), channel_id=1, source_target_pairs={{0,120},{8,96},{16,104},{24,112},{32,152},{40,128},{48,136},{56,14... | collective-permute-start | bytes 897032 | tf_op jit(solution)/shard_map/ppermute | solution.py:41
  192.4 3.7 collective-permute-done.10.rest_1_
  196.2 7.6 %collective-permute-start.15 = (bf16[1168,128]{1,0:T(8,128)(2,1)}, bf16[1168,128]{1,0:T(8,128)(2,1)S(1)}, u32[]{:S(2)}, u32[]{:S(2)}) collective-permute-start(bf16[1168,128]{1,0:T(8,128)(2,1)} %get-tuple-element.90), channel_id=1, source_target_pairs={{0,168},{8,176},{16,184},{24,160},{32,200},{40,208},{48,216},{56,1... | collective-permute-start | bytes 897032 | tf_op jit(solution)/shard_map/ppermute | solution.py:41
  203.7 10.7 %shifted_pairs.3 = (bf16[3,256,128]{2,1,0:T(8,128)(2,1)}, bf16[3,256,128]{2,1,0:T(8,128)(2,1)}, bf16[3,256,128]{2,1,0:T(8,128)(2,1)}, bf16[3,256,128]{2,1,0:T(8,...) custom-call(bf16[32,384,128]{2,1,0:T(8,128)(2,1)} %get-tuple-element, ...), custom_call_target="tpu_custom_call", output_to_operand_aliasing={{8}: (1, {}), {9}: (2, {}), {10}: (3, {})} | custom-call | flops 1006632960 | bytes 12320768 | tf_op jit(solution)/shard_map/shifted_pairs/pallas_call | solution.py:362
  214.5 1.0 collective-permute-start.19
  215.5 4.1 %collective-permute-start.20 = (bf16[3,256,128]{2,1,0:T(8,128)(2,1)}, bf16[3,256,128]{2,1,0:T(8,128)(2,1)}, u32[]{:S(2)}, u32[]{:S(2)}) collective-permute-start(bf16[3,256,128]{2,1,0:T(8,128)(2,1)} %get-tuple-element.98), channel_id=1, source_target_pairs={{0,96},{8,104},{16,112},{24,120},{32,128},{40,136},{48,144},{56,15... | collective-permute-start | bytes 589832 | tf_op jit(solution)/shard_map/ppermute | solution.py:41
  219.9 6.2 %collective-permute-done.14.rest_5_ = bf16[1168,128]{1,0:T(8,128)(2,1)S(1)} collective-permute-done((bf16[1168,128]{1,0:T(8,128)(2,1)}, bf16[1168,128]{1,0:T(8,128)(2,1)S(1)}, u32[]{:S(2)}, u32[]{:S(2)}) %collective-permute-start.14) | collective-permute-done | bytes 299040 | tf_op jit(solution)/shard_map/ppermute | solution.py:41
  226.1 5.6 %collective-permute-start.16 = (bf16[1168,128]{1,0:T(8,128)(2,1)}, bf16[1168,128]{1,0:T(8,128)(2,1)S(1)}, u32[]{:S(2)}, u32[]{:S(2)}) collective-permute-start(bf16[1168,128]{1,0:T(8,128)(2,1)} %get-tuple-element.92), channel_id=1, source_target_pairs={{0,56},{8,32},{16,40},{24,48},{32,88},{40,64},{48,72},{56,80},{64,... | collective-permute-start | bytes 897032 | tf_op jit(solution)/shard_map/ppermute | solution.py:41
  231.6 4.5 %collective-permute-done.15.rest_6_ = bf16[1168,128]{1,0:T(8,128)(2,1)S(1)} collective-permute-done((bf16[1168,128]{1,0:T(8,128)(2,1)}, bf16[1168,128]{1,0:T(8,128)(2,1)S(1)}, u32[]{:S(2)}, u32[]{:S(2)}) %collective-permute-start.15) | collective-permute-done | bytes 299040 | tf_op jit(solution)/shard_map/ppermute | solution.py:41
  236.8 5.7 %collective-permute-done.19.rest_0_ = bf16[3,256,128]{2,1,0:T(8,128)(2,1)} collective-permute-done((bf16[3,256,128]{2,1,0:T(8,128)(2,1)}, bf16[3,256,128]{2,1,0:T(8,128)(2,1)}, u32[]{:S(2)}, u32[]{:S(2)}) %collective-permute-start.19) | collective-permute-done | bytes 196640 | tf_op jit(solution)/shard_map/ppermute | solution.py:41
  242.6 2.8 collective-permute-start.22
  245.4 1.2 collective-permute-start.23
  246.8 4.5 %collective-permute-start.24 = (bf16[3,256,128]{2,1,0:T(8,128)(2,1)}, bf16[3,256,128]{2,1,0:T(8,128)(2,1)S(1)}, u32[]{:S(2)}, u32[]{:S(2)}) collective-permute-start(bf16[3,256,128]{2,1,0:T(8,128)(2,1)} %get-tuple-element.102), channel_id=1, source_target_pairs={{0,104},{8,112},{16,120},{24,96},{32,136},{40,144},{48,152},{56,12... | collective-permute-start | bytes 589832 | tf_op jit(solution)/shard_map/ppermute | solution.py:41
  251.4 9.4 %shifted_pairs.4 = (bf16[3,256,128]{2,1,0:T(8,128)(2,1)}, bf16[3,256,128]{2,1,0:T(8,128)(2,1)}, bf16[3,256,128]{2,1,0:T(8,128)(2,1)}, bf16[3,256,128]{2,1,0:T(8,...) custom-call(bf16[32,384,128]{2,1,0:T(8,128)(2,1)} %get-tuple-element, ...), custom_call_target="tpu_custom_call", output_to_operand_aliasing={{6}: (1, {}), {7}: (2, {})} | custom-call | flops 754974720 | bytes 11337728 | tf_op jit(solution)/shard_map/shifted_pairs/pallas_call | solution.py:362
  260.8 10.3 %all-to-all-start.1 = ((bf16[48,256,128]{2,1,0:T(8,128)(2,1)}), bf16[48,256,128]{2,1,0:T(8,128)(2,1)}, u32[]{:S(2)}, u32[]{:S(2)}) async-start(bf16[48,256,128]{2,1,0:T(8,128)(2,1)} %get-tuple-element.95), calls=%async_computation.1 | async-start | bytes 6291456 | tf_op jit(solution)/shard_map/all_to_all | solution.py:57
  271.4 2.9 collective-permute-start.26
  274.4 4.9 %collective-permute-start.27 = (bf16[3,256,128]{2,1,0:T(8,128)(2,1)}, bf16[3,256,128]{2,1,0:T(8,128)(2,1)}, u32[]{:S(2)}, u32[]{:S(2)}) collective-permute-start(bf16[3,256,128]{2,1,0:T(8,128)(2,1)} %get-tuple-element.105), channel_id=1, source_target_pairs={{0,176},{8,184},{16,160},{24,168},{32,208},{40,216},{48,192},{56,2... | collective-permute-start | bytes 589832 | tf_op jit(solution)/shard_map/ppermute | solution.py:41
  279.3 2.5 collective-permute-start.28
  281.8 1.9 collective-permute-start.29
  283.7 6.5 %shifted_pairs.5 = (bf16[3,256,128]{2,1,0:T(8,128)(2,1)}, bf16[3,256,128]{2,1,0:T(8,128)(2,1)}, f32[32,256,128]{2,1,0:T(8,128)}) custom-call(bf16[32,384,128]{2,1,0:T(8,128)(2,1)} %get-tuple-element.60.own_ref, f32[32,256,128]{2,1,0:T(8,128)} %get-tuple-element.91.given_ref, bf16[1168,128]{1,0:T(8,128)(2,1)} %copy-done.28, ...), custom_call_target="tpu_custom_call", output_to_operand_aliasing={{2}: (1, {})} | custom-call | flops 999999995904 | tf_op jit(solution)/shard_map/shifted_pairs/pallas_call | solution.py:362
  290.3 56.1 %collective-permute-done.25.rest_6_ = bf16[3,256,128]{2,1,0:T(8,128)(2,1)} collective-permute-done((bf16[3,256,128]{2,1,0:T(8,128)(2,1)}, bf16[3,256,128]{2,1,0:T(8,128)(2,1)}, u32[]{:S(2)}, u32[]{:S(2)}) %collective-permute-start.25) | collective-permute-done | bytes 196640 | tf_op jit(solution)/shard_map/ppermute | solution.py:41
  346.4 14.2 %collective-permute-start.30 = (bf16[3,256,128]{2,1,0:T(8,128)(2,1)S(1)}, bf16[3,256,128]{2,1,0:T(8,128)(2,1)S(1)}, u32[]{:S(2)}, u32[]{:S(2)}) collective-permute-start(bf16[3,256,128]{2,1,0:T(8,128)(2,1)S(1)} %copy-done.32), channel_id=1, source_target_pairs={{0,48},{8,56},{16,32},{24,40},{32,80},{40,88},{48,64},{56,72},{64,... | collective-permute-start | bytes 589832 | tf_op jit(solution)/shard_map/ppermute | solution.py:41
  360.6 1.9 collective-permute-start.31
  362.5 10.5 %collective-permute-start.32 = (bf16[3,256,128]{2,1,0:T(8,128)(2,1)S(1)}, bf16[3,256,128]{2,1,0:T(8,128)(2,1)S(1)}, u32[]{:S(2)}, u32[]{:S(2)}) collective-permute-start(bf16[3,256,128]{2,1,0:T(8,128)(2,1)S(1)} %copy-done.30), channel_id=1, source_target_pairs={{0,120},{8,96},{16,104},{24,112},{32,152},{40,128},{48,136},{56,14... | collective-permute-start | bytes 589832 | tf_op jit(solution)/shard_map/ppermute | solution.py:41
  373.0 5.5 %collective-permute-start.33 = (bf16[3,256,128]{2,1,0:T(8,128)(2,1)}, bf16[3,256,128]{2,1,0:T(8,128)(2,1)S(1)}, u32[]{:S(2)}, u32[]{:S(2)}) collective-permute-start(bf16[3,256,128]{2,1,0:T(8,128)(2,1)} %get-tuple-element.111), channel_id=1, source_target_pairs={{0,232},{8,240},{16,248},{24,224},{32,8},{40,16},{48,24},{56,0},{6... | collective-permute-start | bytes 589832 | tf_op jit(solution)/shard_map/ppermute | solution.py:41
  378.5 6.6 %gather_team.1.total_ref = f32[32,256,128]{2,1,0:T(8,128)} custom-call(s32[96]{0:T(128)} %get-tuple-element.59.used_ref, s32[16]{0:T(128)} %fusion.3.team_ref, s32[8]{0:T(128)} %bitcast.31, f32[32,256,128]{2,1,0:T(8,128)} %get-tuple-element.94.given_ref, bf16[48,256,128]{2,1,0:T(8,128)(2,1)} %all-to-all-done.1.back_ref, ...), custom_call_target="tpu_custom_call", output_to_operand_aliasing={{}: (3, {})} | custom-call | flops 1572864 | bytes 11534336 | tf_op jit(solution)/shard_map/gather_team/pallas_call | solution.py:411
  385.1 3.9 collective-permute-done.34.rest_15_
  389.7 10.3 %gather_and_mix.1 = bf16[8192,128]{1,0:T(8,128)(2,1)} custom-call(s32[96]{0:T(128)} %get-tuple-element.59.used_ref, s32[16]{0:T(128)} %stack.70.dests_ref, f32[32,256,128]{2,1,0:T(8,128)} %gather_team.1.total_ref, bf16[8192,128]{1,0:T(8,128)(2,1)} %bitcast.28, bf16[128,128]{1,0:T(8,128)(2,1)} %w_ref.1, f32[1,128]{1,0:T(1,128)} %bitcast.36, ...), custom_call_target="tpu_custom_call" | custom-call | tf_op jit(solution)/shard_map/gather_and_mix/pallas_call | solution.py:455
  (107 shorter events, 7.0 us)
Async XLA Ops:
  13.5 32.5 %collective-permute-start.1 = (bf16[8,384,128]{2,1,0:T(8,128)(2,1)}, bf16[8,384,128]{2,1,0:T(8,128)(2,1)S(1)}, u32[]{:S(2)}, u32[]{:S(2)}) collective-permute-start(bf16[8,384,128]{2,1,0:T(8,128)(2,1)} %get-tuple-element.62), channel_id=1, source_target_pairs={{0,1},{1,2},{2,3},{3,4},{4,5},{5,6},{6,7},{8,9},{9,10},{10,11},{11... | collective-permute-start | bytes 2359304 | tf_op jit(solution)/shard_map/ppermute | solution.py:65
  15.4 27.0 %collective-permute-start.2 = (bf16[1168,128]{1,0:T(8,128)(2,1)}, bf16[1168,128]{1,0:T(8,128)(2,1)S(1)}, u32[]{:S(2)}, u32[]{:S(2)}) collective-permute-start(bf16[1168,128]{1,0:T(8,128)(2,1)} %get-tuple-element.63), channel_id=1, source_target_pairs={{0,96},{8,104},{16,112},{24,120},{32,128},{40,136},{48,144},{56,15... | collective-permute-start | bytes 897032 | tf_op jit(solution)/shard_map/ppermute | solution.py:41
  21.3 24.6 %collective-permute-start.3 = (bf16[1168,128]{1,0:T(8,128)(2,1)}, bf16[1168,128]{1,0:T(8,128)(2,1)S(1)}, u32[]{:S(2)}, u32[]{:S(2)}) collective-permute-start(bf16[1168,128]{1,0:T(8,128)(2,1)} %get-tuple-element.64), channel_id=1, source_target_pairs={{0,160},{8,168},{16,176},{24,184},{32,192},{40,200},{48,208},{56,2... | collective-permute-start | bytes 897032 | tf_op jit(solution)/shard_map/ppermute | solution.py:41
  21.4 14.6 %collective-permute-start = (s32[8,2]{0,1:T(2,128)S(1)}, s32[8,2]{0,1:T(2,128)S(1)}, u32[]{:S(2)}, u32[]{:S(2)}) collective-permute-start(s32[8,2]{0,1:T(2,128)S(1)} %pad_add_fusion), channel_id=1, source_target_pairs={{0,1},{1,2},{2,3},{3,4},{4,5},{5,6},{6,7},{8,9},{9,10},{10,11},{11... | collective-permute-start | bytes 200 | tf_op jit(solution)/shard_map/ppermute | solution.py:65
  24.6 119.5 %all-to-all-start = ((bf16[16,1168,128]{2,1,0:T(8,128)(2,1)}), bf16[16,1168,128]{2,1,0:T(8,128)(2,1)}, u32[]{:S(2)}, u32[]{:S(2)}) async-start(bf16[16,1168,128]{2,1,0:T(8,128)(2,1)} %get-tuple-element.61), calls=%async_computation | async-start | bytes 9568256 | tf_op jit(solution)/shard_map/all_to_all | solution.py:57
  34.1 125.5 %collective-permute-start.4 = (bf16[1168,128]{1,0:T(8,128)(2,1)}, bf16[1168,128]{1,0:T(8,128)(2,1)}, u32[]{:S(2)}, u32[]{:S(2)}) collective-permute-start(bf16[1168,128]{1,0:T(8,128)(2,1)} %get-tuple-element.77), channel_id=1, source_target_pairs={{0,32},{8,40},{16,48},{24,56},{32,64},{40,72},{48,80},{56,88},{64,... | collective-permute-start | bytes 897032 | tf_op jit(solution)/shard_map/ppermute | solution.py:41
  52.9 123.7 %collective-permute-start.18 = (bf16[8,256,128]{2,1,0:T(8,128)(2,1)}, bf16[8,256,128]{2,1,0:T(8,128)(2,1)S(1)}, u32[]{:S(2)}, u32[]{:S(2)}) collective-permute-start(bf16[8,256,128]{2,1,0:T(8,128)(2,1)} %get-tuple-element.96), channel_id=1, source_target_pairs={{1,0},{2,1},{3,2},{4,3},{5,4},{6,5},{7,6},{9,8},{10,9},{11,10},{12... | collective-permute-start | bytes 1572872 | tf_op jit(solution)/shard_map/ppermute | solution.py:65
  56.0 104.6 %collective-permute-start.5 = (bf16[1168,128]{1,0:T(8,128)(2,1)S(1)}, bf16[1168,128]{1,0:T(8,128)(2,1)S(1)}, u32[]{:S(2)}, u32[]{:S(2)}) collective-permute-start(bf16[1168,128]{1,0:T(8,128)(2,1)S(1)} %copy-done.27), channel_id=1, source_target_pairs={{0,224},{8,232},{16,240},{24,248},{32,0},{40,8},{48,16},{56,24},{6... | collective-permute-start | bytes 897032 | tf_op jit(solution)/shard_map/ppermute | solution.py:41
  56.1 112.6 %collective-permute-start.6 = (bf16[1168,128]{1,0:T(8,128)(2,1)S(1)}, bf16[1168,128]{1,0:T(8,128)(2,1)S(1)}, u32[]{:S(2)}, u32[]{:S(2)}) collective-permute-start(bf16[1168,128]{1,0:T(8,128)(2,1)S(1)} %copy-done.26), channel_id=1, source_target_pairs={{0,104},{8,112},{16,120},{24,96},{32,136},{40,144},{48,152},{56,12... | collective-permute-start | bytes 897032 | tf_op jit(solution)/shard_map/ppermute | solution.py:41
  63.5 111.2 %collective-permute-start.7 = (bf16[1168,128]{1,0:T(8,128)(2,1)S(1)}, bf16[1168,128]{1,0:T(8,128)(2,1)S(1)}, u32[]{:S(2)}, u32[]{:S(2)}) collective-permute-start(bf16[1168,128]{1,0:T(8,128)(2,1)S(1)} %copy-done.25), channel_id=1, source_target_pairs={{0,184},{8,160},{16,168},{24,176},{32,216},{40,192},{48,200},{56,2... | collective-permute-start | bytes 897032 | tf_op jit(solution)/shard_map/ppermute | solution.py:41
  159.6 20.8 %collective-permute-start.8 = (bf16[1168,128]{1,0:T(8,128)(2,1)}, bf16[1168,128]{1,0:T(8,128)(2,1)S(1)}, u32[]{:S(2)}, u32[]{:S(2)}) collective-permute-start(bf16[1168,128]{1,0:T(8,128)(2,1)} %get-tuple-element.81), channel_id=1, source_target_pairs={{0,40},{8,48},{16,56},{24,32},{32,72},{40,80},{48,88},{56,64},{64,... | collective-permute-start | bytes 897032 | tf_op jit(solution)/shard_map/ppermute | solution.py:41
  160.6 43.2 %copy-start.7 = (bf16[1168,128]{1,0:T(8,128)(2,1)}, bf16[1168,128]{1,0:T(8,128)(2,1)S(1)}, u32[]{:S(2)}) copy-start(bf16[1168,128]{1,0:T(8,128)(2,1)S(1)} %collective-permute-done.5.rest_5_) | copy-start | bytes 897028
  160.6 20.5 %collective-permute-start.9 = (bf16[1168,128]{1,0:T(8,128)(2,1)}, bf16[1168,128]{1,0:T(8,128)(2,1)S(1)}, u32[]{:S(2)}, u32[]{:S(2)}) collective-permute-start(bf16[1168,128]{1,0:T(8,128)(2,1)} %get-tuple-element.82), channel_id=1, source_target_pairs={{0,248},{8,224},{16,232},{24,240},{32,24},{40,0},{48,8},{56,16},{6... | collective-permute-start | bytes 897032 | tf_op jit(solution)/shard_map/ppermute | solution.py:41
  168.6 35.1 %copy-start.8 = (bf16[1168,128]{1,0:T(8,128)(2,1)}, bf16[1168,128]{1,0:T(8,128)(2,1)S(1)}, u32[]{:S(2)}) copy-start(bf16[1168,128]{1,0:T(8,128)(2,1)S(1)} %collective-permute-done.6.rest_6_) | copy-start | bytes 897028
  168.7 27.5 %collective-permute-start.10 = (bf16[1168,128]{1,0:T(8,128)(2,1)}, bf16[1168,128]{1,0:T(8,128)(2,1)S(1)}, u32[]{:S(2)}, u32[]{:S(2)}) collective-permute-start(bf16[1168,128]{1,0:T(8,128)(2,1)} %get-tuple-element.85), channel_id=1, source_target_pairs={{0,112},{8,120},{16,96},{24,104},{32,144},{40,152},{48,128},{56,13... | collective-permute-start | bytes 897032 | tf_op jit(solution)/shard_map/ppermute | solution.py:41
  174.7 29.0 %copy-start.9 = (bf16[1168,128]{1,0:T(8,128)(2,1)}, bf16[1168,128]{1,0:T(8,128)(2,1)S(1)}, u32[]{:S(2)}) copy-start(bf16[1168,128]{1,0:T(8,128)(2,1)S(1)} %collective-permute-done.7.rest_7_) | copy-start | bytes 897028
  174.7 39.7 %collective-permute-start.11 = (bf16[1168,128]{1,0:T(8,128)(2,1)}, bf16[1168,128]{1,0:T(8,128)(2,1)S(1)}, u32[]{:S(2)}, u32[]{:S(2)}) collective-permute-start(bf16[1168,128]{1,0:T(8,128)(2,1)} %get-tuple-element.86), channel_id=1, source_target_pairs={{0,176},{8,184},{16,160},{24,168},{32,208},{40,216},{48,192},{56,2... | collective-permute-start | bytes 897032 | tf_op jit(solution)/shard_map/ppermute | solution.py:41
  176.6 37.8 %copy-start = (bf16[8,256,128]{2,1,0:T(8,128)(2,1)}, bf16[8,256,128]{2,1,0:T(8,128)(2,1)S(1)}, u32[]{:S(2)}) copy-start(bf16[8,256,128]{2,1,0:T(8,128)(2,1)S(1)} %collective-permute-done.18.back_x_ref) | copy-start | bytes 1572868
  176.6 38.8 %collective-permute-start.12 = (bf16[1168,128]{1,0:T(8,128)(2,1)}, bf16[1168,128]{1,0:T(8,128)(2,1)S(1)}, u32[]{:S(2)}, u32[]{:S(2)}) collective-permute-start(bf16[1168,128]{1,0:T(8,128)(2,1)} %get-tuple-element.87), channel_id=1, source_target_pairs={{0,48},{8,56},{16,32},{24,40},{32,80},{40,88},{48,64},{56,72},{64,... | collective-permute-start | bytes 897032 | tf_op jit(solution)/shard_map/ppermute | solution.py:41
  180.4 39.2 %collective-permute-start.13 = (bf16[1168,128]{1,0:T(8,128)(2,1)}, bf16[1168,128]{1,0:T(8,128)(2,1)S(1)}, u32[]{:S(2)}, u32[]{:S(2)}) collective-permute-start(bf16[1168,128]{1,0:T(8,128)(2,1)} %get-tuple-element.88), channel_id=1, source_target_pairs={{0,240},{8,248},{16,224},{24,232},{32,16},{40,24},{48,0},{56,8},{6... | collective-permute-start | bytes 897032 | tf_op jit(solution)/shard_map/ppermute | solution.py:41
  181.1 45.0 %collective-permute-start.14 = (bf16[1168,128]{1,0:T(8,128)(2,1)}, bf16[1168,128]{1,0:T(8,128)(2,1)S(1)}, u32[]{:S(2)}, u32[]{:S(2)}) collective-permute-start(bf16[1168,128]{1,0:T(8,128)(2,1)} %get-tuple-element.89), channel_id=1, source_target_pairs={{0,120},{8,96},{16,104},{24,112},{32,152},{40,128},{48,136},{56,14... | collective-permute-start | bytes 897032 | tf_op jit(solution)/shard_map/ppermute | solution.py:41
  196.2 39.9 %collective-permute-start.15 = (bf16[1168,128]{1,0:T(8,128)(2,1)}, bf16[1168,128]{1,0:T(8,128)(2,1)S(1)}, u32[]{:S(2)}, u32[]{:S(2)}) collective-permute-start(bf16[1168,128]{1,0:T(8,128)(2,1)} %get-tuple-element.90), channel_id=1, source_target_pairs={{0,168},{8,176},{16,184},{24,160},{32,200},{40,208},{48,216},{56,1... | collective-permute-start | bytes 897032 | tf_op jit(solution)/shard_map/ppermute | solution.py:41
  214.4 36.9 %copy-start.4 = (bf16[1168,128]{1,0:T(8,128)(2,1)}, bf16[1168,128]{1,0:T(8,128)(2,1)S(1)}, u32[]{:S(2)}) copy-start(bf16[1168,128]{1,0:T(8,128)(2,1)S(1)} %collective-permute-done.11.rest_2_) | copy-start | bytes 897028
  214.5 28.1 %collective-permute-start.19 = (bf16[3,256,128]{2,1,0:T(8,128)(2,1)}, bf16[3,256,128]{2,1,0:T(8,128)(2,1)}, u32[]{:S(2)}, u32[]{:S(2)}) collective-permute-start(bf16[3,256,128]{2,1,0:T(8,128)(2,1)} %get-tuple-element.97), channel_id=1, source_target_pairs={{0,160},{8,168},{16,176},{24,184},{32,192},{40,200},{48,208},{56,2... | collective-permute-start | bytes 589832 | tf_op jit(solution)/shard_map/ppermute | solution.py:41
  215.5 35.9 %copy-start.5 = (bf16[1168,128]{1,0:T(8,128)(2,1)}, bf16[1168,128]{1,0:T(8,128)(2,1)S(1)}, u32[]{:S(2)}) copy-start(bf16[1168,128]{1,0:T(8,128)(2,1)S(1)} %collective-permute-done.12.rest_3_) | copy-start | bytes 897028
  215.5 29.9 %collective-permute-start.20 = (bf16[3,256,128]{2,1,0:T(8,128)(2,1)}, bf16[3,256,128]{2,1,0:T(8,128)(2,1)}, u32[]{:S(2)}, u32[]{:S(2)}) collective-permute-start(bf16[3,256,128]{2,1,0:T(8,128)(2,1)} %get-tuple-element.98), channel_id=1, source_target_pairs={{0,96},{8,104},{16,112},{24,120},{32,128},{40,136},{48,144},{56,15... | collective-permute-start | bytes 589832 | tf_op jit(solution)/shard_map/ppermute | solution.py:41
  219.6 31.8 %copy-start.6 = (bf16[1168,128]{1,0:T(8,128)(2,1)}, bf16[1168,128]{1,0:T(8,128)(2,1)S(1)}, u32[]{:S(2)}) copy-start(bf16[1168,128]{1,0:T(8,128)(2,1)S(1)} %collective-permute-done.13.rest_4_) | copy-start | bytes 897028
  219.6 27.3 %collective-permute-start.21 = (bf16[3,256,128]{2,1,0:T(8,128)(2,1)}, bf16[3,256,128]{2,1,0:T(8,128)(2,1)}, u32[]{:S(2)}, u32[]{:S(2)}) collective-permute-start(bf16[3,256,128]{2,1,0:T(8,128)(2,1)} %get-tuple-element.99), channel_id=1, source_target_pairs={{0,224},{8,232},{16,240},{24,248},{32,0},{40,8},{48,16},{56,24},{6... | collective-permute-start | bytes 589832 | tf_op jit(solution)/shard_map/ppermute | solution.py:41
  226.1 25.3 %copy-start.10 = (bf16[1168,128]{1,0:T(8,128)(2,1)}, bf16[1168,128]{1,0:T(8,128)(2,1)S(1)}, u32[]{:S(2)}) copy-start(bf16[1168,128]{1,0:T(8,128)(2,1)S(1)} %collective-permute-done.14.rest_5_) | copy-start | bytes 897028
  226.1 53.2 %collective-permute-start.16 = (bf16[1168,128]{1,0:T(8,128)(2,1)}, bf16[1168,128]{1,0:T(8,128)(2,1)S(1)}, u32[]{:S(2)}, u32[]{:S(2)}) collective-permute-start(bf16[1168,128]{1,0:T(8,128)(2,1)} %get-tuple-element.92), channel_id=1, source_target_pairs={{0,56},{8,32},{16,40},{24,48},{32,88},{40,64},{48,72},{56,80},{64,... | collective-permute-start | bytes 897032 | tf_op jit(solution)/shard_map/ppermute | solution.py:41
  236.1 45.7 %collective-permute-start.17 = (bf16[1168,128]{1,0:T(8,128)(2,1)}, bf16[1168,128]{1,0:T(8,128)(2,1)S(1)}, u32[]{:S(2)}, u32[]{:S(2)}) collective-permute-start(bf16[1168,128]{1,0:T(8,128)(2,1)} %get-tuple-element.93), channel_id=1, source_target_pairs={{0,232},{8,240},{16,248},{24,224},{32,8},{40,16},{48,24},{56,0},{6... | collective-permute-start | bytes 897032 | tf_op jit(solution)/shard_map/ppermute | solution.py:41
  242.6 28.5 %collective-permute-start.22 = (bf16[3,256,128]{2,1,0:T(8,128)(2,1)}, bf16[3,256,128]{2,1,0:T(8,128)(2,1)S(1)}, u32[]{:S(2)}, u32[]{:S(2)}) collective-permute-start(bf16[3,256,128]{2,1,0:T(8,128)(2,1)} %get-tuple-element.100), channel_id=1, source_target_pairs={{0,32},{8,40},{16,48},{24,56},{32,64},{40,72},{48,80},{56,88},{64,... | collective-permute-start | bytes 589832 | tf_op jit(solution)/shard_map/ppermute | solution.py:41
  245.4 26.0 %collective-permute-start.23 = (bf16[3,256,128]{2,1,0:T(8,128)(2,1)}, bf16[3,256,128]{2,1,0:T(8,128)(2,1)S(1)}, u32[]{:S(2)}, u32[]{:S(2)}) collective-permute-start(bf16[3,256,128]{2,1,0:T(8,128)(2,1)} %get-tuple-element.101), channel_id=1, source_target_pairs={{0,184},{8,160},{16,168},{24,176},{32,216},{40,192},{48,200},{56,2... | collective-permute-start | bytes 589832 | tf_op jit(solution)/shard_map/ppermute | solution.py:41
  246.8 27.5 %collective-permute-start.24 = (bf16[3,256,128]{2,1,0:T(8,128)(2,1)}, bf16[3,256,128]{2,1,0:T(8,128)(2,1)S(1)}, u32[]{:S(2)}, u32[]{:S(2)}) collective-permute-start(bf16[3,256,128]{2,1,0:T(8,128)(2,1)} %get-tuple-element.102), channel_id=1, source_target_pairs={{0,104},{8,112},{16,120},{24,96},{32,136},{40,144},{48,152},{56,12... | collective-permute-start | bytes 589832 | tf_op jit(solution)/shard_map/ppermute | solution.py:41
  260.8 117.7 %all-to-all-start.1 = ((bf16[48,256,128]{2,1,0:T(8,128)(2,1)}), bf16[48,256,128]{2,1,0:T(8,128)(2,1)}, u32[]{:S(2)}, u32[]{:S(2)}) async-start(bf16[48,256,128]{2,1,0:T(8,128)(2,1)} %get-tuple-element.95), calls=%async_computation.1 | async-start | bytes 6291456 | tf_op jit(solution)/shard_map/all_to_all | solution.py:57
  271.1 75.3 %collective-permute-start.25 = (bf16[3,256,128]{2,1,0:T(8,128)(2,1)}, bf16[3,256,128]{2,1,0:T(8,128)(2,1)}, u32[]{:S(2)}, u32[]{:S(2)}) collective-permute-start(bf16[3,256,128]{2,1,0:T(8,128)(2,1)} %get-tuple-element.103), channel_id=1, source_target_pairs={{0,248},{8,224},{16,232},{24,240},{32,24},{40,0},{48,8},{56,16},{6... | collective-permute-start | bytes 589832 | tf_op jit(solution)/shard_map/ppermute | solution.py:41
  271.4 89.1 %collective-permute-start.26 = (bf16[3,256,128]{2,1,0:T(8,128)(2,1)}, bf16[3,256,128]{2,1,0:T(8,128)(2,1)}, u32[]{:S(2)}, u32[]{:S(2)}) collective-permute-start(bf16[3,256,128]{2,1,0:T(8,128)(2,1)} %get-tuple-element.104), channel_id=1, source_target_pairs={{0,40},{8,48},{16,56},{24,32},{32,72},{40,80},{48,88},{56,64},{64,... | collective-permute-start | bytes 589832 | tf_op jit(solution)/shard_map/ppermute | solution.py:41
  274.4 88.1 %collective-permute-start.27 = (bf16[3,256,128]{2,1,0:T(8,128)(2,1)}, bf16[3,256,128]{2,1,0:T(8,128)(2,1)}, u32[]{:S(2)}, u32[]{:S(2)}) collective-permute-start(bf16[3,256,128]{2,1,0:T(8,128)(2,1)} %get-tuple-element.105), channel_id=1, source_target_pairs={{0,176},{8,184},{16,160},{24,168},{32,208},{40,216},{48,192},{56,2... | collective-permute-start | bytes 589832 | tf_op jit(solution)/shard_map/ppermute | solution.py:41
  279.3 93.7 %collective-permute-start.28 = (bf16[3,256,128]{2,1,0:T(8,128)(2,1)}, bf16[3,256,128]{2,1,0:T(8,128)(2,1)}, u32[]{:S(2)}, u32[]{:S(2)}) collective-permute-start(bf16[3,256,128]{2,1,0:T(8,128)(2,1)} %get-tuple-element.106), channel_id=1, source_target_pairs={{0,112},{8,120},{16,96},{24,104},{32,144},{40,152},{48,128},{56,13... | collective-permute-start | bytes 589832 | tf_op jit(solution)/shard_map/ppermute | solution.py:41
  281.8 96.7 %collective-permute-start.29 = (bf16[3,256,128]{2,1,0:T(8,128)(2,1)}, bf16[3,256,128]{2,1,0:T(8,128)(2,1)}, u32[]{:S(2)}, u32[]{:S(2)}) collective-permute-start(bf16[3,256,128]{2,1,0:T(8,128)(2,1)} %get-tuple-element.107), channel_id=1, source_target_pairs={{0,240},{8,248},{16,224},{24,232},{32,16},{40,24},{48,0},{56,8},{6... | collective-permute-start | bytes 589832 | tf_op jit(solution)/shard_map/ppermute | solution.py:41
  283.7 62.7 %copy-start.32 = (bf16[3,256,128]{2,1,0:T(8,128)(2,1)S(1)}, bf16[3,256,128]{2,1,0:T(8,128)(2,1)}, u32[]{:S(2)}) copy-start(bf16[3,256,128]{2,1,0:T(8,128)(2,1)} %get-tuple-element.108) | copy-start | bytes 589828
  283.7 76.9 %copy-start.31 = (bf16[3,256,128]{2,1,0:T(8,128)(2,1)S(1)}, bf16[3,256,128]{2,1,0:T(8,128)(2,1)}, u32[]{:S(2)}) copy-start(bf16[3,256,128]{2,1,0:T(8,128)(2,1)} %get-tuple-element.109) | copy-start | bytes 589828
  283.7 78.8 %copy-start.30 = (bf16[3,256,128]{2,1,0:T(8,128)(2,1)S(1)}, bf16[3,256,128]{2,1,0:T(8,128)(2,1)}, u32[]{:S(2)}) copy-start(bf16[3,256,128]{2,1,0:T(8,128)(2,1)} %get-tuple-element.110) | copy-start | bytes 589828
  346.4 38.7 %collective-permute-start.30 = (bf16[3,256,128]{2,1,0:T(8,128)(2,1)S(1)}, bf16[3,256,128]{2,1,0:T(8,128)(2,1)S(1)}, u32[]{:S(2)}, u32[]{:S(2)}) collective-permute-start(bf16[3,256,128]{2,1,0:T(8,128)(2,1)S(1)} %copy-done.32), channel_id=1, source_target_pairs={{0,48},{8,56},{16,32},{24,40},{32,80},{40,88},{48,64},{56,72},{64,... | collective-permute-start | bytes 589832 | tf_op jit(solution)/shard_map/ppermute | solution.py:41
  360.6 24.5 %collective-permute-start.31 = (bf16[3,256,128]{2,1,0:T(8,128)(2,1)S(1)}, bf16[3,256,128]{2,1,0:T(8,128)(2,1)S(1)}, u32[]{:S(2)}, u32[]{:S(2)}) collective-permute-start(bf16[3,256,128]{2,1,0:T(8,128)(2,1)S(1)} %copy-done.31), channel_id=1, source_target_pairs={{0,168},{8,176},{16,184},{24,160},{32,200},{40,208},{48,216},{56,1... | collective-permute-start | bytes 589832 | tf_op jit(solution)/shard_map/ppermute | solution.py:41
  362.5 22.6 %collective-permute-start.32 = (bf16[3,256,128]{2,1,0:T(8,128)(2,1)S(1)}, bf16[3,256,128]{2,1,0:T(8,128)(2,1)S(1)}, u32[]{:S(2)}, u32[]{:S(2)}) collective-permute-start(bf16[3,256,128]{2,1,0:T(8,128)(2,1)S(1)} %copy-done.30), channel_id=1, source_target_pairs={{0,120},{8,96},{16,104},{24,112},{32,152},{40,128},{48,136},{56,14... | collective-permute-start | bytes 589832 | tf_op jit(solution)/shard_map/ppermute | solution.py:41
  373.0 12.1 %collective-permute-start.33 = (bf16[3,256,128]{2,1,0:T(8,128)(2,1)}, bf16[3,256,128]{2,1,0:T(8,128)(2,1)S(1)}, u32[]{:S(2)}, u32[]{:S(2)}) collective-permute-start(bf16[3,256,128]{2,1,0:T(8,128)(2,1)} %get-tuple-element.111), channel_id=1, source_target_pairs={{0,232},{8,240},{16,248},{24,224},{32,8},{40,16},{48,24},{56,0},{6... | collective-permute-start | bytes 589832 | tf_op jit(solution)/shard_map/ppermute | solution.py:41
  378.5 10.5 %collective-permute-start.34 = (bf16[3,256,128]{2,1,0:T(8,128)(2,1)}, bf16[3,256,128]{2,1,0:T(8,128)(2,1)S(1)}, u32[]{:S(2)}, u32[]{:S(2)}) collective-permute-start(bf16[3,256,128]{2,1,0:T(8,128)(2,1)} %get-tuple-element.112), channel_id=1, source_target_pairs={{0,56},{8,32},{16,40},{24,48},{32,88},{40,64},{48,72},{56,80},{64,... | collective-permute-start | bytes 589832 | tf_op jit(solution)/shard_map/ppermute | solution.py:41
  (22 other events, 239.1 us)

commit v4 on v1

--- a/solution.py
+++ b/solution.py
@@ -112,7 +112,7 @@
                     note = jnp.where(row == 2 * CAP + j, cut % 16, note)
                 notes[d] = note.astype(jnp.float32).astype(jnp.bfloat16)
 
-        @pl.loop(0, step, unroll=4)
+        @pl.loop(0, step, unroll=8)
         def _(b):
             upper = pl.ds(pl.multiple_of(b * BLK, BLK), HALF)
             lower = pl.ds(pl.multiple_of(b * BLK + HALF, HALF), HALF)
@@ -438,7 +438,7 @@
             copy.wait()
             add_back(used_ref, dests_ref, back_refs, total)
 
-        @pl.loop(0, some, unroll=2)
+        @pl.loop(0, some, unroll=8)
         def _(b):
             rows = pl.ds(pl.multiple_of(b * BLK, BLK), BLK)
             flat = total[i * some + b]

time: 404 us -> 401 us (level)
  starting transfers between devices: 126 us -> 116 us
  waiting for transfers between devices: 194 us -> 201 us
    ppermute x32, starting transfers between devices: 100 us -> 91.7 us  [space_shift(): lax.ppermute(value, 'space', [(z * SPAN_Y + y, (z + shift[0]) % SPAN_Z *...]
    ppermute x32, waiting for transfers between devices: 41 us -> 49.4 us  [space_shift(): lax.ppermute(value, 'space', [(z * SPAN_Y + y, (z + shift[0]) % SPAN_Z *...]
where the time goes in v4:
time: 401 us; the launch traced here: 399 us
  waiting for transfers between devices  201 us (50%)
  starting transfers between devices  116 us (29%)
  Pallas kernels  75.5 us (19%)
    all_to_all x2, waiting for transfers between devices, team_exchange(): lax.all_to_all(value, 'space', split_axis=0, concat_axis=0, tiled=True, a...  152 us
    ppermute x32, starting transfers between devices, space_shift(): lax.ppermute(value, 'space', [(z * SPAN_Y + y, (z + shift[0]) % SPAN_Z *...  91.7 us
    ppermute x32, waiting for transfers between devices, space_shift(): lax.ppermute(value, 'space', [(z * SPAN_Y + y, (z + shift[0]) % SPAN_Z *...  49.4 us
    pallas_call x3, Pallas kernels, shifted_pairs(): pl.pallas_call(kernel, in_specs=[VMEM] * 2 + [ANYWHERE] * handed + [VMEM]...  26.6 us
    all_to_all x2, starting transfers between devices, team_exchange(): lax.all_to_all(value, 'space', split_axis=0, concat_axis=0, tiled=True, a...  17.2 us
    pallas_call x1, Pallas kernels, team_pairs(): pl.pallas_call(kernel, grid=(MEMBERS // CREW,), in_specs=[pl.BlockSpec((C...  15.5 us
    pallas_call x1, Pallas kernels, project_and_pack(): pl.pallas_call(kernel, grid_spec=pltpu.PrefetchScalarGridSpec(num_scalar_...  10.7 us
    pallas_call x1, Pallas kernels, gather_and_mix(): pl.pallas_call(kernel, grid_spec=pltpu.PrefetchScalarGridSpec(num_scalar_...  10.3 us
  transfers between devices with their start and end apart: 37, of which 10 were waited for; matrix products, arithmetic and copies ran while one was open for 0% of the time, Pallas kernels for 14%

profile of v4, /device:TPU:42, one launch (start us, length us, event | category | flops | bytes accessed | tf_op | source)
XLA Modules:
  0.0 398.7 jit_solution(2335950670280373369)
XLA Ops:
  0.5 0.8 copy.42
  1.3 0.7 fusion.2.wk_ref
  2.0 0.7 stack.70.dests_ref
  2.7 10.7 %project_and_pack.1 = (s32[96]{0:T(128)}, bf16[32,384,128]{2,1,0:T(8,128)(2,1)}, bf16[8,384,128]{2,1,0:T(8,128)(2,1)}, bf16[16,1168,128]{2,1,0:T(8,128)(2,1)}, b...) custom-call(s32[64]{0:T(128)} %bitcast.32, ...), custom_call_target="tpu_custom_call" | custom-call | tf_op jit(solution)/shard_map/project_and_pack/pallas_call | solution.py:155
  13.4 1.9 collective-permute-start.1
  15.4 3.5 collective-permute-start
  18.9 10.7 %all-to-all-start = ((bf16[16,1168,128]{2,1,0:T(8,128)(2,1)}), bf16[16,1168,128]{2,1,0:T(8,128)(2,1)}, u32[]{:S(2)}, u32[]{:S(2)}) async-start(bf16[16,1168,128]{2,1,0:T(8,128)(2,1)} %get-tuple-element.72), calls=%async_computation | async-start | bytes 9568256 | tf_op jit(solution)/shard_map/all_to_all | solution.py:56
  29.5 4.9 %collective-permute-start.2 = (bf16[1168,128]{1,0:T(8,128)(2,1)}, bf16[1168,128]{1,0:T(8,128)(2,1)}, u32[]{:S(2)}, u32[]{:S(2)}) collective-permute-start(bf16[1168,128]{1,0:T(8,128)(2,1)} %get-tuple-element.88), channel_id=1, source_target_pairs={{0,96},{8,104},{16,112},{24,120},{32,128},{40,136},{48,144},{56,15... | collective-permute-start | bytes 897032 | tf_op jit(solution)/shard_map/ppermute | solution.py:40
  34.6 1.9 collective-permute-start.4
  36.7 0.7 reshape.3.cross_ref
  37.3 0.9 copy-done.24
  38.2 5.9 %pairs_above.1 = (bf16[8,256,128]{2,1,0:T(8,128)(2,1)}, f32[32,256,128]{2,1,0:T(8,128)}) custom-call(s32[16]{0:T(128)} %reshape.3.cross_ref, bf16[8,384,128]{2,1,0:T(8,128)(2,1)} %copy-done.24, bf16[32,384,128]{2,1,0:T(8,128)(2,1)} %get-tuple-element.71.own_ref), custom_call_target="tpu_custom_call" | custom-call | flops 999999995904 | tf_op jit(solution)/shard_map/pairs_above/pallas_call | solution.py:257
  44.1 95.5 %all-to-all-done.arrived_ref = bf16[16,1168,128]{2,1,0:T(8,128)(2,1)} async-done(((bf16[16,1168,128]{2,1,0:T(8,128)(2,1)}), bf16[16,1168,128]{2,1,0:T(8,128)(2,1)}, u32[]{:S(2)}, u32[]{:S(2)}) %all-to-all-start) | async-done | bytes 4784160 | tf_op jit(solution)/shard_map/all_to_all | solution.py:56
  139.6 15.5 %team_pairs.1 = (bf16[48,256,128]{2,1,0:T(8,128)(2,1)}, f32[32,256,128]{2,1,0:T(8,128)}, bf16[1168,128]{1,0:T(8,128)(2,1)}, bf16[1168,128]{1,0:T(8,128)(2,1)}, b...) custom-call(bf16[16,1168,128]{2,1,0:T(8,128)(2,1)} %all-to-all-done., ...), custom_call_target="tpu_custom_call", output_to_operand_aliasing={{2}: (3, {}), {3}: (4, {}), {4}: (5, {}), {5}: (6, {}), {6}... | custom-call | flops 2013265920 | bytes 16252928 | tf_op jit(solution)/shard_map/team_pairs/pallas_call | solution.py:305
  155.2 7.0 %collective-permute-start.6 = (bf16[1168,128]{1,0:T(8,128)(2,1)}, bf16[1168,128]{1,0:T(8,128)(2,1)S(1)}, u32[]{:S(2)}, u32[]{:S(2)}) collective-permute-start(bf16[1168,128]{1,0:T(8,128)(2,1)} %get-tuple-element.92), channel_id=1, source_target_pairs={{0,104},{8,112},{16,120},{24,96},{32,136},{40,144},{48,152},{56,12... | collective-permute-start | bytes 897032 | tf_op jit(solution)/shard_map/ppermute | solution.py:40
  162.2 6.0 %collective-permute-start.8 = (bf16[1168,128]{1,0:T(8,128)(2,1)}, bf16[1168,128]{1,0:T(8,128)(2,1)S(1)}, u32[]{:S(2)}, u32[]{:S(2)}) collective-permute-start(bf16[1168,128]{1,0:T(8,128)(2,1)} %get-tuple-element.94), channel_id=1, source_target_pairs={{0,40},{8,48},{16,56},{24,32},{32,72},{40,80},{48,88},{56,64},{64,... | collective-permute-start | bytes 897032 | tf_op jit(solution)/shard_map/ppermute | solution.py:40
  168.2 3.8 collective-permute-start.10
  172.1 9.6 %collective-permute-done.6.rest_6_ = bf16[1168,128]{1,0:T(8,128)(2,1)S(1)} collective-permute-done((bf16[1168,128]{1,0:T(8,128)(2,1)}, bf16[1168,128]{1,0:T(8,128)(2,1)S(1)}, u32[]{:S(2)}, u32[]{:S(2)}) %collective-permute-start.6) | collective-permute-done | bytes 299040 | tf_op jit(solution)/shard_map/ppermute | solution.py:40
  181.7 6.5 %collective-permute-start.11 = (bf16[1168,128]{1,0:T(8,128)(2,1)}, bf16[1168,128]{1,0:T(8,128)(2,1)S(1)}, u32[]{:S(2)}, u32[]{:S(2)}) collective-permute-start(bf16[1168,128]{1,0:T(8,128)(2,1)} %get-tuple-element.99), channel_id=1, source_target_pairs={{0,176},{8,184},{16,160},{24,168},{32,208},{40,216},{48,192},{56,2... | collective-permute-start | bytes 897032 | tf_op jit(solution)/shard_map/ppermute | solution.py:40
  188.7 8.7 %collective-permute-start.13 = (bf16[1168,128]{1,0:T(8,128)(2,1)}, bf16[1168,128]{1,0:T(8,128)(2,1)S(1)}, u32[]{:S(2)}, u32[]{:S(2)}) collective-permute-start(bf16[1168,128]{1,0:T(8,128)(2,1)} %get-tuple-element.101), channel_id=1, source_target_pairs={{0,240},{8,248},{16,224},{24,232},{32,16},{40,24},{48,0},{56,8},{6... | collective-permute-start | bytes 897032 | tf_op jit(solution)/shard_map/ppermute | solution.py:40
  197.4 1.9 collective-permute-start.18
  199.3 12.0 %collective-permute-done.10.rest_1_ = bf16[1168,128]{1,0:T(8,128)(2,1)S(1)} collective-permute-done((bf16[1168,128]{1,0:T(8,128)(2,1)}, bf16[1168,128]{1,0:T(8,128)(2,1)S(1)}, u32[]{:S(2)}, u32[]{:S(2)}) %collective-permute-start.10) | collective-permute-done | bytes 299040 | tf_op jit(solution)/shard_map/ppermute | solution.py:40
  211.3 5.9 %collective-permute-start.15 = (bf16[1168,128]{1,0:T(8,128)(2,1)}, bf16[1168,128]{1,0:T(8,128)(2,1)S(1)}, u32[]{:S(2)}, u32[]{:S(2)}) collective-permute-start(bf16[1168,128]{1,0:T(8,128)(2,1)} %get-tuple-element.103), channel_id=1, source_target_pairs={{0,168},{8,176},{16,184},{24,160},{32,200},{40,208},{48,216},{56,1... | collective-permute-start | bytes 897032 | tf_op jit(solution)/shard_map/ppermute | solution.py:40
  217.3 10.7 %shifted_pairs.3 = (bf16[3,256,128]{2,1,0:T(8,128)(2,1)}, bf16[3,256,128]{2,1,0:T(8,128)(2,1)}, bf16[3,256,128]{2,1,0:T(8,128)(2,1)}, bf16[3,256,128]{2,1,0:T(8,...) custom-call(bf16[32,384,128]{2,1,0:T(8,128)(2,1)} %get-tuple-element, ...), custom_call_target="tpu_custom_call", output_to_operand_aliasing={{8}: (1, {}), {9}: (2, {}), {10}: (3, {})} | custom-call | flops 1006632960 | bytes 12320768 | tf_op jit(solution)/shard_map/shifted_pairs/pallas_call | solution.py:360
  228.0 3.0 collective-permute-start.16
  231.0 7.9 %collective-permute-done.14.rest_5_ = bf16[1168,128]{1,0:T(8,128)(2,1)S(1)} collective-permute-done((bf16[1168,128]{1,0:T(8,128)(2,1)}, bf16[1168,128]{1,0:T(8,128)(2,1)S(1)}, u32[]{:S(2)}, u32[]{:S(2)}) %collective-permute-start.14) | collective-permute-done | bytes 299040 | tf_op jit(solution)/shard_map/ppermute | solution.py:40
  239.1 4.8 %collective-permute-start.20 = (bf16[3,256,128]{2,1,0:T(8,128)(2,1)}, bf16[3,256,128]{2,1,0:T(8,128)(2,1)}, u32[]{:S(2)}, u32[]{:S(2)}) collective-permute-start(bf16[3,256,128]{2,1,0:T(8,128)(2,1)} %get-tuple-element.120), channel_id=1, source_target_pairs={{0,96},{8,104},{16,112},{24,120},{32,128},{40,136},{48,144},{56,15... | collective-permute-start | bytes 589832 | tf_op jit(solution)/shard_map/ppermute | solution.py:40
  243.9 9.4 %shifted_pairs.4 = (bf16[3,256,128]{2,1,0:T(8,128)(2,1)}, bf16[3,256,128]{2,1,0:T(8,128)(2,1)}, bf16[3,256,128]{2,1,0:T(8,128)(2,1)}, bf16[3,256,128]{2,1,0:T(8,...) custom-call(bf16[32,384,128]{2,1,0:T(8,128)(2,1)} %get-tuple-element, ...), custom_call_target="tpu_custom_call", output_to_operand_aliasing={{6}: (1, {}), {7}: (2, {})} | custom-call | flops 754974720 | bytes 11337728 | tf_op jit(solution)/shard_map/shifted_pairs/pallas_call | solution.py:360
  253.4 6.6 %all-to-all-start.1 = ((bf16[48,256,128]{2,1,0:T(8,128)(2,1)}), bf16[48,256,128]{2,1,0:T(8,128)(2,1)}, u32[]{:S(2)}, u32[]{:S(2)}) async-start(bf16[48,256,128]{2,1,0:T(8,128)(2,1)} %get-tuple-element.108), calls=%async_computation.1 | async-start | bytes 6291456 | tf_op jit(solution)/shard_map/all_to_all | solution.py:56
  260.0 2.3 collective-permute-start.21
  262.3 1.0 collective-permute-start.22
  263.3 4.0 %collective-permute-start.23 = (bf16[3,256,128]{2,1,0:T(8,128)(2,1)}, bf16[3,256,128]{2,1,0:T(8,128)(2,1)}, u32[]{:S(2)}, u32[]{:S(2)}) collective-permute-start(bf16[3,256,128]{2,1,0:T(8,128)(2,1)} %get-tuple-element.123), channel_id=1, source_target_pairs={{0,184},{8,160},{16,168},{24,176},{32,216},{40,192},{48,200},{56,2... | collective-permute-start | bytes 589832 | tf_op jit(solution)/shard_map/ppermute | solution.py:40
  267.3 2.1 collective-permute-start.24
  269.4 6.5 %shifted_pairs.5 = (bf16[3,256,128]{2,1,0:T(8,128)(2,1)}, bf16[3,256,128]{2,1,0:T(8,128)(2,1)}, f32[32,256,128]{2,1,0:T(8,128)}) custom-call(bf16[32,384,128]{2,1,0:T(8,128)(2,1)} %get-tuple-element.71.own_ref, f32[32,256,128]{2,1,0:T(8,128)} %get-tuple-element.104.given_ref, bf16[1168,128]{1,0:T(8,128)(2,1)} %copy-done.26, ...), custom_call_target="tpu_custom_call", output_to_operand_aliasing={{2}: (1, {})} | custom-call | flops 999999995904 | tf_op jit(solution)/shard_map/shifted_pairs/pallas_call | solution.py:360
  275.9 56.3 %all-to-all-done.1.back_ref = bf16[48,256,128]{2,1,0:T(8,128)(2,1)} async-done(((bf16[48,256,128]{2,1,0:T(8,128)(2,1)}), bf16[48,256,128]{2,1,0:T(8,128)(2,1)}, u32[]{:S(2)}, u32[]{:S(2)}) %all-to-all-start.1) | async-done | bytes 3145760 | tf_op jit(solution)/shard_map/all_to_all | solution.py:56
  332.2 6.6 %gather_team.1 = (f32[32,256,128]{2,1,0:T(8,128)}, bf16[3,256,128]{2,1,0:T(8,128)(2,1)}, bf16[3,256,128]{2,1,0:T(8,128)(2,1)}, bf16[3,256,128]{2,1,0:T(8,128)(2,...) custom-call(s32[96]{0:T(128)} %get-tuple-element.70.used_ref, ...), custom_call_target="tpu_custom_call", output_to_operand_aliasing={{0}: (3, {}), {1}: (6, {}), {2}: (7, {}), {3}: (8, {}), {4}... | custom-call | flops 1572864 | bytes 11534336 | tf_op jit(solution)/shard_map/gather_team/pallas_call | solution.py:409
  338.9 6.5 %collective-permute-start.25 = (bf16[3,256,128]{2,1,0:T(8,128)(2,1)S(1)}, bf16[3,256,128]{2,1,0:T(8,128)(2,1)S(1)}, u32[]{:S(2)}, u32[]{:S(2)}) collective-permute-start(bf16[3,256,128]{2,1,0:T(8,128)(2,1)S(1)} %copy-done.29), channel_id=1, source_target_pairs={{0,248},{8,224},{16,232},{24,240},{32,24},{40,0},{48,8},{56,16},{6... | collective-permute-start | bytes 589832 | tf_op jit(solution)/shard_map/ppermute | solution.py:40
  345.4 8.5 %collective-permute-start.27 = (bf16[3,256,128]{2,1,0:T(8,128)(2,1)}, bf16[3,256,128]{2,1,0:T(8,128)(2,1)S(1)}, u32[]{:S(2)}, u32[]{:S(2)}) collective-permute-start(bf16[3,256,128]{2,1,0:T(8,128)(2,1)} %get-tuple-element.127), channel_id=1, source_target_pairs={{0,176},{8,184},{16,160},{24,168},{32,208},{40,216},{48,192},{56,2... | collective-permute-start | bytes 589832 | tf_op jit(solution)/shard_map/ppermute | solution.py:40
  353.9 1.5 collective-permute-start.29
  355.4 4.0 collective-permute-start.30
  359.4 3.7 collective-permute-start.31
  363.1 5.2 %collective-permute-done.27.rest_8_ = bf16[3,256,128]{2,1,0:T(8,128)(2,1)S(1)} collective-permute-done((bf16[3,256,128]{2,1,0:T(8,128)(2,1)}, bf16[3,256,128]{2,1,0:T(8,128)(2,1)S(1)}, u32[]{:S(2)}, u32[]{:S(2)}) %collective-permute-start.27) | collective-permute-done | bytes 196640 | tf_op jit(solution)/shard_map/ppermute | solution.py:40
  368.3 2.0 collective-permute-start.32
  370.3 2.3 collective-permute-done.28.rest_9_
  373.3 2.3 collective-permute-start.34
  375.6 6.2 %collective-permute-done.31.rest_12_ = bf16[3,256,128]{2,1,0:T(8,128)(2,1)S(1)} collective-permute-done((bf16[3,256,128]{2,1,0:T(8,128)(2,1)}, bf16[3,256,128]{2,1,0:T(8,128)(2,1)S(1)}, u32[]{:S(2)}, u32[]{:S(2)}) %collective-permute-start.31) | collective-permute-done | bytes 196640 | tf_op jit(solution)/shard_map/ppermute | solution.py:40
  381.8 5.7 %collective-permute-done.32.rest_13_ = bf16[3,256,128]{2,1,0:T(8,128)(2,1)S(1)} collective-permute-done((bf16[3,256,128]{2,1,0:T(8,128)(2,1)}, bf16[3,256,128]{2,1,0:T(8,128)(2,1)S(1)}, u32[]{:S(2)}, u32[]{:S(2)}) %collective-permute-start.32) | collective-permute-done | bytes 196640 | tf_op jit(solution)/shard_map/ppermute | solution.py:40
  388.3 10.3 %gather_and_mix.1 = bf16[8192,128]{1,0:T(8,128)(2,1)} custom-call(s32[96]{0:T(128)} %get-tuple-element.70.used_ref, s32[16]{0:T(128)} %stack.70.dests_ref, f32[32,256,128]{2,1,0:T(8,128)} %get-tuple-element.118.total_ref, bf16[8192,128]{1,0:T(8,128)(2,1)} %bitcast.28, bf16[128,128]{1,0:T(8,128)(2,1)} %w_ref.1, f32[1,128]{1,0:T(1,128)} %bitcast.36, ...), custom_call_target="tpu_custom_call" | custom-call | tf_op jit(solution)/shard_map/gather_and_mix/pallas_call | solution.py:453
  (101 shorter events, 3.1 us)
Async XLA Ops:
  13.4 24.0 %collective-permute-start.1 = (bf16[8,384,128]{2,1,0:T(8,128)(2,1)}, bf16[8,384,128]{2,1,0:T(8,128)(2,1)S(1)}, u32[]{:S(2)}, u32[]{:S(2)}) collective-permute-start(bf16[8,384,128]{2,1,0:T(8,128)(2,1)} %get-tuple-element.73), channel_id=1, source_target_pairs={{0,1},{1,2},{2,3},{3,4},{4,5},{5,6},{6,7},{8,9},{9,10},{10,11},{11... | collective-permute-start | bytes 2359304 | tf_op jit(solution)/shard_map/ppermute | solution.py:64
  15.4 21.1 %collective-permute-start = (s32[8,2]{0,1:T(2,128)S(1)}, s32[8,2]{0,1:T(2,128)S(1)}, u32[]{:S(2)}, u32[]{:S(2)}) collective-permute-start(s32[8,2]{0,1:T(2,128)S(1)} %pad_add_fusion), channel_id=1, source_target_pairs={{0,1},{1,2},{2,3},{3,4},{4,5},{5,6},{6,7},{8,9},{9,10},{10,11},{11... | collective-permute-start | bytes 200 | tf_op jit(solution)/shard_map/ppermute | solution.py:64
  18.9 120.8 %all-to-all-start = ((bf16[16,1168,128]{2,1,0:T(8,128)(2,1)}), bf16[16,1168,128]{2,1,0:T(8,128)(2,1)}, u32[]{:S(2)}, u32[]{:S(2)}) async-start(bf16[16,1168,128]{2,1,0:T(8,128)(2,1)} %get-tuple-element.72), calls=%async_computation | async-start | bytes 9568256 | tf_op jit(solution)/shard_map/all_to_all | solution.py:56
  29.5 132.6 %collective-permute-start.2 = (bf16[1168,128]{1,0:T(8,128)(2,1)}, bf16[1168,128]{1,0:T(8,128)(2,1)}, u32[]{:S(2)}, u32[]{:S(2)}) collective-permute-start(bf16[1168,128]{1,0:T(8,128)(2,1)} %get-tuple-element.88), channel_id=1, source_target_pairs={{0,96},{8,104},{16,112},{24,120},{32,128},{40,136},{48,144},{56,15... | collective-permute-start | bytes 897032 | tf_op jit(solution)/shard_map/ppermute | solution.py:40
  34.5 127.7 %collective-permute-start.3 = (bf16[1168,128]{1,0:T(8,128)(2,1)}, bf16[1168,128]{1,0:T(8,128)(2,1)}, u32[]{:S(2)}, u32[]{:S(2)}) collective-permute-start(bf16[1168,128]{1,0:T(8,128)(2,1)} %get-tuple-element.89), channel_id=1, source_target_pairs={{0,160},{8,168},{16,176},{24,184},{32,192},{40,200},{48,208},{56,2... | collective-permute-start | bytes 897032 | tf_op jit(solution)/shard_map/ppermute | solution.py:40
  34.6 133.7 %collective-permute-start.4 = (bf16[1168,128]{1,0:T(8,128)(2,1)}, bf16[1168,128]{1,0:T(8,128)(2,1)}, u32[]{:S(2)}, u32[]{:S(2)}) collective-permute-start(bf16[1168,128]{1,0:T(8,128)(2,1)} %get-tuple-element.90), channel_id=1, source_target_pairs={{0,32},{8,40},{16,48},{24,56},{32,64},{40,72},{48,80},{56,88},{64,... | collective-permute-start | bytes 897032 | tf_op jit(solution)/shard_map/ppermute | solution.py:40
  36.5 131.8 %collective-permute-start.5 = (bf16[1168,128]{1,0:T(8,128)(2,1)}, bf16[1168,128]{1,0:T(8,128)(2,1)}, u32[]{:S(2)}, u32[]{:S(2)}) collective-permute-start(bf16[1168,128]{1,0:T(8,128)(2,1)} %get-tuple-element.91), channel_id=1, source_target_pairs={{0,224},{8,232},{16,240},{24,248},{32,0},{40,8},{48,16},{56,24},{6... | collective-permute-start | bytes 897032 | tf_op jit(solution)/shard_map/ppermute | solution.py:40
  139.6 57.8 %copy-start.25 = (bf16[8,256,128]{2,1,0:T(8,128)(2,1)S(1)}, bf16[8,256,128]{2,1,0:T(8,128)(2,1)}, u32[]{:S(2)}) copy-start(bf16[8,256,128]{2,1,0:T(8,128)(2,1)} %get-tuple-element.109) | copy-start | bytes 1572868
  155.2 26.5 %collective-permute-start.6 = (bf16[1168,128]{1,0:T(8,128)(2,1)}, bf16[1168,128]{1,0:T(8,128)(2,1)S(1)}, u32[]{:S(2)}, u32[]{:S(2)}) collective-permute-start(bf16[1168,128]{1,0:T(8,128)(2,1)} %get-tuple-element.92), channel_id=1, source_target_pairs={{0,104},{8,112},{16,120},{24,96},{32,136},{40,144},{48,152},{56,12... | collective-permute-start | bytes 897032 | tf_op jit(solution)/shard_map/ppermute | solution.py:40
  162.2 26.1 %collective-permute-start.7 = (bf16[1168,128]{1,0:T(8,128)(2,1)}, bf16[1168,128]{1,0:T(8,128)(2,1)S(1)}, u32[]{:S(2)}, u32[]{:S(2)}) collective-permute-start(bf16[1168,128]{1,0:T(8,128)(2,1)} %get-tuple-element.93), channel_id=1, source_target_pairs={{0,184},{8,160},{16,168},{24,176},{32,216},{40,192},{48,200},{56,2... | collective-permute-start | bytes 897032 | tf_op jit(solution)/shard_map/ppermute | solution.py:40
  162.2 26.5 %collective-permute-start.8 = (bf16[1168,128]{1,0:T(8,128)(2,1)}, bf16[1168,128]{1,0:T(8,128)(2,1)S(1)}, u32[]{:S(2)}, u32[]{:S(2)}) collective-permute-start(bf16[1168,128]{1,0:T(8,128)(2,1)} %get-tuple-element.94), channel_id=1, source_target_pairs={{0,40},{8,48},{16,56},{24,32},{32,72},{40,80},{48,88},{56,64},{64,... | collective-permute-start | bytes 897032 | tf_op jit(solution)/shard_map/ppermute | solution.py:40
  168.2 29.2 %collective-permute-start.9 = (bf16[1168,128]{1,0:T(8,128)(2,1)}, bf16[1168,128]{1,0:T(8,128)(2,1)S(1)}, u32[]{:S(2)}, u32[]{:S(2)}) collective-permute-start(bf16[1168,128]{1,0:T(8,128)(2,1)} %get-tuple-element.95), channel_id=1, source_target_pairs={{0,248},{8,224},{16,232},{24,240},{32,24},{40,0},{48,8},{56,16},{6... | collective-permute-start | bytes 897032 | tf_op jit(solution)/shard_map/ppermute | solution.py:40
  168.2 43.1 %collective-permute-start.10 = (bf16[1168,128]{1,0:T(8,128)(2,1)}, bf16[1168,128]{1,0:T(8,128)(2,1)S(1)}, u32[]{:S(2)}, u32[]{:S(2)}) collective-permute-start(bf16[1168,128]{1,0:T(8,128)(2,1)} %get-tuple-element.98), channel_id=1, source_target_pairs={{0,112},{8,120},{16,96},{24,104},{32,144},{40,152},{48,128},{56,13... | collective-permute-start | bytes 897032 | tf_op jit(solution)/shard_map/ppermute | solution.py:40
  181.7 35.5 %copy-start.4 = (bf16[1168,128]{1,0:T(8,128)(2,1)}, bf16[1168,128]{1,0:T(8,128)(2,1)S(1)}, u32[]{:S(2)}) copy-start(bf16[1168,128]{1,0:T(8,128)(2,1)S(1)} %collective-permute-done.6.rest_6_) | copy-start | bytes 897028
  181.7 29.6 %collective-permute-start.11 = (bf16[1168,128]{1,0:T(8,128)(2,1)}, bf16[1168,128]{1,0:T(8,128)(2,1)S(1)}, u32[]{:S(2)}, u32[]{:S(2)}) collective-permute-start(bf16[1168,128]{1,0:T(8,128)(2,1)} %get-tuple-element.99), channel_id=1, source_target_pairs={{0,176},{8,184},{16,160},{24,168},{32,208},{40,216},{48,192},{56,2... | collective-permute-start | bytes 897032 | tf_op jit(solution)/shard_map/ppermute | solution.py:40
  188.2 29.0 %copy-start.6 = (bf16[1168,128]{1,0:T(8,128)(2,1)}, bf16[1168,128]{1,0:T(8,128)(2,1)S(1)}, u32[]{:S(2)}) copy-start(bf16[1168,128]{1,0:T(8,128)(2,1)S(1)} %collective-permute-done.7.rest_7_) | copy-start | bytes 897028
  188.2 39.7 %collective-permute-start.12 = (bf16[1168,128]{1,0:T(8,128)(2,1)}, bf16[1168,128]{1,0:T(8,128)(2,1)S(1)}, u32[]{:S(2)}, u32[]{:S(2)}) collective-permute-start(bf16[1168,128]{1,0:T(8,128)(2,1)} %get-tuple-element.100), channel_id=1, source_target_pairs={{0,48},{8,56},{16,32},{24,40},{32,80},{40,88},{48,64},{56,72},{64,... | collective-permute-start | bytes 897032 | tf_op jit(solution)/shard_map/ppermute | solution.py:40
  188.7 28.6 %copy-start.7 = (bf16[1168,128]{1,0:T(8,128)(2,1)}, bf16[1168,128]{1,0:T(8,128)(2,1)S(1)}, u32[]{:S(2)}) copy-start(bf16[1168,128]{1,0:T(8,128)(2,1)S(1)} %collective-permute-done.8.rest_8_) | copy-start | bytes 897028
  188.7 42.3 %collective-permute-start.13 = (bf16[1168,128]{1,0:T(8,128)(2,1)}, bf16[1168,128]{1,0:T(8,128)(2,1)S(1)}, u32[]{:S(2)}, u32[]{:S(2)}) collective-permute-start(bf16[1168,128]{1,0:T(8,128)(2,1)} %get-tuple-element.101), channel_id=1, source_target_pairs={{0,240},{8,248},{16,224},{24,232},{32,16},{40,24},{48,0},{56,8},{6... | collective-permute-start | bytes 897032 | tf_op jit(solution)/shard_map/ppermute | solution.py:40
  197.4 19.8 %copy-start.8 = (bf16[1168,128]{1,0:T(8,128)(2,1)}, bf16[1168,128]{1,0:T(8,128)(2,1)S(1)}, u32[]{:S(2)}) copy-start(bf16[1168,128]{1,0:T(8,128)(2,1)S(1)} %collective-permute-done.9.rest_9_) | copy-start | bytes 897028
  197.4 62.5 %collective-permute-start.18 = (bf16[8,256,128]{2,1,0:T(8,128)(2,1)S(1)}, bf16[8,256,128]{2,1,0:T(8,128)(2,1)S(1)}, u32[]{:S(2)}, u32[]{:S(2)}) collective-permute-start(bf16[8,256,128]{2,1,0:T(8,128)(2,1)S(1)} %copy-done.25), channel_id=1, source_target_pairs={{1,0},{2,1},{3,2},{4,3},{5,4},{6,5},{7,6},{9,8},{10,9},{11,10},{12... | collective-permute-start | bytes 1572872 | tf_op jit(solution)/shard_map/ppermute | solution.py:64
  211.3 16.6 %copy-start.1 = (bf16[1168,128]{1,0:T(8,128)(2,1)}, bf16[1168,128]{1,0:T(8,128)(2,1)S(1)}, u32[]{:S(2)}) copy-start(bf16[1168,128]{1,0:T(8,128)(2,1)S(1)} %collective-permute-done.10.rest_1_) | copy-start | bytes 897028
  211.3 27.6 %collective-permute-start.14 = (bf16[1168,128]{1,0:T(8,128)(2,1)}, bf16[1168,128]{1,0:T(8,128)(2,1)S(1)}, u32[]{:S(2)}, u32[]{:S(2)}) collective-permute-start(bf16[1168,128]{1,0:T(8,128)(2,1)} %get-tuple-element.102), channel_id=1, source_target_pairs={{0,120},{8,96},{16,104},{24,112},{32,152},{40,128},{48,136},{56,14... | collective-permute-start | bytes 897032 | tf_op jit(solution)/shard_map/ppermute | solution.py:40
  211.3 16.6 %copy-start.2 = (bf16[1168,128]{1,0:T(8,128)(2,1)}, bf16[1168,128]{1,0:T(8,128)(2,1)S(1)}, u32[]{:S(2)}) copy-start(bf16[1168,128]{1,0:T(8,128)(2,1)S(1)} %collective-permute-done.11.rest_2_) | copy-start | bytes 897028
  211.3 27.8 %collective-permute-start.15 = (bf16[1168,128]{1,0:T(8,128)(2,1)}, bf16[1168,128]{1,0:T(8,128)(2,1)S(1)}, u32[]{:S(2)}, u32[]{:S(2)}) collective-permute-start(bf16[1168,128]{1,0:T(8,128)(2,1)} %get-tuple-element.103), channel_id=1, source_target_pairs={{0,168},{8,176},{16,184},{24,160},{32,200},{40,208},{48,216},{56,1... | collective-permute-start | bytes 897032 | tf_op jit(solution)/shard_map/ppermute | solution.py:40
  228.0 16.0 %copy-start.3 = (bf16[1168,128]{1,0:T(8,128)(2,1)}, bf16[1168,128]{1,0:T(8,128)(2,1)S(1)}, u32[]{:S(2)}) copy-start(bf16[1168,128]{1,0:T(8,128)(2,1)S(1)} %collective-permute-done.12.rest_3_) | copy-start | bytes 897028
  228.0 35.3 %collective-permute-start.16 = (bf16[1168,128]{1,0:T(8,128)(2,1)}, bf16[1168,128]{1,0:T(8,128)(2,1)S(1)}, u32[]{:S(2)}, u32[]{:S(2)}) collective-permute-start(bf16[1168,128]{1,0:T(8,128)(2,1)} %get-tuple-element.105), channel_id=1, source_target_pairs={{0,56},{8,32},{16,40},{24,48},{32,88},{40,64},{48,72},{56,80},{64,... | collective-permute-start | bytes 897032 | tf_op jit(solution)/shard_map/ppermute | solution.py:40
  231.0 36.3 %collective-permute-start.17 = (bf16[1168,128]{1,0:T(8,128)(2,1)}, bf16[1168,128]{1,0:T(8,128)(2,1)S(1)}, u32[]{:S(2)}, u32[]{:S(2)}) collective-permute-start(bf16[1168,128]{1,0:T(8,128)(2,1)} %get-tuple-element.106), channel_id=1, source_target_pairs={{0,232},{8,240},{16,248},{24,224},{32,8},{40,16},{48,24},{56,0},{6... | collective-permute-start | bytes 897032 | tf_op jit(solution)/shard_map/ppermute | solution.py:40
  238.9 23.4 %collective-permute-start.19 = (bf16[3,256,128]{2,1,0:T(8,128)(2,1)}, bf16[3,256,128]{2,1,0:T(8,128)(2,1)S(1)}, u32[]{:S(2)}, u32[]{:S(2)}) collective-permute-start(bf16[3,256,128]{2,1,0:T(8,128)(2,1)} %get-tuple-element.119), channel_id=1, source_target_pairs={{0,160},{8,168},{16,176},{24,184},{32,192},{40,200},{48,208},{56,2... | collective-permute-start | bytes 589832 | tf_op jit(solution)/shard_map/ppermute | solution.py:40
  239.1 99.7 %collective-permute-start.20 = (bf16[3,256,128]{2,1,0:T(8,128)(2,1)}, bf16[3,256,128]{2,1,0:T(8,128)(2,1)}, u32[]{:S(2)}, u32[]{:S(2)}) collective-permute-start(bf16[3,256,128]{2,1,0:T(8,128)(2,1)} %get-tuple-element.120), channel_id=1, source_target_pairs={{0,96},{8,104},{16,112},{24,120},{32,128},{40,136},{48,144},{56,15... | collective-permute-start | bytes 589832 | tf_op jit(solution)/shard_map/ppermute | solution.py:40
  253.4 78.8 %all-to-all-start.1 = ((bf16[48,256,128]{2,1,0:T(8,128)(2,1)}), bf16[48,256,128]{2,1,0:T(8,128)(2,1)}, u32[]{:S(2)}, u32[]{:S(2)}) async-start(bf16[48,256,128]{2,1,0:T(8,128)(2,1)} %get-tuple-element.108), calls=%async_computation.1 | async-start | bytes 6291456 | tf_op jit(solution)/shard_map/all_to_all | solution.py:56
  260.0 85.4 %collective-permute-start.21 = (bf16[3,256,128]{2,1,0:T(8,128)(2,1)}, bf16[3,256,128]{2,1,0:T(8,128)(2,1)}, u32[]{:S(2)}, u32[]{:S(2)}) collective-permute-start(bf16[3,256,128]{2,1,0:T(8,128)(2,1)} %get-tuple-element.121), channel_id=1, source_target_pairs={{0,224},{8,232},{16,240},{24,248},{32,0},{40,8},{48,16},{56,24},{6... | collective-permute-start | bytes 589832 | tf_op jit(solution)/shard_map/ppermute | solution.py:40
  262.3 83.1 %collective-permute-start.22 = (bf16[3,256,128]{2,1,0:T(8,128)(2,1)}, bf16[3,256,128]{2,1,0:T(8,128)(2,1)}, u32[]{:S(2)}, u32[]{:S(2)}) collective-permute-start(bf16[3,256,128]{2,1,0:T(8,128)(2,1)} %get-tuple-element.122), channel_id=1, source_target_pairs={{0,32},{8,40},{16,48},{24,56},{32,64},{40,72},{48,80},{56,88},{64,... | collective-permute-start | bytes 589832 | tf_op jit(solution)/shard_map/ppermute | solution.py:40
  263.3 90.6 %collective-permute-start.23 = (bf16[3,256,128]{2,1,0:T(8,128)(2,1)}, bf16[3,256,128]{2,1,0:T(8,128)(2,1)}, u32[]{:S(2)}, u32[]{:S(2)}) collective-permute-start(bf16[3,256,128]{2,1,0:T(8,128)(2,1)} %get-tuple-element.123), channel_id=1, source_target_pairs={{0,184},{8,160},{16,168},{24,176},{32,216},{40,192},{48,200},{56,2... | collective-permute-start | bytes 589832 | tf_op jit(solution)/shard_map/ppermute | solution.py:40
  267.3 86.6 %collective-permute-start.24 = (bf16[3,256,128]{2,1,0:T(8,128)(2,1)}, bf16[3,256,128]{2,1,0:T(8,128)(2,1)}, u32[]{:S(2)}, u32[]{:S(2)}) collective-permute-start(bf16[3,256,128]{2,1,0:T(8,128)(2,1)} %get-tuple-element.124), channel_id=1, source_target_pairs={{0,104},{8,112},{16,120},{24,96},{32,136},{40,144},{48,152},{56,12... | collective-permute-start | bytes 589832 | tf_op jit(solution)/shard_map/ppermute | solution.py:40
  338.9 16.5 %collective-permute-start.25 = (bf16[3,256,128]{2,1,0:T(8,128)(2,1)S(1)}, bf16[3,256,128]{2,1,0:T(8,128)(2,1)S(1)}, u32[]{:S(2)}, u32[]{:S(2)}) collective-permute-start(bf16[3,256,128]{2,1,0:T(8,128)(2,1)S(1)} %copy-done.29), channel_id=1, source_target_pairs={{0,248},{8,224},{16,232},{24,240},{32,24},{40,0},{48,8},{56,16},{6... | collective-permute-start | bytes 589832 | tf_op jit(solution)/shard_map/ppermute | solution.py:40
  345.4 14.0 %collective-permute-start.26 = (bf16[3,256,128]{2,1,0:T(8,128)(2,1)S(1)}, bf16[3,256,128]{2,1,0:T(8,128)(2,1)S(1)}, u32[]{:S(2)}, u32[]{:S(2)}) collective-permute-start(bf16[3,256,128]{2,1,0:T(8,128)(2,1)S(1)} %copy-done.28), channel_id=1, source_target_pairs={{0,40},{8,48},{16,56},{24,32},{32,72},{40,80},{48,88},{56,64},{64,... | collective-permute-start | bytes 589832 | tf_op jit(solution)/shard_map/ppermute | solution.py:40
  345.4 22.9 %collective-permute-start.27 = (bf16[3,256,128]{2,1,0:T(8,128)(2,1)}, bf16[3,256,128]{2,1,0:T(8,128)(2,1)S(1)}, u32[]{:S(2)}, u32[]{:S(2)}) collective-permute-start(bf16[3,256,128]{2,1,0:T(8,128)(2,1)} %get-tuple-element.127), channel_id=1, source_target_pairs={{0,176},{8,184},{16,160},{24,168},{32,208},{40,216},{48,192},{56,2... | collective-permute-start | bytes 589832 | tf_op jit(solution)/shard_map/ppermute | solution.py:40
  353.9 18.7 %collective-permute-start.28 = (bf16[3,256,128]{2,1,0:T(8,128)(2,1)}, bf16[3,256,128]{2,1,0:T(8,128)(2,1)S(1)}, u32[]{:S(2)}, u32[]{:S(2)}) collective-permute-start(bf16[3,256,128]{2,1,0:T(8,128)(2,1)} %get-tuple-element.128), channel_id=1, source_target_pairs={{0,112},{8,120},{16,96},{24,104},{32,144},{40,152},{48,128},{56,13... | collective-permute-start | bytes 589832 | tf_op jit(solution)/shard_map/ppermute | solution.py:40
  353.9 19.3 %collective-permute-start.29 = (bf16[3,256,128]{2,1,0:T(8,128)(2,1)}, bf16[3,256,128]{2,1,0:T(8,128)(2,1)S(1)}, u32[]{:S(2)}, u32[]{:S(2)}) collective-permute-start(bf16[3,256,128]{2,1,0:T(8,128)(2,1)} %get-tuple-element.129), channel_id=1, source_target_pairs={{0,240},{8,248},{16,224},{24,232},{32,16},{40,24},{48,0},{56,8},{6... | collective-permute-start | bytes 589832 | tf_op jit(solution)/shard_map/ppermute | solution.py:40
  355.4 32.0 %copy-start.12 = (bf16[3,256,128]{2,1,0:T(8,128)(2,1)}, bf16[3,256,128]{2,1,0:T(8,128)(2,1)S(1)}, u32[]{:S(2)}) copy-start(bf16[3,256,128]{2,1,0:T(8,128)(2,1)S(1)} %collective-permute-done.25.rest_6_) | copy-start | bytes 589828
  355.4 20.1 %collective-permute-start.30 = (bf16[3,256,128]{2,1,0:T(8,128)(2,1)}, bf16[3,256,128]{2,1,0:T(8,128)(2,1)S(1)}, u32[]{:S(2)}, u32[]{:S(2)}) collective-permute-start(bf16[3,256,128]{2,1,0:T(8,128)(2,1)} %get-tuple-element.130), channel_id=1, source_target_pairs={{0,48},{8,56},{16,32},{24,40},{32,80},{40,88},{48,64},{56,72},{64,... | collective-permute-start | bytes 589832 | tf_op jit(solution)/shard_map/ppermute | solution.py:40
  359.4 28.1 %copy-start.13 = (bf16[3,256,128]{2,1,0:T(8,128)(2,1)}, bf16[3,256,128]{2,1,0:T(8,128)(2,1)S(1)}, u32[]{:S(2)}) copy-start(bf16[3,256,128]{2,1,0:T(8,128)(2,1)S(1)} %collective-permute-done.26.rest_7_) | copy-start | bytes 589828
  359.4 22.3 %collective-permute-start.31 = (bf16[3,256,128]{2,1,0:T(8,128)(2,1)}, bf16[3,256,128]{2,1,0:T(8,128)(2,1)S(1)}, u32[]{:S(2)}, u32[]{:S(2)}) collective-permute-start(bf16[3,256,128]{2,1,0:T(8,128)(2,1)} %get-tuple-element.131), channel_id=1, source_target_pairs={{0,168},{8,176},{16,184},{24,160},{32,200},{40,208},{48,216},{56,1... | collective-permute-start | bytes 589832 | tf_op jit(solution)/shard_map/ppermute | solution.py:40
  368.3 19.2 %copy-start.14 = (bf16[3,256,128]{2,1,0:T(8,128)(2,1)}, bf16[3,256,128]{2,1,0:T(8,128)(2,1)S(1)}, u32[]{:S(2)}) copy-start(bf16[3,256,128]{2,1,0:T(8,128)(2,1)S(1)} %collective-permute-done.27.rest_8_) | copy-start | bytes 589828
  368.3 19.1 %collective-permute-start.32 = (bf16[3,256,128]{2,1,0:T(8,128)(2,1)}, bf16[3,256,128]{2,1,0:T(8,128)(2,1)S(1)}, u32[]{:S(2)}, u32[]{:S(2)}) collective-permute-start(bf16[3,256,128]{2,1,0:T(8,128)(2,1)} %get-tuple-element.132), channel_id=1, source_target_pairs={{0,120},{8,96},{16,104},{24,112},{32,152},{40,128},{48,136},{56,14... | collective-permute-start | bytes 589832 | tf_op jit(solution)/shard_map/ppermute | solution.py:40
  372.6 14.8 %collective-permute-start.33 = (bf16[3,256,128]{2,1,0:T(8,128)(2,1)}, bf16[3,256,128]{2,1,0:T(8,128)(2,1)S(1)}, u32[]{:S(2)}, u32[]{:S(2)}) collective-permute-start(bf16[3,256,128]{2,1,0:T(8,128)(2,1)} %get-tuple-element.133), channel_id=1, source_target_pairs={{0,232},{8,240},{16,248},{24,224},{32,8},{40,16},{48,24},{56,0},{6... | collective-permute-start | bytes 589832 | tf_op jit(solution)/shard_map/ppermute | solution.py:40
  373.3 14.2 %collective-permute-start.34 = (bf16[3,256,128]{2,1,0:T(8,128)(2,1)}, bf16[3,256,128]{2,1,0:T(8,128)(2,1)S(1)}, u32[]{:S(2)}, u32[]{:S(2)}) collective-permute-start(bf16[3,256,128]{2,1,0:T(8,128)(2,1)} %get-tuple-element.134), channel_id=1, source_target_pairs={{0,56},{8,32},{16,40},{24,48},{32,88},{40,64},{48,72},{56,80},{64,... | collective-permute-start | bytes 589832 | tf_op jit(solution)/shard_map/ppermute | solution.py:40
  (19 other events, 161.0 us)

commit v5 on v4

--- a/solution.py
+++ b/solution.py
@@ -25,7 +25,7 @@
 PASSED = 1
 MEMBERS = SPACES // 2
 TEAMS = [[z * SPAN_Y + y for z in range(p, SPAN_Z, 2) for y in range(SPAN_Y)] for p in range(2)]
-LATE = 8
+LATE = 12
 STAGE = 6
 LONG = 10**12
 SMEM = pl.BlockSpec(memory_space=pltpu.SMEM)

time: 401 us -> 402 us (level)
  starting transfers between devices: 116 us -> 125 us
  waiting for transfers between devices: 201 us -> 194 us
    all_to_all x2, waiting for transfers between devices: 152 us -> 144 us  [team_exchange(): lax.all_to_all(value, 'space', split_axis=0, concat_axis=0, tiled=True, a...]
    ppermute x32, starting transfers between devices: 91.7 us -> 99 us  [space_shift(): lax.ppermute(value, 'space', [(z * SPAN_Y + y, (z + shift[0]) % SPAN_Z *...]
  transfers between devices with their start and end apart: 37 -> 37, of which waited for: 10 -> 13; matrix products, arithmetic and copies ran while one was open for 0% -> 0% of each run, Pallas kernels for 14% -> 14%
where the time goes in v5:
time: 402 us; the launch traced here: 401 us
  waiting for transfers between devices  194 us (48%)
  starting transfers between devices  125 us (31%)
  Pallas kernels  75.7 us (19%)
    all_to_all x2, waiting for transfers between devices, team_exchange(): lax.all_to_all(value, 'space', split_axis=0, concat_axis=0, tiled=True, a...  144 us
    ppermute x32, starting transfers between devices, space_shift(): lax.ppermute(value, 'space', [(z * SPAN_Y + y, (z + shift[0]) % SPAN_Z *...  99 us
    ppermute x32, waiting for transfers between devices, space_shift(): lax.ppermute(value, 'space', [(z * SPAN_Y + y, (z + shift[0]) % SPAN_Z *...  49.8 us
    pallas_call x3, Pallas kernels, shifted_pairs(): pl.pallas_call(kernel, in_specs=[VMEM] * 2 + [ANYWHERE] * handed + [VMEM]...  26.6 us
    all_to_all x2, starting transfers between devices, team_exchange(): lax.all_to_all(value, 'space', split_axis=0, concat_axis=0, tiled=True, a...  19.1 us
    pallas_call x1, Pallas kernels, team_pairs(): pl.pallas_call(kernel, grid=(MEMBERS // CREW,), in_specs=[pl.BlockSpec((C...  15.5 us
    pallas_call x1, Pallas kernels, project_and_pack(): pl.pallas_call(kernel, grid_spec=pltpu.PrefetchScalarGridSpec(num_scalar_...  10.7 us
    pallas_call x1, Pallas kernels, gather_and_mix(): pl.pallas_call(kernel, grid_spec=pltpu.PrefetchScalarGridSpec(num_scalar_...  10.3 us
  transfers between devices with their start and end apart: 37, of which 13 were waited for; matrix products, arithmetic and copies ran while one was open for 0% of the time, Pallas kernels for 14%

profile of v5, /device:TPU:42, one launch (start us, length us, event | category | flops | bytes accessed | tf_op | source)
XLA Modules:
  0.0 400.7 jit_solution(16331442710204195062)
XLA Ops:
  2.8 10.7 %project_and_pack.1 = (s32[96]{0:T(128)}, bf16[32,384,128]{2,1,0:T(8,128)(2,1)}, bf16[8,384,128]{2,1,0:T(8,128)(2,1)}, bf16[16,1168,128]{2,1,0:T(8,128)(2,1)}, b...) custom-call(s32[64]{0:T(128)} %bitcast.32, ...), custom_call_target="tpu_custom_call" | custom-call | tf_op jit(solution)/shard_map/project_and_pack/pallas_call | solution.py:155
  13.4 1.9 collective-permute-start.1
  15.4 3.5 collective-permute-start
  18.9 10.7 %all-to-all-start = ((bf16[16,1168,128]{2,1,0:T(8,128)(2,1)}), bf16[16,1168,128]{2,1,0:T(8,128)(2,1)}, u32[]{:S(2)}, u32[]{:S(2)}) async-start(bf16[16,1168,128]{2,1,0:T(8,128)(2,1)} %get-tuple-element.68), calls=%async_computation | async-start | bytes 9568256 | tf_op jit(solution)/shard_map/all_to_all | solution.py:56
  30.3 0.9 copy-done.25
  31.1 6.0 %pairs_above.1 = (bf16[8,256,128]{2,1,0:T(8,128)(2,1)}, f32[32,256,128]{2,1,0:T(8,128)}) custom-call(s32[16]{0:T(128)} %reshape.3.cross_ref, bf16[8,384,128]{2,1,0:T(8,128)(2,1)} %copy-done.25, bf16[32,384,128]{2,1,0:T(8,128)(2,1)} %get-tuple-element.67.own_ref), custom_call_target="tpu_custom_call" | custom-call | flops 999999995904 | tf_op jit(solution)/shard_map/pairs_above/pallas_call | solution.py:257
  37.1 1.9 collective-permute-start.18
  39.1 5.0 %collective-permute-start.2 = (bf16[1168,128]{1,0:T(8,128)(2,1)S(1)}, bf16[1168,128]{1,0:T(8,128)(2,1)S(1)}, u32[]{:S(2)}, u32[]{:S(2)}) collective-permute-start(bf16[1168,128]{1,0:T(8,128)(2,1)S(1)} %copy-done.31), channel_id=1, source_target_pairs={{0,96},{8,104},{16,112},{24,120},{32,128},{40,136},{48,144},{56,15... | collective-permute-start | bytes 897032 | tf_op jit(solution)/shard_map/ppermute | solution.py:40
  44.2 1.9 collective-permute-start.4
  46.2 93.5 %all-to-all-done.arrived_ref = bf16[16,1168,128]{2,1,0:T(8,128)(2,1)} async-done(((bf16[16,1168,128]{2,1,0:T(8,128)(2,1)}), bf16[16,1168,128]{2,1,0:T(8,128)(2,1)}, u32[]{:S(2)}, u32[]{:S(2)}) %all-to-all-start) | async-done | bytes 4784160 | tf_op jit(solution)/shard_map/all_to_all | solution.py:56
  139.7 15.5 %team_pairs.1 = (bf16[48,256,128]{2,1,0:T(8,128)(2,1)}, f32[32,256,128]{2,1,0:T(8,128)}, bf16[1168,128]{1,0:T(8,128)(2,1)}, bf16[1168,128]{1,0:T(8,128)(2,1)}, b...) custom-call(bf16[16,1168,128]{2,1,0:T(8,128)(2,1)} %all-to-all-done., ...), custom_call_target="tpu_custom_call", output_to_operand_aliasing={{2}: (3, {}), {3}: (4, {}), {4}: (5, {}), {5}: (6, {}), {6}... | custom-call | flops 2013265920 | bytes 16252928 | tf_op jit(solution)/shard_map/team_pairs/pallas_call | solution.py:305
  155.2 1.1 collective-permute-done.2.rest_2_
  156.3 5.9 %collective-permute-start.6 = (bf16[1168,128]{1,0:T(8,128)(2,1)}, bf16[1168,128]{1,0:T(8,128)(2,1)S(1)}, u32[]{:S(2)}, u32[]{:S(2)}) collective-permute-start(bf16[1168,128]{1,0:T(8,128)(2,1)} %get-tuple-element.88), channel_id=1, source_target_pairs={{0,104},{8,112},{16,120},{24,96},{32,136},{40,144},{48,152},{56,12... | collective-permute-start | bytes 897032 | tf_op jit(solution)/shard_map/ppermute | solution.py:40
  162.2 6.0 %collective-permute-start.8 = (bf16[1168,128]{1,0:T(8,128)(2,1)}, bf16[1168,128]{1,0:T(8,128)(2,1)S(1)}, u32[]{:S(2)}, u32[]{:S(2)}) collective-permute-start(bf16[1168,128]{1,0:T(8,128)(2,1)} %get-tuple-element.90), channel_id=1, source_target_pairs={{0,40},{8,48},{16,56},{24,32},{32,72},{40,80},{48,88},{56,64},{64,... | collective-permute-start | bytes 897032 | tf_op jit(solution)/shard_map/ppermute | solution.py:40
  168.3 6.9 %collective-permute-start.10 = (bf16[1168,128]{1,0:T(8,128)(2,1)}, bf16[1168,128]{1,0:T(8,128)(2,1)S(1)}, u32[]{:S(2)}, u32[]{:S(2)}) collective-permute-start(bf16[1168,128]{1,0:T(8,128)(2,1)} %get-tuple-element.94), channel_id=1, source_target_pairs={{0,112},{8,120},{16,96},{24,104},{32,144},{40,152},{48,128},{56,13... | collective-permute-start | bytes 897032 | tf_op jit(solution)/shard_map/ppermute | solution.py:40
  175.1 6.8 %collective-permute-done.6.rest_6_ = bf16[1168,128]{1,0:T(8,128)(2,1)S(1)} collective-permute-done((bf16[1168,128]{1,0:T(8,128)(2,1)}, bf16[1168,128]{1,0:T(8,128)(2,1)S(1)}, u32[]{:S(2)}, u32[]{:S(2)}) %collective-permute-start.6) | collective-permute-done | bytes 299040 | tf_op jit(solution)/shard_map/ppermute | solution.py:40
  182.0 6.3 %collective-permute-start.11 = (bf16[1168,128]{1,0:T(8,128)(2,1)}, bf16[1168,128]{1,0:T(8,128)(2,1)S(1)}, u32[]{:S(2)}, u32[]{:S(2)}) collective-permute-start(bf16[1168,128]{1,0:T(8,128)(2,1)} %get-tuple-element.95), channel_id=1, source_target_pairs={{0,176},{8,184},{16,160},{24,168},{32,208},{40,216},{48,192},{56,2... | collective-permute-start | bytes 897032 | tf_op jit(solution)/shard_map/ppermute | solution.py:40
  188.7 8.7 %collective-permute-start.13 = (bf16[1168,128]{1,0:T(8,128)(2,1)}, bf16[1168,128]{1,0:T(8,128)(2,1)S(1)}, u32[]{:S(2)}, u32[]{:S(2)}) collective-permute-start(bf16[1168,128]{1,0:T(8,128)(2,1)} %get-tuple-element.97), channel_id=1, source_target_pairs={{0,240},{8,248},{16,224},{24,232},{32,16},{40,24},{48,0},{56,8},{6... | collective-permute-start | bytes 897032 | tf_op jit(solution)/shard_map/ppermute | solution.py:40
  198.0 2.0 collective-permute-start.14
  199.9 11.7 %collective-permute-done.10.rest_1_ = bf16[1168,128]{1,0:T(8,128)(2,1)S(1)} collective-permute-done((bf16[1168,128]{1,0:T(8,128)(2,1)}, bf16[1168,128]{1,0:T(8,128)(2,1)S(1)}, u32[]{:S(2)}, u32[]{:S(2)}) %collective-permute-start.10) | collective-permute-done | bytes 299040 | tf_op jit(solution)/shard_map/ppermute | solution.py:40
  211.6 1.1 collective-permute-start.15
  212.8 10.7 %shifted_pairs.3 = (bf16[3,256,128]{2,1,0:T(8,128)(2,1)}, bf16[3,256,128]{2,1,0:T(8,128)(2,1)}, bf16[3,256,128]{2,1,0:T(8,128)(2,1)}, bf16[3,256,128]{2,1,0:T(8,...) custom-call(bf16[32,384,128]{2,1,0:T(8,128)(2,1)} %get-tuple-element, ...), custom_call_target="tpu_custom_call", output_to_operand_aliasing={{8}: (1, {}), {9}: (2, {}), {10}: (3, {})} | custom-call | flops 1006632960 | bytes 12320768 | tf_op jit(solution)/shard_map/shifted_pairs/pallas_call | solution.py:360
  223.9 2.4 collective-permute-done.12.rest_3_
  226.4 2.2 collective-permute-start.20
  228.6 15.5 %collective-permute-done.14.rest_5_ = bf16[1168,128]{1,0:T(8,128)(2,1)S(1)} collective-permute-done((bf16[1168,128]{1,0:T(8,128)(2,1)}, bf16[1168,128]{1,0:T(8,128)(2,1)S(1)}, u32[]{:S(2)}, u32[]{:S(2)}) %collective-permute-start.14) | collective-permute-done | bytes 299040 | tf_op jit(solution)/shard_map/ppermute | solution.py:40
  244.1 2.9 collective-permute-start.17
  247.1 4.1 %collective-permute-start.22 = (bf16[3,256,128]{2,1,0:T(8,128)(2,1)}, bf16[3,256,128]{2,1,0:T(8,128)(2,1)S(1)}, u32[]{:S(2)}, u32[]{:S(2)}) collective-permute-start(bf16[3,256,128]{2,1,0:T(8,128)(2,1)} %get-tuple-element.114), channel_id=1, source_target_pairs={{0,32},{8,40},{16,48},{24,56},{32,64},{40,72},{48,80},{56,88},{64,... | collective-permute-start | bytes 589832 | tf_op jit(solution)/shard_map/ppermute | solution.py:40
  251.1 4.5 %collective-permute-start.23 = (bf16[3,256,128]{2,1,0:T(8,128)(2,1)}, bf16[3,256,128]{2,1,0:T(8,128)(2,1)S(1)}, u32[]{:S(2)}, u32[]{:S(2)}) collective-permute-start(bf16[3,256,128]{2,1,0:T(8,128)(2,1)} %get-tuple-element.115), channel_id=1, source_target_pairs={{0,184},{8,160},{16,168},{24,176},{32,216},{40,192},{48,200},{56,2... | collective-permute-start | bytes 589832 | tf_op jit(solution)/shard_map/ppermute | solution.py:40
  255.7 1.4 collective-permute-start.24
  257.1 9.5 %shifted_pairs.4 = (bf16[3,256,128]{2,1,0:T(8,128)(2,1)}, bf16[3,256,128]{2,1,0:T(8,128)(2,1)}, bf16[3,256,128]{2,1,0:T(8,128)(2,1)}, bf16[3,256,128]{2,1,0:T(8,...) custom-call(bf16[32,384,128]{2,1,0:T(8,128)(2,1)} %get-tuple-element, ...), custom_call_target="tpu_custom_call", output_to_operand_aliasing={{6}: (1, {}), {7}: (2, {})} | custom-call | flops 754974720 | bytes 11337728 | tf_op jit(solution)/shard_map/shifted_pairs/pallas_call | solution.py:360
  266.6 8.5 %all-to-all-start.1 = ((bf16[48,256,128]{2,1,0:T(8,128)(2,1)}), bf16[48,256,128]{2,1,0:T(8,128)(2,1)}, u32[]{:S(2)}, u32[]{:S(2)}) async-start(bf16[48,256,128]{2,1,0:T(8,128)(2,1)} %get-tuple-element.104), calls=%async_computation.1 | async-start | bytes 6291456 | tf_op jit(solution)/shard_map/all_to_all | solution.py:56
  275.1 1.0 collective-permute-start.25
  276.0 2.3 collective-permute-start.26
  278.3 6.7 %collective-permute-start.27 = (bf16[3,256,128]{2,1,0:T(8,128)(2,1)}, bf16[3,256,128]{2,1,0:T(8,128)(2,1)}, u32[]{:S(2)}, u32[]{:S(2)}) collective-permute-start(bf16[3,256,128]{2,1,0:T(8,128)(2,1)} %get-tuple-element.119), channel_id=1, source_target_pairs={{0,176},{8,184},{16,160},{24,168},{32,208},{40,216},{48,192},{56,2... | collective-permute-start | bytes 589832 | tf_op jit(solution)/shard_map/ppermute | solution.py:40
  285.1 1.0 collective-permute-start.28
  286.1 2.2 collective-permute-start.29
  288.3 6.5 %shifted_pairs.5 = (bf16[3,256,128]{2,1,0:T(8,128)(2,1)}, bf16[3,256,128]{2,1,0:T(8,128)(2,1)}, f32[32,256,128]{2,1,0:T(8,128)}) custom-call(bf16[32,384,128]{2,1,0:T(8,128)(2,1)} %get-tuple-element.67.own_ref, f32[32,256,128]{2,1,0:T(8,128)} %get-tuple-element.100.given_ref, bf16[1168,128]{1,0:T(8,128)(2,1)} %copy-done.28, ...), custom_call_target="tpu_custom_call", output_to_operand_aliasing={{2}: (1, {})} | custom-call | flops 999999995904 | tf_op jit(solution)/shard_map/shifted_pairs/pallas_call | solution.py:360
  294.8 50.8 %all-to-all-done.1.back_ref = bf16[48,256,128]{2,1,0:T(8,128)(2,1)} async-done(((bf16[48,256,128]{2,1,0:T(8,128)(2,1)}), bf16[48,256,128]{2,1,0:T(8,128)(2,1)}, u32[]{:S(2)}, u32[]{:S(2)}) %all-to-all-start.1) | async-done | bytes 3145760 | tf_op jit(solution)/shard_map/all_to_all | solution.py:56
  345.6 6.6 %gather_team.1 = (f32[32,256,128]{2,1,0:T(8,128)}, bf16[3,256,128]{2,1,0:T(8,128)(2,1)}, bf16[3,256,128]{2,1,0:T(8,128)(2,1)}, bf16[3,256,128]{2,1,0:T(8,128)(2,1)}, bf16[3,256,128]{2,1,0:T(8,128)(2,1)}) custom-call(s32[96]{0:T(128)} %get-tuple-element.66.used_ref, ...), custom_call_target="tpu_custom_call", output_to_operand_aliasing={{0}: (3, {}), {1}: (6, {}), {2}: (7, {}), {3}: (8, {}), {4}... | custom-call | flops 1572864 | bytes 11534336 | tf_op jit(solution)/shard_map/gather_team/pallas_call | solution.py:409
  352.3 8.9 %collective-permute-start.30 = (bf16[3,256,128]{2,1,0:T(8,128)(2,1)S(1)}, bf16[3,256,128]{2,1,0:T(8,128)(2,1)S(1)}, u32[]{:S(2)}, u32[]{:S(2)}) collective-permute-start(bf16[3,256,128]{2,1,0:T(8,128)(2,1)S(1)} %copy-done.32), channel_id=1, source_target_pairs={{0,48},{8,56},{16,32},{24,40},{32,80},{40,88},{48,64},{56,72},{64,... | collective-permute-start | bytes 589832 | tf_op jit(solution)/shard_map/ppermute | solution.py:40
  361.2 3.4 collective-permute-start.31
  364.8 5.1 %collective-permute-start.32 = (bf16[3,256,128]{2,1,0:T(8,128)(2,1)}, bf16[3,256,128]{2,1,0:T(8,128)(2,1)S(1)}, u32[]{:S(2)}, u32[]{:S(2)}) collective-permute-start(bf16[3,256,128]{2,1,0:T(8,128)(2,1)} %get-tuple-element.124), channel_id=1, source_target_pairs={{0,120},{8,96},{16,104},{24,112},{32,152},{40,128},{48,136},{56,14... | collective-permute-start | bytes 589832 | tf_op jit(solution)/shard_map/ppermute | solution.py:40
  369.9 6.8 %collective-permute-start.33 = (bf16[3,256,128]{2,1,0:T(8,128)(2,1)}, bf16[3,256,128]{2,1,0:T(8,128)(2,1)S(1)}, u32[]{:S(2)}, u32[]{:S(2)}) collective-permute-start(bf16[3,256,128]{2,1,0:T(8,128)(2,1)} %get-tuple-element.125), channel_id=1, source_target_pairs={{0,232},{8,240},{16,248},{24,224},{32,8},{40,16},{48,24},{56,0},{6... | collective-permute-start | bytes 589832 | tf_op jit(solution)/shard_map/ppermute | solution.py:40
  376.7 1.9 collective-permute-start.34
  378.6 0.9 collective-permute-done.31.rest_12_
  379.5 4.6 %collective-permute-done.32.rest_13_ = bf16[3,256,128]{2,1,0:T(8,128)(2,1)S(1)} collective-permute-done((bf16[3,256,128]{2,1,0:T(8,128)(2,1)}, bf16[3,256,128]{2,1,0:T(8,128)(2,1)S(1)}, u32[]{:S(2)}, u32[]{:S(2)}) %collective-permute-start.32) | collective-permute-done | bytes 196640 | tf_op jit(solution)/shard_map/ppermute | solution.py:40
  384.1 5.5 %collective-permute-done.34.rest_15_ = bf16[3,256,128]{2,1,0:T(8,128)(2,1)S(1)} collective-permute-done((bf16[3,256,128]{2,1,0:T(8,128)(2,1)}, bf16[3,256,128]{2,1,0:T(8,128)(2,1)S(1)}, u32[]{:S(2)}, u32[]{:S(2)}) %collective-permute-start.34) | collective-permute-done | bytes 196640 | tf_op jit(solution)/shard_map/ppermute | solution.py:40
  390.3 10.3 %gather_and_mix.1 = bf16[8192,128]{1,0:T(8,128)(2,1)} custom-call(s32[96]{0:T(128)} %get-tuple-element.66.used_ref, s32[16]{0:T(128)} %stack.70.dests_ref, f32[32,256,128]{2,1,0:T(8,128)} %get-tuple-element.110.total_ref, bf16[8192,128]{1,0:T(8,128)(2,1)} %bitcast.28, bf16[128,128]{1,0:T(8,128)(2,1)} %w_ref.1, f32[1,128]{1,0:T(1,128)} %bitcast.36, ...), custom_call_target="tpu_custom_call" | custom-call | tf_op jit(solution)/shard_map/gather_and_mix/pallas_call | solution.py:453
  (107 shorter events, 6.2 us)
Async XLA Ops:
  13.4 16.8 %collective-permute-start.1 = (bf16[8,384,128]{2,1,0:T(8,128)(2,1)}, bf16[8,384,128]{2,1,0:T(8,128)(2,1)S(1)}, u32[]{:S(2)}, u32[]{:S(2)}) collective-permute-start(bf16[8,384,128]{2,1,0:T(8,128)(2,1)} %get-tuple-element.69), channel_id=1, source_target_pairs={{0,1},{1,2},{2,3},{3,4},{4,5},{5,6},{6,7},{8,9},{9,10},{10,11},{11... | collective-permute-start | bytes 2359304 | tf_op jit(solution)/shard_map/ppermute | solution.py:64
  15.4 14.2 %collective-permute-start = (s32[8,2]{0,1:T(2,128)S(1)}, s32[8,2]{0,1:T(2,128)S(1)}, u32[]{:S(2)}, u32[]{:S(2)}) collective-permute-start(s32[8,2]{0,1:T(2,128)S(1)} %pad_add_fusion), channel_id=1, source_target_pairs={{0,1},{1,2},{2,3},{3,4},{4,5},{5,6},{6,7},{8,9},{9,10},{10,11},{11... | collective-permute-start | bytes 200 | tf_op jit(solution)/shard_map/ppermute | solution.py:64
  18.9 120.8 %all-to-all-start = ((bf16[16,1168,128]{2,1,0:T(8,128)(2,1)}), bf16[16,1168,128]{2,1,0:T(8,128)(2,1)}, u32[]{:S(2)}, u32[]{:S(2)}) async-start(bf16[16,1168,128]{2,1,0:T(8,128)(2,1)} %get-tuple-element.68), calls=%async_computation | async-start | bytes 9568256 | tf_op jit(solution)/shard_map/all_to_all | solution.py:56
  37.1 131.1 %collective-permute-start.18 = (bf16[8,256,128]{2,1,0:T(8,128)(2,1)}, bf16[8,256,128]{2,1,0:T(8,128)(2,1)S(1)}, u32[]{:S(2)}, u32[]{:S(2)}) collective-permute-start(bf16[8,256,128]{2,1,0:T(8,128)(2,1)} %get-tuple-element.105), channel_id=1, source_target_pairs={{1,0},{2,1},{3,2},{4,3},{5,4},{6,5},{7,6},{9,8},{10,9},{11,10},{12... | collective-permute-start | bytes 1572872 | tf_op jit(solution)/shard_map/ppermute | solution.py:64
  39.1 117.2 %collective-permute-start.2 = (bf16[1168,128]{1,0:T(8,128)(2,1)S(1)}, bf16[1168,128]{1,0:T(8,128)(2,1)S(1)}, u32[]{:S(2)}, u32[]{:S(2)}) collective-permute-start(bf16[1168,128]{1,0:T(8,128)(2,1)S(1)} %copy-done.31), channel_id=1, source_target_pairs={{0,96},{8,104},{16,112},{24,120},{32,128},{40,136},{48,144},{56,15... | collective-permute-start | bytes 897032 | tf_op jit(solution)/shard_map/ppermute | solution.py:40
  44.1 118.1 %collective-permute-start.3 = (bf16[1168,128]{1,0:T(8,128)(2,1)S(1)}, bf16[1168,128]{1,0:T(8,128)(2,1)S(1)}, u32[]{:S(2)}, u32[]{:S(2)}) collective-permute-start(bf16[1168,128]{1,0:T(8,128)(2,1)S(1)} %copy-done.29), channel_id=1, source_target_pairs={{0,160},{8,168},{16,176},{24,184},{32,192},{40,200},{48,208},{56,2... | collective-permute-start | bytes 897032 | tf_op jit(solution)/shard_map/ppermute | solution.py:40
  44.2 118.0 %collective-permute-start.4 = (bf16[1168,128]{1,0:T(8,128)(2,1)S(1)}, bf16[1168,128]{1,0:T(8,128)(2,1)S(1)}, u32[]{:S(2)}, u32[]{:S(2)}) collective-permute-start(bf16[1168,128]{1,0:T(8,128)(2,1)S(1)} %copy-done.27), channel_id=1, source_target_pairs={{0,32},{8,40},{16,48},{24,56},{32,64},{40,72},{48,80},{56,88},{64,... | collective-permute-start | bytes 897032 | tf_op jit(solution)/shard_map/ppermute | solution.py:40
  46.1 122.2 %collective-permute-start.5 = (bf16[1168,128]{1,0:T(8,128)(2,1)S(1)}, bf16[1168,128]{1,0:T(8,128)(2,1)S(1)}, u32[]{:S(2)}, u32[]{:S(2)}) collective-permute-start(bf16[1168,128]{1,0:T(8,128)(2,1)S(1)} %copy-done.26), channel_id=1, source_target_pairs={{0,224},{8,232},{16,240},{24,248},{32,0},{40,8},{48,16},{56,24},{6... | collective-permute-start | bytes 897032 | tf_op jit(solution)/shard_map/ppermute | solution.py:40
  156.2 56.5 %copy-start.2 = (bf16[1168,128]{1,0:T(8,128)(2,1)}, bf16[1168,128]{1,0:T(8,128)(2,1)S(1)}, u32[]{:S(2)}) copy-start(bf16[1168,128]{1,0:T(8,128)(2,1)S(1)} %collective-permute-done.2.rest_2_) | copy-start | bytes 897028
  156.3 25.7 %collective-permute-start.6 = (bf16[1168,128]{1,0:T(8,128)(2,1)}, bf16[1168,128]{1,0:T(8,128)(2,1)S(1)}, u32[]{:S(2)}, u32[]{:S(2)}) collective-permute-start(bf16[1168,128]{1,0:T(8,128)(2,1)} %get-tuple-element.88), channel_id=1, source_target_pairs={{0,104},{8,112},{16,120},{24,96},{32,136},{40,144},{48,152},{56,12... | collective-permute-start | bytes 897032 | tf_op jit(solution)/shard_map/ppermute | solution.py:40
  162.2 50.5 %copy-start.3 = (bf16[1168,128]{1,0:T(8,128)(2,1)}, bf16[1168,128]{1,0:T(8,128)(2,1)S(1)}, u32[]{:S(2)}) copy-start(bf16[1168,128]{1,0:T(8,128)(2,1)S(1)} %collective-permute-done.3.rest_3_) | copy-start | bytes 897028
  162.2 26.1 %collective-permute-start.7 = (bf16[1168,128]{1,0:T(8,128)(2,1)}, bf16[1168,128]{1,0:T(8,128)(2,1)S(1)}, u32[]{:S(2)}, u32[]{:S(2)}) collective-permute-start(bf16[1168,128]{1,0:T(8,128)(2,1)} %get-tuple-element.89), channel_id=1, source_target_pairs={{0,184},{8,160},{16,168},{24,176},{32,216},{40,192},{48,200},{56,2... | collective-permute-start | bytes 897032 | tf_op jit(solution)/shard_map/ppermute | solution.py:40
  162.2 50.5 %copy-start.4 = (bf16[1168,128]{1,0:T(8,128)(2,1)}, bf16[1168,128]{1,0:T(8,128)(2,1)S(1)}, u32[]{:S(2)}) copy-start(bf16[1168,128]{1,0:T(8,128)(2,1)S(1)} %collective-permute-done.4.rest_4_) | copy-start | bytes 897028
  162.2 26.5 %collective-permute-start.8 = (bf16[1168,128]{1,0:T(8,128)(2,1)}, bf16[1168,128]{1,0:T(8,128)(2,1)S(1)}, u32[]{:S(2)}, u32[]{:S(2)}) collective-permute-start(bf16[1168,128]{1,0:T(8,128)(2,1)} %get-tuple-element.90), channel_id=1, source_target_pairs={{0,40},{8,48},{16,56},{24,32},{32,72},{40,80},{48,88},{56,64},{64,... | collective-permute-start | bytes 897032 | tf_op jit(solution)/shard_map/ppermute | solution.py:40
  168.2 44.5 %copy-start.6 = (bf16[1168,128]{1,0:T(8,128)(2,1)}, bf16[1168,128]{1,0:T(8,128)(2,1)S(1)}, u32[]{:S(2)}) copy-start(bf16[1168,128]{1,0:T(8,128)(2,1)S(1)} %collective-permute-done.5.rest_5_) | copy-start | bytes 897028
  168.2 29.7 %collective-permute-start.9 = (bf16[1168,128]{1,0:T(8,128)(2,1)}, bf16[1168,128]{1,0:T(8,128)(2,1)S(1)}, u32[]{:S(2)}, u32[]{:S(2)}) collective-permute-start(bf16[1168,128]{1,0:T(8,128)(2,1)} %get-tuple-element.91), channel_id=1, source_target_pairs={{0,248},{8,224},{16,232},{24,240},{32,24},{40,0},{48,8},{56,16},{6... | collective-permute-start | bytes 897032 | tf_op jit(solution)/shard_map/ppermute | solution.py:40
  168.3 55.2 %copy-start = (bf16[8,256,128]{2,1,0:T(8,128)(2,1)}, bf16[8,256,128]{2,1,0:T(8,128)(2,1)S(1)}, u32[]{:S(2)}) copy-start(bf16[8,256,128]{2,1,0:T(8,128)(2,1)S(1)} %collective-permute-done.18.back_x_ref) | copy-start | bytes 1572868
  168.3 43.3 %collective-permute-start.10 = (bf16[1168,128]{1,0:T(8,128)(2,1)}, bf16[1168,128]{1,0:T(8,128)(2,1)S(1)}, u32[]{:S(2)}, u32[]{:S(2)}) collective-permute-start(bf16[1168,128]{1,0:T(8,128)(2,1)} %get-tuple-element.94), channel_id=1, source_target_pairs={{0,112},{8,120},{16,96},{24,104},{32,144},{40,152},{48,128},{56,13... | collective-permute-start | bytes 897032 | tf_op jit(solution)/shard_map/ppermute | solution.py:40
  182.0 30.8 %copy-start.11 = (bf16[1168,128]{1,0:T(8,128)(2,1)}, bf16[1168,128]{1,0:T(8,128)(2,1)S(1)}, u32[]{:S(2)}) copy-start(bf16[1168,128]{1,0:T(8,128)(2,1)S(1)} %collective-permute-done.6.rest_6_) | copy-start | bytes 897028
  182.0 41.5 %collective-permute-start.11 = (bf16[1168,128]{1,0:T(8,128)(2,1)}, bf16[1168,128]{1,0:T(8,128)(2,1)S(1)}, u32[]{:S(2)}, u32[]{:S(2)}) collective-permute-start(bf16[1168,128]{1,0:T(8,128)(2,1)} %get-tuple-element.95), channel_id=1, source_target_pairs={{0,176},{8,184},{16,160},{24,168},{32,208},{40,216},{48,192},{56,2... | collective-permute-start | bytes 897032 | tf_op jit(solution)/shard_map/ppermute | solution.py:40
  188.3 24.5 %copy-start.12 = (bf16[1168,128]{1,0:T(8,128)(2,1)}, bf16[1168,128]{1,0:T(8,128)(2,1)S(1)}, u32[]{:S(2)}) copy-start(bf16[1168,128]{1,0:T(8,128)(2,1)S(1)} %collective-permute-done.7.rest_7_) | copy-start | bytes 897028
  188.3 38.1 %collective-permute-start.12 = (bf16[1168,128]{1,0:T(8,128)(2,1)}, bf16[1168,128]{1,0:T(8,128)(2,1)S(1)}, u32[]{:S(2)}, u32[]{:S(2)}) collective-permute-start(bf16[1168,128]{1,0:T(8,128)(2,1)} %get-tuple-element.96), channel_id=1, source_target_pairs={{0,48},{8,56},{16,32},{24,40},{32,80},{40,88},{48,64},{56,72},{64,... | collective-permute-start | bytes 897032 | tf_op jit(solution)/shard_map/ppermute | solution.py:40
  188.7 24.0 %copy-start.13 = (bf16[1168,128]{1,0:T(8,128)(2,1)}, bf16[1168,128]{1,0:T(8,128)(2,1)S(1)}, u32[]{:S(2)}) copy-start(bf16[1168,128]{1,0:T(8,128)(2,1)S(1)} %collective-permute-done.8.rest_8_) | copy-start | bytes 897028
  188.7 39.9 %collective-permute-start.13 = (bf16[1168,128]{1,0:T(8,128)(2,1)}, bf16[1168,128]{1,0:T(8,128)(2,1)S(1)}, u32[]{:S(2)}, u32[]{:S(2)}) collective-permute-start(bf16[1168,128]{1,0:T(8,128)(2,1)} %get-tuple-element.97), channel_id=1, source_target_pairs={{0,240},{8,248},{16,224},{24,232},{32,16},{40,24},{48,0},{56,8},{6... | collective-permute-start | bytes 897032 | tf_op jit(solution)/shard_map/ppermute | solution.py:40
  198.0 46.2 %collective-permute-start.14 = (bf16[1168,128]{1,0:T(8,128)(2,1)}, bf16[1168,128]{1,0:T(8,128)(2,1)S(1)}, u32[]{:S(2)}, u32[]{:S(2)}) collective-permute-start(bf16[1168,128]{1,0:T(8,128)(2,1)} %get-tuple-element.98), channel_id=1, source_target_pairs={{0,120},{8,96},{16,104},{24,112},{32,152},{40,128},{48,136},{56,14... | collective-permute-start | bytes 897032 | tf_op jit(solution)/shard_map/ppermute | solution.py:40
  211.6 32.5 %collective-permute-start.15 = (bf16[1168,128]{1,0:T(8,128)(2,1)}, bf16[1168,128]{1,0:T(8,128)(2,1)S(1)}, u32[]{:S(2)}, u32[]{:S(2)}) collective-permute-start(bf16[1168,128]{1,0:T(8,128)(2,1)} %get-tuple-element.99), channel_id=1, source_target_pairs={{0,168},{8,176},{16,184},{24,160},{32,200},{40,208},{48,216},{56,1... | collective-permute-start | bytes 897032 | tf_op jit(solution)/shard_map/ppermute | solution.py:40
  223.5 33.6 %copy-start.5 = (bf16[1168,128]{1,0:T(8,128)(2,1)}, bf16[1168,128]{1,0:T(8,128)(2,1)S(1)}, u32[]{:S(2)}) copy-start(bf16[1168,128]{1,0:T(8,128)(2,1)S(1)} %collective-permute-done.11.rest_2_) | copy-start | bytes 897028
  223.5 23.6 %collective-permute-start.19 = (bf16[3,256,128]{2,1,0:T(8,128)(2,1)}, bf16[3,256,128]{2,1,0:T(8,128)(2,1)}, u32[]{:S(2)}, u32[]{:S(2)}) collective-permute-start(bf16[3,256,128]{2,1,0:T(8,128)(2,1)} %get-tuple-element.111), channel_id=1, source_target_pairs={{0,160},{8,168},{16,176},{24,184},{32,192},{40,200},{48,208},{56,2... | collective-permute-start | bytes 589832 | tf_op jit(solution)/shard_map/ppermute | solution.py:40
  226.4 30.7 %copy-start.7 = (bf16[1168,128]{1,0:T(8,128)(2,1)}, bf16[1168,128]{1,0:T(8,128)(2,1)S(1)}, u32[]{:S(2)}) copy-start(bf16[1168,128]{1,0:T(8,128)(2,1)S(1)} %collective-permute-done.12.rest_3_) | copy-start | bytes 897028
  226.4 24.8 %collective-permute-start.20 = (bf16[3,256,128]{2,1,0:T(8,128)(2,1)}, bf16[3,256,128]{2,1,0:T(8,128)(2,1)}, u32[]{:S(2)}, u32[]{:S(2)}) collective-permute-start(bf16[3,256,128]{2,1,0:T(8,128)(2,1)} %get-tuple-element.112), channel_id=1, source_target_pairs={{0,96},{8,104},{16,112},{24,120},{32,128},{40,136},{48,144},{56,15... | collective-permute-start | bytes 589832 | tf_op jit(solution)/shard_map/ppermute | solution.py:40
  228.6 28.5 %copy-start.8 = (bf16[1168,128]{1,0:T(8,128)(2,1)}, bf16[1168,128]{1,0:T(8,128)(2,1)S(1)}, u32[]{:S(2)}) copy-start(bf16[1168,128]{1,0:T(8,128)(2,1)S(1)} %collective-permute-done.13.rest_4_) | copy-start | bytes 897028
  228.6 27.0 %collective-permute-start.21 = (bf16[3,256,128]{2,1,0:T(8,128)(2,1)}, bf16[3,256,128]{2,1,0:T(8,128)(2,1)}, u32[]{:S(2)}, u32[]{:S(2)}) collective-permute-start(bf16[3,256,128]{2,1,0:T(8,128)(2,1)} %get-tuple-element.113), channel_id=1, source_target_pairs={{0,224},{8,232},{16,240},{24,248},{32,0},{40,8},{48,16},{56,24},{6... | collective-permute-start | bytes 589832 | tf_op jit(solution)/shard_map/ppermute | solution.py:40
  244.1 41.0 %collective-permute-start.16 = (bf16[1168,128]{1,0:T(8,128)(2,1)}, bf16[1168,128]{1,0:T(8,128)(2,1)S(1)}, u32[]{:S(2)}, u32[]{:S(2)}) collective-permute-start(bf16[1168,128]{1,0:T(8,128)(2,1)} %get-tuple-element.101), channel_id=1, source_target_pairs={{0,56},{8,32},{16,40},{24,48},{32,88},{40,64},{48,72},{56,80},{64,... | collective-permute-start | bytes 897032 | tf_op jit(solution)/shard_map/ppermute | solution.py:40
  244.1 42.0 %collective-permute-start.17 = (bf16[1168,128]{1,0:T(8,128)(2,1)}, bf16[1168,128]{1,0:T(8,128)(2,1)S(1)}, u32[]{:S(2)}, u32[]{:S(2)}) collective-permute-start(bf16[1168,128]{1,0:T(8,128)(2,1)} %get-tuple-element.102), channel_id=1, source_target_pairs={{0,232},{8,240},{16,248},{24,224},{32,8},{40,16},{48,24},{56,0},{6... | collective-permute-start | bytes 897032 | tf_op jit(solution)/shard_map/ppermute | solution.py:40
  247.1 28.0 %collective-permute-start.22 = (bf16[3,256,128]{2,1,0:T(8,128)(2,1)}, bf16[3,256,128]{2,1,0:T(8,128)(2,1)S(1)}, u32[]{:S(2)}, u32[]{:S(2)}) collective-permute-start(bf16[3,256,128]{2,1,0:T(8,128)(2,1)} %get-tuple-element.114), channel_id=1, source_target_pairs={{0,32},{8,40},{16,48},{24,56},{32,64},{40,72},{48,80},{56,88},{64,... | collective-permute-start | bytes 589832 | tf_op jit(solution)/shard_map/ppermute | solution.py:40
  251.1 24.9 %collective-permute-start.23 = (bf16[3,256,128]{2,1,0:T(8,128)(2,1)}, bf16[3,256,128]{2,1,0:T(8,128)(2,1)S(1)}, u32[]{:S(2)}, u32[]{:S(2)}) collective-permute-start(bf16[3,256,128]{2,1,0:T(8,128)(2,1)} %get-tuple-element.115), channel_id=1, source_target_pairs={{0,184},{8,160},{16,168},{24,176},{32,216},{40,192},{48,200},{56,2... | collective-permute-start | bytes 589832 | tf_op jit(solution)/shard_map/ppermute | solution.py:40
  255.7 22.7 %collective-permute-start.24 = (bf16[3,256,128]{2,1,0:T(8,128)(2,1)}, bf16[3,256,128]{2,1,0:T(8,128)(2,1)S(1)}, u32[]{:S(2)}, u32[]{:S(2)}) collective-permute-start(bf16[3,256,128]{2,1,0:T(8,128)(2,1)} %get-tuple-element.116), channel_id=1, source_target_pairs={{0,104},{8,112},{16,120},{24,96},{32,136},{40,144},{48,152},{56,12... | collective-permute-start | bytes 589832 | tf_op jit(solution)/shard_map/ppermute | solution.py:40
  266.6 79.1 %all-to-all-start.1 = ((bf16[48,256,128]{2,1,0:T(8,128)(2,1)}), bf16[48,256,128]{2,1,0:T(8,128)(2,1)}, u32[]{:S(2)}, u32[]{:S(2)}) async-start(bf16[48,256,128]{2,1,0:T(8,128)(2,1)} %get-tuple-element.104), calls=%async_computation.1 | async-start | bytes 6291456 | tf_op jit(solution)/shard_map/all_to_all | solution.py:56
  275.1 77.2 %collective-permute-start.25 = (bf16[3,256,128]{2,1,0:T(8,128)(2,1)}, bf16[3,256,128]{2,1,0:T(8,128)(2,1)}, u32[]{:S(2)}, u32[]{:S(2)}) collective-permute-start(bf16[3,256,128]{2,1,0:T(8,128)(2,1)} %get-tuple-element.117), channel_id=1, source_target_pairs={{0,248},{8,224},{16,232},{24,240},{32,24},{40,0},{48,8},{56,16},{6... | collective-permute-start | bytes 589832 | tf_op jit(solution)/shard_map/ppermute | solution.py:40
  276.0 85.2 %collective-permute-start.26 = (bf16[3,256,128]{2,1,0:T(8,128)(2,1)}, bf16[3,256,128]{2,1,0:T(8,128)(2,1)}, u32[]{:S(2)}, u32[]{:S(2)}) collective-permute-start(bf16[3,256,128]{2,1,0:T(8,128)(2,1)} %get-tuple-element.118), channel_id=1, source_target_pairs={{0,40},{8,48},{16,56},{24,32},{32,72},{40,80},{48,88},{56,64},{64,... | collective-permute-start | bytes 589832 | tf_op jit(solution)/shard_map/ppermute | solution.py:40
  278.3 86.5 %collective-permute-start.27 = (bf16[3,256,128]{2,1,0:T(8,128)(2,1)}, bf16[3,256,128]{2,1,0:T(8,128)(2,1)}, u32[]{:S(2)}, u32[]{:S(2)}) collective-permute-start(bf16[3,256,128]{2,1,0:T(8,128)(2,1)} %get-tuple-element.119), channel_id=1, source_target_pairs={{0,176},{8,184},{16,160},{24,168},{32,208},{40,216},{48,192},{56,2... | collective-permute-start | bytes 589832 | tf_op jit(solution)/shard_map/ppermute | solution.py:40
  285.1 84.8 %collective-permute-start.28 = (bf16[3,256,128]{2,1,0:T(8,128)(2,1)}, bf16[3,256,128]{2,1,0:T(8,128)(2,1)}, u32[]{:S(2)}, u32[]{:S(2)}) collective-permute-start(bf16[3,256,128]{2,1,0:T(8,128)(2,1)} %get-tuple-element.120), channel_id=1, source_target_pairs={{0,112},{8,120},{16,96},{24,104},{32,144},{40,152},{48,128},{56,13... | collective-permute-start | bytes 589832 | tf_op jit(solution)/shard_map/ppermute | solution.py:40
  286.1 90.6 %collective-permute-start.29 = (bf16[3,256,128]{2,1,0:T(8,128)(2,1)}, bf16[3,256,128]{2,1,0:T(8,128)(2,1)}, u32[]{:S(2)}, u32[]{:S(2)}) collective-permute-start(bf16[3,256,128]{2,1,0:T(8,128)(2,1)} %get-tuple-element.121), channel_id=1, source_target_pairs={{0,240},{8,248},{16,224},{24,232},{32,16},{40,24},{48,0},{56,8},{6... | collective-permute-start | bytes 589832 | tf_op jit(solution)/shard_map/ppermute | solution.py:40
  352.3 26.3 %collective-permute-start.30 = (bf16[3,256,128]{2,1,0:T(8,128)(2,1)S(1)}, bf16[3,256,128]{2,1,0:T(8,128)(2,1)S(1)}, u32[]{:S(2)}, u32[]{:S(2)}) collective-permute-start(bf16[3,256,128]{2,1,0:T(8,128)(2,1)S(1)} %copy-done.32), channel_id=1, source_target_pairs={{0,48},{8,56},{16,32},{24,40},{32,80},{40,88},{48,64},{56,72},{64,... | collective-permute-start | bytes 589832 | tf_op jit(solution)/shard_map/ppermute | solution.py:40
  361.2 18.3 %collective-permute-start.31 = (bf16[3,256,128]{2,1,0:T(8,128)(2,1)}, bf16[3,256,128]{2,1,0:T(8,128)(2,1)S(1)}, u32[]{:S(2)}, u32[]{:S(2)}) collective-permute-start(bf16[3,256,128]{2,1,0:T(8,128)(2,1)} %get-tuple-element.123), channel_id=1, source_target_pairs={{0,168},{8,176},{16,184},{24,160},{32,200},{40,208},{48,216},{56,1... | collective-permute-start | bytes 589832 | tf_op jit(solution)/shard_map/ppermute | solution.py:40
  364.8 19.3 %collective-permute-start.32 = (bf16[3,256,128]{2,1,0:T(8,128)(2,1)}, bf16[3,256,128]{2,1,0:T(8,128)(2,1)S(1)}, u32[]{:S(2)}, u32[]{:S(2)}) collective-permute-start(bf16[3,256,128]{2,1,0:T(8,128)(2,1)} %get-tuple-element.124), channel_id=1, source_target_pairs={{0,120},{8,96},{16,104},{24,112},{32,152},{40,128},{48,136},{56,14... | collective-permute-start | bytes 589832 | tf_op jit(solution)/shard_map/ppermute | solution.py:40
  369.9 14.3 %collective-permute-start.33 = (bf16[3,256,128]{2,1,0:T(8,128)(2,1)}, bf16[3,256,128]{2,1,0:T(8,128)(2,1)S(1)}, u32[]{:S(2)}, u32[]{:S(2)}) collective-permute-start(bf16[3,256,128]{2,1,0:T(8,128)(2,1)} %get-tuple-element.125), channel_id=1, source_target_pairs={{0,232},{8,240},{16,248},{24,224},{32,8},{40,16},{48,24},{56,0},{6... | collective-permute-start | bytes 589832 | tf_op jit(solution)/shard_map/ppermute | solution.py:40
  376.7 12.9 %collective-permute-start.34 = (bf16[3,256,128]{2,1,0:T(8,128)(2,1)}, bf16[3,256,128]{2,1,0:T(8,128)(2,1)S(1)}, u32[]{:S(2)}, u32[]{:S(2)}) collective-permute-start(bf16[3,256,128]{2,1,0:T(8,128)(2,1)} %get-tuple-element.126), channel_id=1, source_target_pairs={{0,56},{8,32},{16,40},{24,48},{32,88},{40,64},{48,72},{56,80},{64,... | collective-permute-start | bytes 589832 | tf_op jit(solution)/shard_map/ppermute | solution.py:40
  (22 other events, 233.0 us)
